TPU v7x, 512 devices: a whole 4x4x16 slice. The times are simulated.
512 devices in a mesh: panel: 16 (over x_lo, y, core), sc: 32 (over z, x_hi).
Axes of the slice: x: 4 (x_hi: 2, x_lo: 2; x = x_hi * 2 + x_lo), y: 4, z: 16, core: 2. Of those that a mesh axis runs over, the one named last changes fastest.
Arguments:
- captured_waveform: bfloat16 [16, 14, 1024, 4096], P(None, None, 'sc', 'panel'), may hold values from -6 to 6
- element_lookup: int32 [2048], P('panel'), may hold values from 0 to 2047, as said below
- combiner: bfloat16 [2048, 128], P('panel'), may hold values from -0.09375 to 0.09375
- pilot_syms: int32 [2], replicated, may hold values from 0 to 13
- pilot_values: float32 [2, 16384], P(None, ('panel', 'sc')), may hold values from -5 to 5
- mod_order: int32 [4096], P(('panel', 'sc')), may hold values from 1 to 4
- conv_first: bfloat16 [3, 3, 256, 128], replicated, may hold values from -0.1875 to 0.1875
- conv_rest: bfloat16 [5, 3, 3, 128, 128], replicated, may hold values from -0.25 to 0.25
- conv_bias: float32 [6, 128], replicated, may hold values from -1.5 to 1.5
- demap_in: bfloat16 [128, 256], replicated, may hold values from -0.75 to 0.75
- demap_bias: float32 [256], replicated, may hold values from -1.5 to 1.5
- demap_out: bfloat16 [256, 128], replicated, may hold values from -0.5 to 0.5
Outputs:
- llr: float32 [14, 16384, 128], P(None, ('panel', 'sc'))
Inputs may be any that keep to these rules, and one draw needn't show every extreme that they name: `element_lookup`: the rows of each panel (blocks of 2048 // 16 rows) map to a permutation of that block's own indices.
All inputs are finite; a program needn't handle non-finite values.
Results may differ from a plain program's by a relative error of at most 0.035.
Values may be sent and summed in bfloat16 or wider, within the bound.
No kernel may reach another device: no remote copies, remote signals or barrier semaphores. Data moves between devices by JAX's collectives and lax.ppermute only.
A program may use at most 64 MiB of HBM per device.

v0:
```python
import jax
import jax.numpy as jnp
from jax import lax
from jax.sharding import PartitionSpec as P

RB_SC = 4
BITS = 8


def with_halo(cells, sides, width):
    for axis, dim in sides:
        count = lax.axis_size(axis)
        ends = count - 1
        head = lax.slice_in_dim(cells, 0, width, axis=dim)
        tail = lax.slice_in_dim(cells, cells.shape[dim] - width, cells.shape[dim], axis=dim)
        cells = jnp.concatenate(
            [
                lax.ppermute(tail, axis, [(i, (i + 1) % count) for i in range(ends)]),
                cells,
                lax.ppermute(head, axis, [((i + 1) % count, i) for i in range(ends)]),
            ],
            axis=dim,
        )
    return cells


def build_matrix(combiner_rows):
    beam_count = combiner_rows.shape[1] // 2
    real_part = combiner_rows[:, :beam_count]
    imag_part = combiner_rows[:, beam_count:]
    real_row = jnp.concatenate([real_part, imag_part], 1)
    imag_row = jnp.concatenate([-imag_part, real_part], 1)
    return jnp.stack([real_row, imag_row], 1).reshape(2 * combiner_rows.shape[0], 2 * beam_count)


def convolve_valid(field, kernel, layer_bias):
    sym_count, wide_count, channels = field.shape
    out_count = wide_count - 2
    padded = jnp.pad(field, ((1, 1), (0, 0), (0, 0)))
    pieces = []
    for shift_sym in range(3):
        for shift_sub in range(3):
            pieces.append(
                padded[shift_sym : shift_sym + sym_count, shift_sub : shift_sub + out_count]
            )
    stacked = jnp.concatenate(pieces, -1).reshape(sym_count * out_count, 9 * channels)
    reduced_totals = jnp.dot(
        stacked, kernel.reshape(9 * channels, kernel.shape[3]), preferred_element_type=jnp.float32
    )
    result = jax.nn.relu(reduced_totals + layer_bias[None, :]).astype(jnp.bfloat16)
    return result.reshape(sym_count, out_count, -1)


def edge_extend(field, rim_depth):
    return with_halo(field, ((("panel", "sc"), 1),), rim_depth)


def per_device(
    captured_waveform,
    element_lookup,
    combiner,
    pilot_syms,
    pilot_values,
    mod_order,
    conv_first,
    conv_rest,
    conv_bias,
    demap_in,
    demap_bias,
    demap_out,
):
    sym_count = captured_waveform.shape[1]
    sub_count = captured_waveform.shape[2]
    antenna_span = captured_waveform.shape[3]
    beam_width = combiner.shape[1]
    resident_rows = element_lookup - lax.axis_index("panel") * (antenna_span // 2)
    matrix = build_matrix(jnp.take(combiner, resident_rows, axis=0))
    reduced_totals = lax.psum_scatter(
        jnp.einsum(
            "gtsk,kc->gtsc", captured_waveform, matrix, preferred_element_type=jnp.float32
        ).astype(jnp.bfloat16),
        "panel",
        scatter_dimension=0,
        tiled=True,
    ).astype(jnp.float32)
    lobe_outputs = reduced_totals[0].astype(jnp.bfloat16)
    beam_count = beam_width // 2
    is_pilot = jnp.any(jnp.arange(sym_count)[:, None] == pilot_syms[None, :], axis=1).astype(
        jnp.float32
    )
    beam_float = lobe_outputs.astype(jnp.float32)
    beam_re = beam_float[..., :beam_count]
    beam_im = beam_float[..., beam_count:]
    pilot_re = pilot_values[0][None, :, None]
    pilot_im = pilot_values[1][None, :, None]
    estimate = jnp.concatenate(
        [beam_re * pilot_re + beam_im * pilot_im, beam_im * pilot_re - beam_re * pilot_im], -1
    )
    estimate = (estimate * is_pilot[:, None, None]).astype(jnp.bfloat16)
    field = jnp.concatenate([lobe_outputs, estimate], -1)
    layer_count = conv_rest.shape[0] + 1
    for layer_idx in range(layer_count):
        kernel = conv_first if layer_idx == 0 else conv_rest[layer_idx - 1]
        field = convolve_valid(edge_extend(field, 1), kernel, conv_bias[layer_idx])
    channels = field.shape[2]
    hidden = jnp.dot(
        field.reshape(sym_count * sub_count, channels), demap_in, preferred_element_type=jnp.float32
    )
    hidden = jax.nn.relu(hidden + demap_bias[None, :]).astype(jnp.bfloat16)
    llr_values = jnp.dot(hidden, demap_out, preferred_element_type=jnp.float32).reshape(
        sym_count, sub_count, -1
    )
    bit_limit = 2 * jnp.repeat(mod_order, RB_SC)
    bit_index = jnp.arange(llr_values.shape[2]) % BITS
    keep_mask = (bit_index[None, None, :] < bit_limit[None, :, None]) & (
        is_pilot[:, None, None] == 0.0
    )
    return jnp.where(keep_mask, llr_values, jnp.float32(0.0))


def solution(mesh):
    in_specs = (
        P(None, None, "sc", "panel"),
        P("panel"),
        P("panel", None),
        P(),
        P(None, ("panel", "sc")),
        P(("panel", "sc")),
        P(),
        P(),
        P(),
        P(),
        P(),
        P(),
    )
    out_specs = P(None, ("panel", "sc"), None)
    return jax.shard_map(
        per_device, mesh=mesh, in_specs=in_specs, out_specs=out_specs, check_vma=False
    )
```

profile of v0, /device:TPU:36, one launch (start us, length us, event | category | flops | bytes accessed | tf_op | source)
XLA Modules:
  0.0 177.4 jit_solution(18392152177469189183)
XLA Ops:
  6.5 0.7 compare_and_fusion
  7.3 1.4 gather_fusion
  9.2 4.4 %convert_bitcast_fusion = bf16[16,14,32,128]{3,2,1,0:T(8,128)(2,1)} fusion(bf16[256,128,1,1]{1,0,3,2:T(8,128)(2,1)S(1)} %bitcast.166, bf16[16,14,32,256]{3,2,1,0:T(8,128)(2,1)} %param.12), kind=kOutput, calls=%fused_computation.1 | convolution fusion | flops 470679552 | bytes 5570560 | tf_op jit(solution)/shard_map/gtsk,kc->gtsc/dot_general | solution.py:79
  13.7 74.2 %reduce-scatter.2.cloned.1.call-done = bf16[1,14,32,128]{3,2,1,0:T(8,128)(2,1)} async-done(((bf16[16,14,32,128]{3,2,1,0:T(8,128)(2,1)}), bf16[1,14,32,128]{3,2,1,0:T(8,128)(2,1)}) %reduce-scatter.2.cloned.1.call-update) | async-done | bytes 114704 | tf_op jit(solution)/shard_map/reduce_scatter | solution.py:78
  87.9 1.0 bitcast_convert_fusion
  89.2 0.8 pad_maximum_fusion.16
  90.0 3.9 %collective-permute-start = (bf16[14,1,256]{2,1,0:T(2,128)(2,1)S(1)}, bf16[14,1,256]{2,1,0:T(2,128)(2,1)S(1)}, u32[]{:S(2)}, u32[]{:S(2)}) collective-permute-start(bf16[14,1,256]{2,1,0:T(2,128)(2,1)S(1)} %get-tuple-element.14), channel_id=1, source_target_pairs={{0,1},{1,2},{2,3},{3,4},{4,5},{5,6},{6,7},{7,8},{8,9},{9,10},{10,1... | collective-permute-start | bytes 21512 | tf_op jit(solution)/shard_map/ppermute | solution.py:18
  93.9 3.4 %collective-permute-start.1 = (bf16[14,1,256]{2,1,0:T(2,128)(2,1)S(1)}, bf16[14,1,256]{2,1,0:T(2,128)(2,1)S(1)}, u32[]{:S(2)}, u32[]{:S(2)}) collective-permute-start(bf16[14,1,256]{2,1,0:T(2,128)(2,1)S(1)} %get-tuple-element.15), channel_id=1, source_target_pairs={{1,0},{2,1},{3,2},{4,3},{5,4},{6,5},{7,6},{8,7},{9,8},{10,9},{11,1... | collective-permute-start | bytes 21512 | tf_op jit(solution)/shard_map/ppermute | solution.py:20
  97.4 4.5 %collective-permute-done.1 = bf16[14,1,256]{2,1,0:T(2,128)(2,1)S(1)} collective-permute-done((bf16[14,1,256]{2,1,0:T(2,128)(2,1)S(1)}, bf16[14,1,256]{2,1,0:T(2,128)(2,1)S(1)}, u32[]{:S(2)}, u32[]{:S(2)}) %collective-permute-start.1) | collective-permute-done | bytes 7200 | tf_op jit(solution)/shard_map/ppermute | solution.py:20
  102.8 0.7 fusion.9
  103.5 3.5 %collective-permute-start.2 = (bf16[14,1,128]{2,1,0:T(2,128)(2,1)S(1)}, bf16[14,1,128]{2,1,0:T(2,128)(2,1)S(1)}, u32[]{:S(2)}, u32[]{:S(2)}) collective-permute-start(bf16[14,1,128]{2,1,0:T(2,128)(2,1)S(1)} %get-tuple-element.64), channel_id=1, source_target_pairs={{0,1},{1,2},{2,3},{3,4},{4,5},{5,6},{6,7},{7,8},{8,9},{9,10},{10,1... | collective-permute-start | bytes 10760 | tf_op jit(solution)/shard_map/ppermute | solution.py:18
  107.1 3.8 %collective-permute-start.3 = (bf16[14,1,128]{2,1,0:T(2,128)(2,1)S(1)}, bf16[14,1,128]{2,1,0:T(2,128)(2,1)S(1)}, u32[]{:S(2)}, u32[]{:S(2)}) collective-permute-start(bf16[14,1,128]{2,1,0:T(2,128)(2,1)S(1)} %get-tuple-element.65), channel_id=1, source_target_pairs={{1,0},{2,1},{3,2},{4,3},{5,4},{6,5},{7,6},{8,7},{9,8},{10,9},{11,1... | collective-permute-start | bytes 10760 | tf_op jit(solution)/shard_map/ppermute | solution.py:20
  111.0 4.0 %collective-permute-done.3 = bf16[14,1,128]{2,1,0:T(2,128)(2,1)S(1)} collective-permute-done((bf16[14,1,128]{2,1,0:T(2,128)(2,1)S(1)}, bf16[14,1,128]{2,1,0:T(2,128)(2,1)S(1)}, u32[]{:S(2)}, u32[]{:S(2)}) %collective-permute-start.3) | collective-permute-done | bytes 3616 | tf_op jit(solution)/shard_map/ppermute | solution.py:20
  115.6 0.4 fusion.10
  116.1 3.9 %collective-permute-start.4 = (bf16[14,1,128]{2,1,0:T(2,128)(2,1)S(1)}, bf16[14,1,128]{2,1,0:T(2,128)(2,1)S(1)}, u32[]{:S(2)}, u32[]{:S(2)}) collective-permute-start(bf16[14,1,128]{2,1,0:T(2,128)(2,1)S(1)} %get-tuple-element.60), channel_id=1, source_target_pairs={{0,1},{1,2},{2,3},{3,4},{4,5},{5,6},{6,7},{7,8},{8,9},{9,10},{10,1... | collective-permute-start | bytes 10760 | tf_op jit(solution)/shard_map/ppermute | solution.py:18
  120.0 3.4 %collective-permute-start.5 = (bf16[14,1,128]{2,1,0:T(2,128)(2,1)S(1)}, bf16[14,1,128]{2,1,0:T(2,128)(2,1)S(1)}, u32[]{:S(2)}, u32[]{:S(2)}) collective-permute-start(bf16[14,1,128]{2,1,0:T(2,128)(2,1)S(1)} %get-tuple-element.61), channel_id=1, source_target_pairs={{1,0},{2,1},{3,2},{4,3},{5,4},{6,5},{7,6},{8,7},{9,8},{10,9},{11,1... | collective-permute-start | bytes 10760 | tf_op jit(solution)/shard_map/ppermute | solution.py:20
  123.4 4.5 %collective-permute-done.5 = bf16[14,1,128]{2,1,0:T(2,128)(2,1)S(1)} collective-permute-done((bf16[14,1,128]{2,1,0:T(2,128)(2,1)S(1)}, bf16[14,1,128]{2,1,0:T(2,128)(2,1)S(1)}, u32[]{:S(2)}, u32[]{:S(2)}) %collective-permute-start.5) | collective-permute-done | bytes 3616 | tf_op jit(solution)/shard_map/ppermute | solution.py:20
  128.5 0.4 fusion.11
  129.0 4.4 %collective-permute-start.6 = (bf16[14,1,128]{2,1,0:T(2,128)(2,1)S(1)}, bf16[14,1,128]{2,1,0:T(2,128)(2,1)S(1)}, u32[]{:S(2)}, u32[]{:S(2)}) collective-permute-start(bf16[14,1,128]{2,1,0:T(2,128)(2,1)S(1)} %get-tuple-element.56), channel_id=1, source_target_pairs={{0,1},{1,2},{2,3},{3,4},{4,5},{5,6},{6,7},{7,8},{8,9},{9,10},{10,1... | collective-permute-start | bytes 10760 | tf_op jit(solution)/shard_map/ppermute | solution.py:18
  133.4 2.9 %collective-permute-start.7 = (bf16[14,1,128]{2,1,0:T(2,128)(2,1)S(1)}, bf16[14,1,128]{2,1,0:T(2,128)(2,1)S(1)}, u32[]{:S(2)}, u32[]{:S(2)}) collective-permute-start(bf16[14,1,128]{2,1,0:T(2,128)(2,1)S(1)} %get-tuple-element.57), channel_id=1, source_target_pairs={{1,0},{2,1},{3,2},{4,3},{5,4},{6,5},{7,6},{8,7},{9,8},{10,9},{11,1... | collective-permute-start | bytes 10760 | tf_op jit(solution)/shard_map/ppermute | solution.py:20
  136.4 5.0 %collective-permute-done.7 = bf16[14,1,128]{2,1,0:T(2,128)(2,1)S(1)} collective-permute-done((bf16[14,1,128]{2,1,0:T(2,128)(2,1)S(1)}, bf16[14,1,128]{2,1,0:T(2,128)(2,1)S(1)}, u32[]{:S(2)}, u32[]{:S(2)}) %collective-permute-start.7) | collective-permute-done | bytes 3616 | tf_op jit(solution)/shard_map/ppermute | solution.py:20
  142.0 0.4 fusion.12
  142.4 5.4 %collective-permute-start.8 = (bf16[14,1,128]{2,1,0:T(2,128)(2,1)S(1)}, bf16[14,1,128]{2,1,0:T(2,128)(2,1)S(1)}, u32[]{:S(2)}, u32[]{:S(2)}) collective-permute-start(bf16[14,1,128]{2,1,0:T(2,128)(2,1)S(1)} %get-tuple-element.52), channel_id=1, source_target_pairs={{0,1},{1,2},{2,3},{3,4},{4,5},{5,6},{6,7},{7,8},{8,9},{9,10},{10,1... | collective-permute-start | bytes 10760 | tf_op jit(solution)/shard_map/ppermute | solution.py:18
  147.9 1.9 %collective-permute-start.9 = (bf16[14,1,128]{2,1,0:T(2,128)(2,1)S(1)}, bf16[14,1,128]{2,1,0:T(2,128)(2,1)S(1)}, u32[]{:S(2)}, u32[]{:S(2)}) collective-permute-start(bf16[14,1,128]{2,1,0:T(2,128)(2,1)S(1)} %get-tuple-element.53), channel_id=1, source_target_pairs={{1,0},{2,1},{3,2},{4,3},{5,4},{6,5},{7,6},{8,7},{9,8},{10,9},{11,1... | collective-permute-start | bytes 10760 | tf_op jit(solution)/shard_map/ppermute | solution.py:20
  150.0 5.8 %collective-permute-done.9 = bf16[14,1,128]{2,1,0:T(2,128)(2,1)S(1)} collective-permute-done((bf16[14,1,128]{2,1,0:T(2,128)(2,1)S(1)}, bf16[14,1,128]{2,1,0:T(2,128)(2,1)S(1)}, u32[]{:S(2)}, u32[]{:S(2)}) %collective-permute-start.9) | collective-permute-done | bytes 3616 | tf_op jit(solution)/shard_map/ppermute | solution.py:20
  156.4 0.4 fusion.13
  156.9 3.5 %collective-permute-start.10 = (bf16[14,1,128]{2,1,0:T(2,128)(2,1)S(1)}, bf16[14,1,128]{2,1,0:T(2,128)(2,1)S(1)}, u32[]{:S(2)}, u32[]{:S(2)}) collective-permute-start(bf16[14,1,128]{2,1,0:T(2,128)(2,1)S(1)} %get-tuple-element.48), channel_id=1, source_target_pairs={{0,1},{1,2},{2,3},{3,4},{4,5},{5,6},{6,7},{7,8},{8,9},{9,10},{10,1... | collective-permute-start | bytes 10760 | tf_op jit(solution)/shard_map/ppermute | solution.py:18
  160.4 3.8 %collective-permute-start.11 = (bf16[14,1,128]{2,1,0:T(2,128)(2,1)S(1)}, bf16[14,1,128]{2,1,0:T(2,128)(2,1)S(1)}, u32[]{:S(2)}, u32[]{:S(2)}) collective-permute-start(bf16[14,1,128]{2,1,0:T(2,128)(2,1)S(1)} %get-tuple-element.49), channel_id=1, source_target_pairs={{1,0},{2,1},{3,2},{4,3},{5,4},{6,5},{7,6},{8,7},{9,8},{10,9},{11,1... | collective-permute-start | bytes 10760 | tf_op jit(solution)/shard_map/ppermute | solution.py:20
  164.3 4.0 %collective-permute-done.11 = bf16[14,1,128]{2,1,0:T(2,128)(2,1)S(1)} collective-permute-done((bf16[14,1,128]{2,1,0:T(2,128)(2,1)S(1)}, bf16[14,1,128]{2,1,0:T(2,128)(2,1)S(1)}, u32[]{:S(2)}, u32[]{:S(2)}) %collective-permute-start.11) | collective-permute-done | bytes 3616 | tf_op jit(solution)/shard_map/ppermute | solution.py:20
  168.9 0.4 fusion.14
  169.4 0.4 fusion.8
  169.8 0.8 and_select_fusion
  (123 shorter events, 4.6 us)
Async XLA Ops:
  6.5 96.2 %copy-start = (bf16[3,3,256,128]{3,2,1,0:T(8,128)(2,1)S(1)}, bf16[3,3,256,128]{3,2,1,0:T(8,128)(2,1)}, u32[]{:S(2)}) copy-start(bf16[3,3,256,128]{3,2,1,0:T(8,128)(2,1)} %param.18) | copy-start | bytes 1769476
  6.5 81.4 %reduce-scatter.2.cloned.1.call-start = ((), (), s32[]{:S(2)}) async-start(), calls=%async_computation.1 | async-start | bytes 1949696 | tf_op jit(solution)/shard_map/reduce_scatter | solution.py:78
  9.1 4.5 %copy-start.8 = (s32[2]{0:T(128)S(1)}, s32[2]{0:T(128)}, u32[]{:S(2)}) copy-start(s32[2]{0:T(128)} %param.15) | copy-start | bytes 28
  9.2 4.6 %copy-start.7 = (f32[2,32]{1,0:T(2,128)S(1)}, f32[2,32]{1,0:T(2,128)}, u32[]{:S(2)}) copy-start(f32[2,32]{1,0:T(2,128)} %param.16) | copy-start | bytes 772
  13.6 83.8 %copy-start.5 = (f32[6,128]{1,0:T(8,128)S(1)}, f32[6,128]{1,0:T(8,128)}, u32[]{:S(2)}) copy-start(f32[6,128]{1,0:T(8,128)} %param.20) | copy-start | bytes 9220
  87.9 14.0 %copy-start.1 = (bf16[1,14,32,128]{3,2,1,0:T(8,128)(2,1)S(1)}, bf16[1,14,32,128]{3,2,1,0:T(8,128)(2,1)}, u32[]{:S(2)}) copy-start(bf16[1,14,32,128]{3,2,1,0:T(8,128)(2,1)} %reduce-scatter.2.cloned.1.call-done) | copy-start | bytes 344068
  90.0 7.4 %collective-permute-start = (bf16[14,1,256]{2,1,0:T(2,128)(2,1)S(1)}, bf16[14,1,256]{2,1,0:T(2,128)(2,1)S(1)}, u32[]{:S(2)}, u32[]{:S(2)}) collective-permute-start(bf16[14,1,256]{2,1,0:T(2,128)(2,1)S(1)} %get-tuple-element.14), channel_id=1, source_target_pairs={{0,1},{1,2},{2,3},{3,4},{4,5},{5,6},{6,7},{7,8},{8,9},{9,10},{10,1... | collective-permute-start | bytes 21512 | tf_op jit(solution)/shard_map/ppermute | solution.py:18
  93.9 8.0 %collective-permute-start.1 = (bf16[14,1,256]{2,1,0:T(2,128)(2,1)S(1)}, bf16[14,1,256]{2,1,0:T(2,128)(2,1)S(1)}, u32[]{:S(2)}, u32[]{:S(2)}) collective-permute-start(bf16[14,1,256]{2,1,0:T(2,128)(2,1)S(1)} %get-tuple-element.15), channel_id=1, source_target_pairs={{1,0},{2,1},{3,2},{4,3},{5,4},{6,5},{7,6},{8,7},{9,8},{10,9},{11,1... | collective-permute-start | bytes 21512 | tf_op jit(solution)/shard_map/ppermute | solution.py:20
  102.8 8.1 %copy-start.2 = (bf16[5,3,3,128,128]{4,3,2,1,0:T(8,128)(2,1)S(1)}, bf16[5,3,3,128,128]{4,3,2,1,0:T(8,128)(2,1)}, u32[]{:S(2)}) copy-start(bf16[5,3,3,128,128]{4,3,2,1,0:T(8,128)(2,1)} %param.19) | copy-start | bytes 4423684
  103.5 7.5 %collective-permute-start.2 = (bf16[14,1,128]{2,1,0:T(2,128)(2,1)S(1)}, bf16[14,1,128]{2,1,0:T(2,128)(2,1)S(1)}, u32[]{:S(2)}, u32[]{:S(2)}) collective-permute-start(bf16[14,1,128]{2,1,0:T(2,128)(2,1)S(1)} %get-tuple-element.64), channel_id=1, source_target_pairs={{0,1},{1,2},{2,3},{3,4},{4,5},{5,6},{6,7},{7,8},{8,9},{9,10},{10,1... | collective-permute-start | bytes 10760 | tf_op jit(solution)/shard_map/ppermute | solution.py:18
  107.1 7.9 %collective-permute-start.3 = (bf16[14,1,128]{2,1,0:T(2,128)(2,1)S(1)}, bf16[14,1,128]{2,1,0:T(2,128)(2,1)S(1)}, u32[]{:S(2)}, u32[]{:S(2)}) collective-permute-start(bf16[14,1,128]{2,1,0:T(2,128)(2,1)S(1)} %get-tuple-element.65), channel_id=1, source_target_pairs={{1,0},{2,1},{3,2},{4,3},{5,4},{6,5},{7,6},{8,7},{9,8},{10,9},{11,1... | collective-permute-start | bytes 10760 | tf_op jit(solution)/shard_map/ppermute | solution.py:20
  116.1 7.4 %collective-permute-start.4 = (bf16[14,1,128]{2,1,0:T(2,128)(2,1)S(1)}, bf16[14,1,128]{2,1,0:T(2,128)(2,1)S(1)}, u32[]{:S(2)}, u32[]{:S(2)}) collective-permute-start(bf16[14,1,128]{2,1,0:T(2,128)(2,1)S(1)} %get-tuple-element.60), channel_id=1, source_target_pairs={{0,1},{1,2},{2,3},{3,4},{4,5},{5,6},{6,7},{7,8},{8,9},{9,10},{10,1... | collective-permute-start | bytes 10760 | tf_op jit(solution)/shard_map/ppermute | solution.py:18
  120.0 7.9 %collective-permute-start.5 = (bf16[14,1,128]{2,1,0:T(2,128)(2,1)S(1)}, bf16[14,1,128]{2,1,0:T(2,128)(2,1)S(1)}, u32[]{:S(2)}, u32[]{:S(2)}) collective-permute-start(bf16[14,1,128]{2,1,0:T(2,128)(2,1)S(1)} %get-tuple-element.61), channel_id=1, source_target_pairs={{1,0},{2,1},{3,2},{4,3},{5,4},{6,5},{7,6},{8,7},{9,8},{10,9},{11,1... | collective-permute-start | bytes 10760 | tf_op jit(solution)/shard_map/ppermute | solution.py:20
  128.1 8.3 %copy-start.9 = (s32[8]{0:T(128)S(1)}, s32[8]{0:T(128)}, u32[]{:S(2)}) copy-start(s32[8]{0:T(128)} %param.17) | copy-start | bytes 100
  129.0 7.4 %collective-permute-start.6 = (bf16[14,1,128]{2,1,0:T(2,128)(2,1)S(1)}, bf16[14,1,128]{2,1,0:T(2,128)(2,1)S(1)}, u32[]{:S(2)}, u32[]{:S(2)}) collective-permute-start(bf16[14,1,128]{2,1,0:T(2,128)(2,1)S(1)} %get-tuple-element.56), channel_id=1, source_target_pairs={{0,1},{1,2},{2,3},{3,4},{4,5},{5,6},{6,7},{7,8},{8,9},{9,10},{10,1... | collective-permute-start | bytes 10760 | tf_op jit(solution)/shard_map/ppermute | solution.py:18
  133.4 7.9 %collective-permute-start.7 = (bf16[14,1,128]{2,1,0:T(2,128)(2,1)S(1)}, bf16[14,1,128]{2,1,0:T(2,128)(2,1)S(1)}, u32[]{:S(2)}, u32[]{:S(2)}) collective-permute-start(bf16[14,1,128]{2,1,0:T(2,128)(2,1)S(1)} %get-tuple-element.57), channel_id=1, source_target_pairs={{1,0},{2,1},{3,2},{4,3},{5,4},{6,5},{7,6},{8,7},{9,8},{10,9},{11,1... | collective-permute-start | bytes 10760 | tf_op jit(solution)/shard_map/ppermute | solution.py:20
  142.4 7.5 %collective-permute-start.8 = (bf16[14,1,128]{2,1,0:T(2,128)(2,1)S(1)}, bf16[14,1,128]{2,1,0:T(2,128)(2,1)S(1)}, u32[]{:S(2)}, u32[]{:S(2)}) collective-permute-start(bf16[14,1,128]{2,1,0:T(2,128)(2,1)S(1)} %get-tuple-element.52), channel_id=1, source_target_pairs={{0,1},{1,2},{2,3},{3,4},{4,5},{5,6},{6,7},{7,8},{8,9},{9,10},{10,1... | collective-permute-start | bytes 10760 | tf_op jit(solution)/shard_map/ppermute | solution.py:18
  147.9 7.9 %collective-permute-start.9 = (bf16[14,1,128]{2,1,0:T(2,128)(2,1)S(1)}, bf16[14,1,128]{2,1,0:T(2,128)(2,1)S(1)}, u32[]{:S(2)}, u32[]{:S(2)}) collective-permute-start(bf16[14,1,128]{2,1,0:T(2,128)(2,1)S(1)} %get-tuple-element.53), channel_id=1, source_target_pairs={{1,0},{2,1},{3,2},{4,3},{5,4},{6,5},{7,6},{8,7},{9,8},{10,9},{11,1... | collective-permute-start | bytes 10760 | tf_op jit(solution)/shard_map/ppermute | solution.py:20
  156.9 7.4 %collective-permute-start.10 = (bf16[14,1,128]{2,1,0:T(2,128)(2,1)S(1)}, bf16[14,1,128]{2,1,0:T(2,128)(2,1)S(1)}, u32[]{:S(2)}, u32[]{:S(2)}) collective-permute-start(bf16[14,1,128]{2,1,0:T(2,128)(2,1)S(1)} %get-tuple-element.48), channel_id=1, source_target_pairs={{0,1},{1,2},{2,3},{3,4},{4,5},{5,6},{6,7},{7,8},{8,9},{9,10},{10,1... | collective-permute-start | bytes 10760 | tf_op jit(solution)/shard_map/ppermute | solution.py:18
  160.4 7.9 %collective-permute-start.11 = (bf16[14,1,128]{2,1,0:T(2,128)(2,1)S(1)}, bf16[14,1,128]{2,1,0:T(2,128)(2,1)S(1)}, u32[]{:S(2)}, u32[]{:S(2)}) collective-permute-start(bf16[14,1,128]{2,1,0:T(2,128)(2,1)S(1)} %get-tuple-element.49), channel_id=1, source_target_pairs={{1,0},{2,1},{3,2},{4,3},{5,4},{6,5},{7,6},{8,7},{9,8},{10,9},{11,1... | collective-permute-start | bytes 10760 | tf_op jit(solution)/shard_map/ppermute | solution.py:20
  168.5 0.9 copy-start.3
  168.5 0.9 copy-start.4
  168.5 0.9 copy-start.6
Sparse Core Ops, SparseCore 0:
  13.7 74.1 reduce-scatter.1
where the time goes:
time: 179 us; the launch traced here: 177 us
  waiting for transfers between devices  102 us (57%)
  starting transfers between devices  44.1 us (25%)
  between operations  14.3 us (8%)
  matrix products  7.69 us (4%)
  other arithmetic  5.19 us (3%)
  local copies, waits for them, and re-layouts  4.06 us (2%)
    reduce_scatter x1, waiting for transfers between devices, per_device(): lax.psum_scatter(jnp.einsum('gtsk,kc->gtsc', captured_waveform, matrix, p...  74.2 us
    ppermute x6, waiting for transfers between devices, with_halo(): lax.ppermute(head, axis, [((i + 1) % count, i) for i in range(ends)])  27.8 us
    ppermute x6, starting transfers between devices, with_halo(): lax.ppermute(tail, axis, [(i, (i + 1) % count) for i in range(ends)])  24.7 us
    ppermute x6, starting transfers between devices, with_halo(): lax.ppermute(head, axis, [((i + 1) % count, i) for i in range(ends)])  19.3 us
    dot_general x1, matrix products, per_device(): jnp.einsum('gtsk,kc->gtsc', captured_waveform, matrix, preferred_element_...  4.42 us
  transfers between devices with their start and end apart: 13, of which 7 were waited for; matrix products, arithmetic and copies ran while one was open for 0% of the time, Pallas kernels for 0%

commit v1 on v0

v1 whole, which is shorter than its diff:
```python
import jax
import jax.numpy as jnp
from jax import lax
from jax.experimental import pallas as pl
from jax.experimental.pallas import tpu as pltpu
from jax.sharding import PartitionSpec as P

RB_SC = 4
BITS = 8
EDGE = 8
PANEL = "panel"
SUB = "sc"


def lookup_matrix(lookup, rows):
    n, c = rows.shape
    member = lax.broadcasted_iota(jnp.int32, (n, n), 0) == lookup % n
    picked = lax.dot_general(
        member.astype(jnp.bfloat16), rows, (((0,), (0,)), ((), ())), preferred_element_type=jnp.float32
    ).astype(jnp.bfloat16)
    doubled = (
        lax.broadcasted_iota(jnp.int32, (2 * n, n), 0) // 2 == lax.broadcasted_iota(jnp.int32, (2 * n, n), 1)
    )
    w = jnp.dot(doubled.astype(jnp.bfloat16), picked, preferred_element_type=jnp.float32)
    lane = lax.broadcasted_iota(jnp.int32, w.shape, 1)
    turned = pltpu.roll(w, c // 2, 1) * jnp.where(lane < c // 2, -1.0, 1.0)
    odd = lax.broadcasted_iota(jnp.int32, w.shape, 0) % 2 == 1
    return jnp.where(odd, turned, w).astype(jnp.bfloat16)


def partial_kernel(lookup_ref, rows_ref, wave_ref, out_ref, matrix_ref):
    @pl.when(pl.program_id(0) == 0)
    def _():
        matrix_ref[...] = lookup_matrix(lookup_ref[...], rows_ref[...])

    g, t, s, k = wave_ref.shape
    out_ref[...] = (
        jnp.dot(wave_ref[...].reshape(g * t * s, k), matrix_ref[...], preferred_element_type=jnp.float32)
        .astype(jnp.bfloat16)
        .reshape(out_ref.shape)
    )


def beam_partials(wave, lookup, rows, step):
    groups, syms, subs, k = wave.shape
    c = rows.shape[1]
    return pl.pallas_call(
        partial_kernel,
        grid=(groups // step,),
        in_specs=[
            pl.BlockSpec((1, lookup.shape[0]), lambda i: (0, 0)),
            pl.BlockSpec(rows.shape, lambda i: (0, 0)),
            pl.BlockSpec((step, syms, subs, k), lambda i: (i, 0, 0, 0)),
        ],
        out_specs=pl.BlockSpec((step, syms, subs, c), lambda i: (i, 0, 0, 0)),
        out_shape=jax.ShapeDtypeStruct((groups, syms, subs, c), jnp.bfloat16),
        scratch_shapes=[pltpu.VMEM((k, c), jnp.bfloat16)],
        compiler_params=pltpu.CompilerParams(vmem_limit_bytes=16 * 2**20),
        name="partials",
    )(lookup.reshape(1, -1), rows, wave)


def as_column(row, count):
    diagonal = lax.broadcasted_iota(jnp.int32, (count, count), 0) == lax.broadcasted_iota(
        jnp.int32, (count, count), 1
    )
    return jnp.sum(jnp.where(diagonal, jnp.broadcast_to(row, (count, count)), 0.0), axis=1, keepdims=True)


def estimate_of(beams, pilot_re, pilot_im):
    c = beams.shape[-1]
    return beams * pilot_re + pltpu.roll(beams, c // 2, beams.ndim - 1) * pilot_im


def signed_pilots(pilot_ref, c):
    s = pilot_ref.shape[1]
    re = jnp.broadcast_to(as_column(pilot_ref[0:1, :], s), (s, c))
    im = jnp.broadcast_to(as_column(pilot_ref[1:2, :], s), (s, c))
    lane = lax.broadcasted_iota(jnp.int32, (s, c), 1)
    return re, jnp.where(lane < c // 2, im, -im)


def sum_kernel(syms_ref, pilot_ref, parts_ref, own_ref, head_ref, tail_ref):
    panels, syms, subs, c = parts_ref.shape
    re, im = signed_pilots(pilot_ref, c)
    for t in range(syms):
        total = parts_ref[0, t].astype(jnp.float32)
        for p in range(1, panels):
            total = total + parts_ref[p, t].astype(jnp.float32)
        beams = total.astype(jnp.bfloat16)
        is_pilot = jnp.where((syms_ref[0] == t) | (syms_ref[1] == t), 1.0, 0.0)
        estimate = (estimate_of(beams.astype(jnp.float32), re, im) * is_pilot).astype(jnp.bfloat16)
        own_ref[t, :, :c] = beams
        own_ref[t, :, c:] = estimate
        head_ref[t, :, :c] = beams[:EDGE]
        head_ref[t, :, c:] = estimate[:EDGE]
        tail_ref[t, :, :c] = beams[subs - EDGE :]
        tail_ref[t, :, c:] = estimate[subs - EDGE :]


def sum_beams(parts, pilot_syms, pilot_values):
    _, syms, subs, c = parts.shape
    vmem = pl.BlockSpec(memory_space=pltpu.VMEM)
    return pl.pallas_call(
        sum_kernel,
        in_specs=[pl.BlockSpec(memory_space=pltpu.SMEM), vmem, vmem],
        out_specs=[vmem] * 3,
        out_shape=[
            jax.ShapeDtypeStruct((syms, subs, 2 * c), jnp.bfloat16),
            jax.ShapeDtypeStruct((syms, EDGE, 2 * c), jnp.bfloat16),
            jax.ShapeDtypeStruct((syms, EDGE, 2 * c), jnp.bfloat16),
        ],
        compiler_params=pltpu.CompilerParams(vmem_limit_bytes=16 * 2**20),
        name="sum_beams",
    )(pilot_syms, pilot_values, parts)


def receiver_kernel(
    ends_ref, syms_ref, order_ref, own_ref, left_ref, right_ref, first_ref, rest_ref, bias_ref,
    in_ref, in_bias_ref, out_w_ref, llr_ref, wide_ref, even_ref, odd_ref,
):
    syms, subs, feats = own_ref.shape
    layers = rest_ref.shape[0] + 1
    width = subs + 2 * EDGE
    rows = syms * width
    c = bias_ref.shape[1]
    skip = EDGE - layers

    def put(ref, whole, ch):
        for shift in range(3):
            moved = whole if shift == 0 else pltpu.roll(whole, rows - shift, 0)
            ref[width : width + rows, shift * ch : (shift + 1) * ch] = moved.astype(jnp.bfloat16)

    for ref in (wide_ref, even_ref, odd_ref):
        ref[0:width] = jnp.zeros((width, ref.shape[1]), jnp.bfloat16)
        ref[width + rows :] = jnp.zeros((width, ref.shape[1]), jnp.bfloat16)

    field = jnp.concatenate(
        [
            left_ref[...].astype(jnp.float32),
            own_ref[...].astype(jnp.float32),
            right_ref[...].astype(jnp.float32),
        ],
        axis=1,
    ).reshape(rows, feats)
    field = pltpu.roll(field, rows - skip, 0)
    put(wide_ref, field, feats)

    column = lax.broadcasted_iota(jnp.int32, (width, c), 0)
    src = wide_ref
    for layer in range(layers):
        kernel = first_ref[...] if layer == 0 else rest_ref[layer - 1]
        taps = jnp.concatenate([src[dt * width : dt * width + rows] for dt in range(3)], axis=1)
        total = jnp.dot(taps, kernel, preferred_element_type=jnp.float32)
        total = jnp.maximum(total + bias_ref[layer : layer + 1, :], 0.0)
        off = layers - 1 - layer
        inside = (column >= jnp.where(ends_ref[0] == 1, off, 0)) & (
            column < jnp.where(ends_ref[1] == 1, off + subs, width)
        )
        total = jnp.where(inside[None], total.reshape(syms, width, c), 0.0).reshape(rows, c)
        if layer < layers - 1:
            src = (even_ref, odd_ref)[layer % 2]
            put(src, total, c)

    final = total.astype(jnp.bfloat16).reshape(syms, width, c)[:, :subs].reshape(syms * subs, c)
    hidden = jnp.dot(final, in_ref[...], preferred_element_type=jnp.float32)
    hidden = jnp.maximum(hidden + in_bias_ref[...], 0.0).astype(jnp.bfloat16)
    llr = jnp.dot(hidden, out_w_ref[...], preferred_element_type=jnp.float32)
    bits = llr.shape[1]
    block = lax.broadcasted_iota(jnp.int32, (subs, bits), 0) // RB_SC
    limit = jnp.zeros((subs, bits), jnp.int32)
    for b in range(subs // RB_SC):
        limit = jnp.where(block == b, 2 * order_ref[b], limit)
    bit = lax.broadcasted_iota(jnp.int32, (subs, bits), 1) % BITS
    for t in range(syms):
        data = jnp.where((syms_ref[0] == t) | (syms_ref[1] == t), 0, 1)
        llr_ref[t] = jnp.where(bit < limit * data, llr[t * subs : (t + 1) * subs], 0.0)


def receive(ends, pilot_syms, mod_order, own, left, right, first, rest, bias, d_in, d_bias, d_out):
    syms, subs, feats = own.shape
    layers = bias.shape[0]
    c = bias.shape[1]
    width = subs + 2 * EDGE
    smem = pl.BlockSpec(memory_space=pltpu.SMEM)
    vmem = pl.BlockSpec(memory_space=pltpu.VMEM)
    padded = (syms + 2) * width
    return pl.pallas_call(
        receiver_kernel,
        in_specs=[smem] * 3 + [vmem] * 9,
        out_specs=vmem,
        out_shape=jax.ShapeDtypeStruct((syms, subs, d_out.shape[1]), jnp.float32),
        scratch_shapes=[
            pltpu.VMEM((padded, 3 * feats), jnp.bfloat16),
            pltpu.VMEM((padded, 3 * c), jnp.bfloat16),
            pltpu.VMEM((padded, 3 * c), jnp.bfloat16),
        ],
        compiler_params=pltpu.CompilerParams(vmem_limit_bytes=32 * 2**20),
        name="receiver",
    )(
        ends, pilot_syms, mod_order, own, left, right,
        first.reshape(9 * feats, c), rest.reshape(layers - 1, 9 * c, c), bias,
        d_in, d_bias.reshape(1, -1), d_out,
    )


def per_device(
    captured_waveform,
    element_lookup,
    combiner,
    pilot_syms,
    pilot_values,
    mod_order,
    conv_first,
    conv_rest,
    conv_bias,
    demap_in,
    demap_bias,
    demap_out,
):
    parts = beam_partials(captured_waveform, element_lookup, combiner, 2)
    parts = lax.all_to_all(parts, PANEL, 0, 0, tiled=True)
    own, head, tail = sum_beams(parts, pilot_syms, pilot_values)
    both = (PANEL, SUB)
    count = lax.axis_size(both)
    left = lax.ppermute(tail, both, [(i, i + 1) for i in range(count - 1)])
    right = lax.ppermute(head, both, [(i + 1, i) for i in range(count - 1)])
    at = lax.axis_index(both)
    ends = jnp.stack([at == 0, at == count - 1]).astype(jnp.int32)
    return receive(
        ends, pilot_syms, mod_order, own, left, right, conv_first, conv_rest, conv_bias,
        demap_in, demap_bias, demap_out,
    )


def solution(mesh):
    in_specs = (
        P(None, None, SUB, PANEL),
        P(PANEL),
        P(PANEL, None),
        P(),
        P(None, (PANEL, SUB)),
        P((PANEL, SUB)),
        P(),
        P(),
        P(),
        P(),
        P(),
        P(),
    )
    out_specs = P(None, (PANEL, SUB), None)
    return jax.shard_map(
        per_device, mesh=mesh, in_specs=in_specs, out_specs=out_specs, check_vma=False
    )
```

time: 179 us -> 66.2 us (0.37)
  the two profiles are of different devices: /device:TPU:36 before, /device:TPU:1 now
where the time goes in v1:
time: 66.2 us; the launch traced here: 65.4 us
  waiting for transfers between devices  26 us (39%)
  starting transfers between devices  22.9 us (35%)
  Pallas kernels  10.5 us (16%)
  local copies, waits for them, and re-layouts  5.81 us (9%)
    all_to_all x1, waiting for transfers between devices, per_device(): parts = lax.all_to_all(parts, PANEL, 0, 0, tiled=True)  24.9 us
    all_to_all x1, starting transfers between devices, per_device(): parts = lax.all_to_all(parts, PANEL, 0, 0, tiled=True)  10.5 us
    ppermute x1, starting transfers between devices, per_device(): right = lax.ppermute(head, both, [(i + 1, i) for i in range(count - 1)])  10.5 us
    pallas_call x1, Pallas kernels, receive(): pl.pallas_call(receiver_kernel, in_specs=[smem] * 3 + [vmem] * 9, out_spe...  6.86 us
    unnamed x26, local copies, waits for them, and re-layouts  5.81 us
    pallas_call x1, Pallas kernels, beam_partials(): pl.pallas_call(partial_kernel, grid=(groups // step,), in_specs=[pl.Block...  2.72 us
    ppermute x1, starting transfers between devices, per_device(): left = lax.ppermute(tail, both, [(i, i + 1) for i in range(count - 1)])  1.91 us
  transfers between devices with their start and end apart: 3, of which 2 were waited for; matrix products, arithmetic and copies ran while one was open for 0% of the time, Pallas kernels for 0%

profile of v1, /device:TPU:1, one launch (start us, length us, event | category | flops | bytes accessed | tf_op | source)
XLA Modules:
  0.0 65.4 jit_solution(152850822822195184)
XLA Ops:
  0.0 0.0 copy-start.1
  0.0 2.0 %copy-done.1 = bf16[16,14,32,256]{3,2,1,0:T(8,128)(2,1)S(1)} copy-done((bf16[16,14,32,256]{3,2,1,0:T(8,128)(2,1)S(1)}, bf16[16,14,32,256]{3,2,1,0:T(8,128)(2,1)}, u32[]{:S(2)}) %copy-start.1) | copy-done | bytes 3670040
  2.0 0.0 copy-start.6
  2.0 0.8 %copy-done.6 = bf16[128,128]{1,0:T(8,128)(2,1)S(1)} copy-done((bf16[128,128]{1,0:T(8,128)(2,1)S(1)}, bf16[128,128]{1,0:T(8,128)(2,1)}, u32[]{:S(2)}) %copy-start.6) | copy-done | bytes 32792
  2.8 0.7 copy-done.11
  3.5 2.7 %partials.1 = bf16[16,14,32,128]{3,2,1,0:T(8,128)(2,1)S(1)} custom-call(s32[1,128]{1,0:T(1,128)S(1)} %bitcast.9, bf16[128,128]{1,0:T(8,128)(2,1)S(1)} %copy-done.6, bf16[16,14,32,256]{3,2,1,0:T(8,128)(2,1)S(1)} %copy-done.1), custom_call_target="tpu_custom_call" | custom-call | tf_op jit(solution)/shard_map/partials/pallas_call | solution.py:47
  6.2 0.0 copy-start
  6.2 1.3 %copy-done = bf16[16,14,32,128]{3,2,1,0:T(8,128)(2,1)} copy-done((bf16[16,14,32,128]{3,2,1,0:T(8,128)(2,1)}, bf16[16,14,32,128]{3,2,1,0:T(8,128)(2,1)S(1)}, u32[]{:S(2)}) %copy-start) | copy-done | bytes 1835032
  7.4 10.5 %all-to-all-start = ((bf16[16,14,32,128]{3,2,1,0:T(8,128)(2,1)}), bf16[16,14,32,128]{3,2,1,0:T(8,128)(2,1)S(1)}, u32[]{:S(2)}, u32[]{:S(2)}) async-start(bf16[16,14,32,128]{3,2,1,0:T(8,128)(2,1)} %copy-done), calls=%async_computation | async-start | bytes 3670016 | tf_op jit(solution)/shard_map/all_to_all | solution.py:222
  18.0 0.0 copy-start.4
  18.0 0.0 copy-start.5
  18.0 0.0 copy-start.7
  18.0 0.0 copy-start.10
  18.0 0.0 copy-start.12
  18.0 24.9 %all-to-all-done.parts_ref = bf16[16,14,32,128]{3,2,1,0:T(8,128)(2,1)S(1)} async-done(((bf16[16,14,32,128]{3,2,1,0:T(8,128)(2,1)}), bf16[16,14,32,128]{3,2,1,0:T(8,128)(2,1)S(1)}, u32[]{:S(2)}, u32[]{:S(2)}) %all-to-all-start) | async-done | bytes 1835040 | tf_op jit(solution)/shard_map/all_to_all | solution.py:222
  42.9 0.0 copy-done.8
  42.9 0.0 copy-done.9
  42.9 0.9 %sum_beams.1 = (bf16[14,32,256]{2,1,0:T(8,128)(2,1)S(1)}, bf16[14,8,256]{2,1,0:T(8,128)(2,1)S(1)}, bf16[14,8,256]{2,1,0:T(8,128)(2,1)S(1)}) custom-call(s32[2]{0:T(128)S(1)} %copy-done.8, f32[2,32]{1,0:T(2,128)S(1)} %copy-done.9, bf16[16,14,32,128]{3,2,1,0:T(8,128)(2,1)S(1)} %all-to-all-done.parts_ref), custom_call_target="tpu_custom_call" | custom-call | tf_op jit(solution)/shard_map/sum_beams/pallas_call | solution.py:104
  43.8 1.9 %collective-permute-start = (bf16[14,8,256]{2,1,0:T(8,128)(2,1)S(1)}, bf16[14,8,256]{2,1,0:T(8,128)(2,1)S(1)}, u32[]{:S(2)}, u32[]{:S(2)}) collective-permute-start(bf16[14,8,256]{2,1,0:T(8,128)(2,1)S(1)} %get-tuple-element.9), channel_id=1, source_target_pairs={{0,1},{1,2},{2,3},{3,4},{4,5},{5,6},{6,7},{7,8},{8,9},{9,10},{10,1... | collective-permute-start | bytes 172040 | tf_op jit(solution)/shard_map/ppermute | solution.py:226
  45.7 10.5 %collective-permute-start.1 = (bf16[14,8,256]{2,1,0:T(8,128)(2,1)S(1)}, bf16[14,8,256]{2,1,0:T(8,128)(2,1)S(1)}, u32[]{:S(2)}, u32[]{:S(2)}) collective-permute-start(bf16[14,8,256]{2,1,0:T(8,128)(2,1)S(1)} %get-tuple-element.10), channel_id=1, source_target_pairs={{1,0},{2,1},{3,2},{4,3},{5,4},{6,5},{7,6},{8,7},{9,8},{10,9},{11,1... | collective-permute-start | bytes 172040 | tf_op jit(solution)/shard_map/ppermute | solution.py:227
  56.2 0.1 add_convert_fusion.ends_ref
  56.3 0.0 collective-permute-done.left_ref
  56.3 1.2 %collective-permute-done.1.right_ref = bf16[14,8,256]{2,1,0:T(8,128)(2,1)S(1)} collective-permute-done((bf16[14,8,256]{2,1,0:T(8,128)(2,1)S(1)}, bf16[14,8,256]{2,1,0:T(8,128)(2,1)S(1)}, u32[]{:S(2)}, u32[]{:S(2)}) %collective-permute-start.1) | collective-permute-done | bytes 57376 | tf_op jit(solution)/shard_map/ppermute | solution.py:227
  57.5 0.0 copy-done.2
  57.5 0.0 copy-done.4
  57.5 0.0 copy-done.5
  57.5 0.0 copy-done.7
  57.5 0.0 copy-done.10
  57.5 0.0 copy-done.12
  57.5 0.0 copy-start.3
  57.5 1.1 %copy-done.3 = bf16[3,3,256,128]{3,2,1,0:T(8,128)(2,1)S(1)} copy-done((bf16[3,3,256,128]{3,2,1,0:T(8,128)(2,1)S(1)}, bf16[3,3,256,128]{3,2,1,0:T(8,128)(2,1)}, u32[]{:S(2)}) %copy-start.3) | copy-done | bytes 589848
  58.6 6.9 %receiver.1 = f32[14,32,128]{2,1,0:T(8,128)} custom-call(s32[2]{0:T(128)S(1)} %add_convert_fusion.ends_ref, s32[2]{0:T(128)S(1)} %copy-done.8, s32[8]{0:T(128)S(1)} %copy-done.12, bf16[14,32,256]{2,1,0:T(8,128)(2,1)S(1)} %get-tuple-element.8.own_ref, bf16[14,8,256]{2,1,0:T(8,128)(2,1)S(1)} %collective-permute-done.left_ref, ...), custom_call_target="tpu_custom_call" | custom-call | tf_op jit(solution)/shard_map/receiver/pallas_call | solution.py:188
  (4 shorter events, 0.0 us)
Async XLA Ops:
  0.0 2.0 %copy-start.1 = (bf16[16,14,32,256]{3,2,1,0:T(8,128)(2,1)S(1)}, bf16[16,14,32,256]{3,2,1,0:T(8,128)(2,1)}, u32[]{:S(2)}) copy-start(bf16[16,14,32,256]{3,2,1,0:T(8,128)(2,1)} %wave_ref.1) | copy-start | bytes 11010052
  2.0 0.8 %copy-start.6 = (bf16[128,128]{1,0:T(8,128)(2,1)S(1)}, bf16[128,128]{1,0:T(8,128)(2,1)}, u32[]{:S(2)}) copy-start(bf16[128,128]{1,0:T(8,128)(2,1)} %rows_ref.1) | copy-start | bytes 98308
  2.8 0.7 %copy-start.11 = (s32[128]{0:T(128)S(1)}, s32[128]{0:T(128)}, u32[]{:S(2)}) copy-start(s32[128]{0:T(128)} %param.13) | copy-start | bytes 1540
  6.2 1.3 %copy-start = (bf16[16,14,32,128]{3,2,1,0:T(8,128)(2,1)}, bf16[16,14,32,128]{3,2,1,0:T(8,128)(2,1)S(1)}, u32[]{:S(2)}) copy-start(bf16[16,14,32,128]{3,2,1,0:T(8,128)(2,1)S(1)} %partials.1) | copy-start | bytes 5505028
  7.4 35.5 %copy-start.8 = (s32[2]{0:T(128)S(1)}, s32[2]{0:T(128)}, u32[]{:S(2)}) copy-start(s32[2]{0:T(128)} %syms_ref.3) | copy-start | bytes 28
  7.4 35.5 %copy-start.9 = (f32[2,32]{1,0:T(2,128)S(1)}, f32[2,32]{1,0:T(2,128)}, u32[]{:S(2)}) copy-start(f32[2,32]{1,0:T(2,128)} %pilot_ref.1) | copy-start | bytes 772
  7.4 35.5 %all-to-all-start = ((bf16[16,14,32,128]{3,2,1,0:T(8,128)(2,1)}), bf16[16,14,32,128]{3,2,1,0:T(8,128)(2,1)S(1)}, u32[]{:S(2)}, u32[]{:S(2)}) async-start(bf16[16,14,32,128]{3,2,1,0:T(8,128)(2,1)} %copy-done), calls=%async_computation | async-start | bytes 3670016 | tf_op jit(solution)/shard_map/all_to_all | solution.py:222
  18.0 39.5 %copy-start.2 = (bf16[5,3,3,128,128]{4,3,2,1,0:T(8,128)(2,1)S(1)}, bf16[5,3,3,128,128]{4,3,2,1,0:T(8,128)(2,1)}, u32[]{:S(2)}) copy-start(bf16[5,3,3,128,128]{4,3,2,1,0:T(8,128)(2,1)} %param.19) | copy-start | bytes 4423684
  18.0 39.5 %copy-start.4 = (bf16[128,256]{1,0:T(8,128)(2,1)S(1)}, bf16[128,256]{1,0:T(8,128)(2,1)}, u32[]{:S(2)}) copy-start(bf16[128,256]{1,0:T(8,128)(2,1)} %in_ref.1) | copy-start | bytes 196612
  18.0 39.5 %copy-start.5 = (bf16[256,128]{1,0:T(8,128)(2,1)S(1)}, bf16[256,128]{1,0:T(8,128)(2,1)}, u32[]{:S(2)}) copy-start(bf16[256,128]{1,0:T(8,128)(2,1)} %out_w_ref.1) | copy-start | bytes 196612
  18.0 39.5 %copy-start.7 = (f32[6,128]{1,0:T(8,128)S(1)}, f32[6,128]{1,0:T(8,128)}, u32[]{:S(2)}) copy-start(f32[6,128]{1,0:T(8,128)} %bias_ref.1) | copy-start | bytes 9220
  18.0 39.5 %copy-start.10 = (f32[256]{0:T(256)S(1)}, f32[256]{0:T(256)}, u32[]{:S(2)}) copy-start(f32[256]{0:T(256)} %param.22) | copy-start | bytes 3076
  18.0 39.5 %copy-start.12 = (s32[8]{0:T(128)S(1)}, s32[8]{0:T(128)}, u32[]{:S(2)}) copy-start(s32[8]{0:T(128)} %order_ref.1) | copy-start | bytes 100
  43.8 12.5 %collective-permute-start = (bf16[14,8,256]{2,1,0:T(8,128)(2,1)S(1)}, bf16[14,8,256]{2,1,0:T(8,128)(2,1)S(1)}, u32[]{:S(2)}, u32[]{:S(2)}) collective-permute-start(bf16[14,8,256]{2,1,0:T(8,128)(2,1)S(1)} %get-tuple-element.9), channel_id=1, source_target_pairs={{0,1},{1,2},{2,3},{3,4},{4,5},{5,6},{6,7},{7,8},{8,9},{9,10},{10,1... | collective-permute-start | bytes 172040 | tf_op jit(solution)/shard_map/ppermute | solution.py:226
  45.7 11.7 %collective-permute-start.1 = (bf16[14,8,256]{2,1,0:T(8,128)(2,1)S(1)}, bf16[14,8,256]{2,1,0:T(8,128)(2,1)S(1)}, u32[]{:S(2)}, u32[]{:S(2)}) collective-permute-start(bf16[14,8,256]{2,1,0:T(8,128)(2,1)S(1)} %get-tuple-element.10), channel_id=1, source_target_pairs={{1,0},{2,1},{3,2},{4,3},{5,4},{6,5},{7,6},{8,7},{9,8},{10,9},{11,1... | collective-permute-start | bytes 172040 | tf_op jit(solution)/shard_map/ppermute | solution.py:227
  57.5 1.1 %copy-start.3 = (bf16[3,3,256,128]{3,2,1,0:T(8,128)(2,1)S(1)}, bf16[3,3,256,128]{3,2,1,0:T(8,128)(2,1)}, u32[]{:S(2)}) copy-start(bf16[3,3,256,128]{3,2,1,0:T(8,128)(2,1)} %param.18) | copy-start | bytes 1769476

commit v2 on v1

--- a/solution.py
+++ b/solution.py
@@ -7,6 +7,7 @@
 
 RB_SC = 4
 BITS = 8
+PILOTS = 2
 EDGE = 8
 PANEL = "panel"
 SUB = "sc"
@@ -28,36 +29,88 @@
     return jnp.where(odd, turned, w).astype(jnp.bfloat16)
 
 
-def partial_kernel(lookup_ref, rows_ref, wave_ref, out_ref, matrix_ref):
-    @pl.when(pl.program_id(0) == 0)
-    def _():
-        matrix_ref[...] = lookup_matrix(lookup_ref[...], rows_ref[...])
-
-    g, t, s, k = wave_ref.shape
-    out_ref[...] = (
-        jnp.dot(wave_ref[...].reshape(g * t * s, k), matrix_ref[...], preferred_element_type=jnp.float32)
-        .astype(jnp.bfloat16)
-        .reshape(out_ref.shape)
-    )
-
-
-def beam_partials(wave, lookup, rows, step):
+def matrix_kernel_body(wave_ref, out_ref, blocks_ref, sems, matrix, parity):
+    count, syms, subs, c = out_ref.shape
+    k = wave_ref.shape[3]
+
+    def fetch(i):
+        return pltpu.make_async_copy(wave_ref.at[2 * i + parity], blocks_ref.at[i], sems.at[i])
+
+    for i in range(count):
+        fetch(i).start()
+    weights = matrix()
+    for i in range(count):
+        fetch(i).wait()
+        out_ref[i] = (
+            jnp.dot(blocks_ref[i].reshape(syms * subs, k), weights, preferred_element_type=jnp.float32)
+            .astype(jnp.bfloat16)
+            .reshape(syms, subs, c)
+        )
+
+
+def given_kernel(lookup_ref, rows_ref, wave_ref, out_ref, matrix_ref, blocks_ref, lookup_buf, rows_buf, sems):
+    count = out_ref.shape[0]
+    copies = [
+        pltpu.make_async_copy(lookup_ref, lookup_buf, sems.at[count]),
+        pltpu.make_async_copy(rows_ref, rows_buf, sems.at[count + 1]),
+    ]
+    for copy in copies:
+        copy.start()
+
+    def matrix():
+        for copy in copies:
+            copy.wait()
+        matrix_ref[...] = lookup_matrix(lookup_buf[...], rows_buf[...])
+        return matrix_ref[...]
+
+    parity = 1 - lax.axis_index(PANEL) % 2
+    matrix_kernel_body(wave_ref, out_ref, blocks_ref, sems, matrix, parity)
+
+
+def kept_kernel(matrix_ref, wave_ref, out_ref, blocks_ref, sems):
+    parity = lax.axis_index(PANEL) % 2
+    matrix_kernel_body(wave_ref, out_ref, blocks_ref, sems, lambda: matrix_ref[...], parity)
+
+
+def beam_partials(wave, lookup, rows):
     groups, syms, subs, k = wave.shape
-    c = rows.shape[1]
-    return pl.pallas_call(
-        partial_kernel,
-        grid=(groups // step,),
-        in_specs=[
-            pl.BlockSpec((1, lookup.shape[0]), lambda i: (0, 0)),
-            pl.BlockSpec(rows.shape, lambda i: (0, 0)),
-            pl.BlockSpec((step, syms, subs, k), lambda i: (i, 0, 0, 0)),
+    n, c = rows.shape
+    half = groups // 2
+    lookup, rows, wave = (
+        pltpu.with_memory_space_constraint(array, pltpu.HBM) for array in (lookup.reshape(1, -1), rows, wave)
+    )
+    hbm = pl.BlockSpec(memory_space=pltpu.HBM)
+    vmem = pl.BlockSpec(memory_space=pltpu.VMEM)
+    params = pltpu.CompilerParams(vmem_limit_bytes=8 * 2**20)
+    out = jax.ShapeDtypeStruct((half, syms, subs, c), jnp.bfloat16)
+    blocks = pltpu.VMEM((half, syms, subs, k), jnp.bfloat16)
+    given, matrix = pl.pallas_call(
+        given_kernel,
+        in_specs=[hbm] * 3,
+        out_specs=[vmem] * 2,
+        out_shape=[out, jax.ShapeDtypeStruct((k, c), jnp.bfloat16)],
+        scratch_shapes=[
+            blocks,
+            pltpu.VMEM((1, n), jnp.int32),
+            pltpu.VMEM((n, c), jnp.bfloat16),
+            pltpu.SemaphoreType.DMA((half + 2,)),
         ],
-        out_specs=pl.BlockSpec((step, syms, subs, c), lambda i: (i, 0, 0, 0)),
-        out_shape=jax.ShapeDtypeStruct((groups, syms, subs, c), jnp.bfloat16),
-        scratch_shapes=[pltpu.VMEM((k, c), jnp.bfloat16)],
-        compiler_params=pltpu.CompilerParams(vmem_limit_bytes=16 * 2**20),
-        name="partials",
-    )(lookup.reshape(1, -1), rows, wave)
+        compiler_params=params,
+        name="given",
+    )(lookup, rows, wave)
+    kept = pl.pallas_call(
+        kept_kernel,
+        in_specs=[vmem, hbm],
+        out_specs=vmem,
+        out_shape=out,
+        scratch_shapes=[blocks, pltpu.SemaphoreType.DMA((half,))],
+        compiler_params=params,
+        cost_estimate=pl.CostEstimate(
+            flops=2 * half * syms * subs * k * c, bytes_accessed=2 * half * syms * subs * k, transcendentals=0
+        ),
+        name="kept",
+    )(matrix, wave)
+    return given, kept
 
 
 def as_column(row, count):
@@ -82,20 +135,21 @@
 
 def sum_kernel(syms_ref, pilot_ref, parts_ref, own_ref, head_ref, tail_ref):
     panels, syms, subs, c = parts_ref.shape
-    re, im = signed_pilots(pilot_ref, c)
     for t in range(syms):
         total = parts_ref[0, t].astype(jnp.float32)
         for p in range(1, panels):
             total = total + parts_ref[p, t].astype(jnp.float32)
         beams = total.astype(jnp.bfloat16)
-        is_pilot = jnp.where((syms_ref[0] == t) | (syms_ref[1] == t), 1.0, 0.0)
-        estimate = (estimate_of(beams.astype(jnp.float32), re, im) * is_pilot).astype(jnp.bfloat16)
-        own_ref[t, :, :c] = beams
-        own_ref[t, :, c:] = estimate
-        head_ref[t, :, :c] = beams[:EDGE]
-        head_ref[t, :, c:] = estimate[:EDGE]
-        tail_ref[t, :, :c] = beams[subs - EDGE :]
-        tail_ref[t, :, c:] = estimate[subs - EDGE :]
+        own_ref[t] = beams
+        head_ref[t] = beams[:EDGE]
+        tail_ref[t] = beams[subs - EDGE :]
+    re, im = signed_pilots(pilot_ref, c)
+    for i in range(PILOTS):
+        at_pilot = own_ref[syms_ref[i]].astype(jnp.float32)
+        estimate = estimate_of(at_pilot, re, im).astype(jnp.bfloat16)
+        own_ref[syms + i] = estimate
+        head_ref[syms + i] = estimate[:EDGE]
+        tail_ref[syms + i] = estimate[subs - EDGE :]
 
 
 def sum_beams(parts, pilot_syms, pilot_values):
@@ -106,11 +160,11 @@
         in_specs=[pl.BlockSpec(memory_space=pltpu.SMEM), vmem, vmem],
         out_specs=[vmem] * 3,
         out_shape=[
-            jax.ShapeDtypeStruct((syms, subs, 2 * c), jnp.bfloat16),
-            jax.ShapeDtypeStruct((syms, EDGE, 2 * c), jnp.bfloat16),
-            jax.ShapeDtypeStruct((syms, EDGE, 2 * c), jnp.bfloat16),
+            jax.ShapeDtypeStruct((syms + PILOTS, subs, c), jnp.bfloat16),
+            jax.ShapeDtypeStruct((syms + PILOTS, EDGE, c), jnp.bfloat16),
+            jax.ShapeDtypeStruct((syms + PILOTS, EDGE, c), jnp.bfloat16),
         ],
-        compiler_params=pltpu.CompilerParams(vmem_limit_bytes=16 * 2**20),
+        compiler_params=pltpu.CompilerParams(vmem_limit_bytes=8 * 2**20),
         name="sum_beams",
     )(pilot_syms, pilot_values, parts)
 
@@ -119,11 +173,11 @@
     ends_ref, syms_ref, order_ref, own_ref, left_ref, right_ref, first_ref, rest_ref, bias_ref,
     in_ref, in_bias_ref, out_w_ref, llr_ref, wide_ref, even_ref, odd_ref,
 ):
-    syms, subs, feats = own_ref.shape
+    syms, subs, c = own_ref.shape
+    syms, feats = syms - PILOTS, 2 * c
     layers = rest_ref.shape[0] + 1
     width = subs + 2 * EDGE
     rows = syms * width
-    c = bias_ref.shape[1]
     skip = EDGE - layers
 
     def put(ref, whole, ch):
@@ -135,14 +189,21 @@
         ref[0:width] = jnp.zeros((width, ref.shape[1]), jnp.bfloat16)
         ref[width + rows :] = jnp.zeros((width, ref.shape[1]), jnp.bfloat16)
 
-    field = jnp.concatenate(
+    pieces = jnp.concatenate(
         [
             left_ref[...].astype(jnp.float32),
             own_ref[...].astype(jnp.float32),
             right_ref[...].astype(jnp.float32),
         ],
         axis=1,
-    ).reshape(rows, feats)
+    )
+    estimates = []
+    for t in range(syms):
+        estimate = jnp.zeros((width, c), jnp.float32)
+        for i in range(PILOTS):
+            estimate = jnp.where(syms_ref[i] == t, pieces[syms + i], estimate)
+        estimates.append(estimate)
+    field = jnp.concatenate([pieces[:syms], jnp.stack(estimates, 0)], axis=2).reshape(rows, feats)
     field = pltpu.roll(field, rows - skip, 0)
     put(wide_ref, field, feats)
 
@@ -178,9 +239,9 @@
 
 
 def receive(ends, pilot_syms, mod_order, own, left, right, first, rest, bias, d_in, d_bias, d_out):
-    syms, subs, feats = own.shape
+    syms, subs, c = own.shape
+    syms, feats = syms - PILOTS, 2 * c
     layers = bias.shape[0]
-    c = bias.shape[1]
     width = subs + 2 * EDGE
     smem = pl.BlockSpec(memory_space=pltpu.SMEM)
     vmem = pl.BlockSpec(memory_space=pltpu.VMEM)
@@ -218,8 +279,12 @@
     demap_bias,
     demap_out,
 ):
-    parts = beam_partials(captured_waveform, element_lookup, combiner, 2)
-    parts = lax.all_to_all(parts, PANEL, 0, 0, tiled=True)
+    given, kept = beam_partials(captured_waveform, element_lookup, combiner)
+    panels = lax.axis_size(PANEL)
+    got = lax.ppermute(given, PANEL, [(p, p ^ 1) for p in range(panels)])
+    pairs = (kept.astype(jnp.float32) + got.astype(jnp.float32)).astype(jnp.bfloat16)
+    same_core = [list(range(core, panels, 2)) for core in range(2)]
+    parts = lax.all_to_all(pairs, PANEL, 0, 0, axis_index_groups=same_core, tiled=True)
     own, head, tail = sum_beams(parts, pilot_syms, pilot_values)
     both = (PANEL, SUB)
     count = lax.axis_size(both)

time: 66.2 us -> 55 us (0.83)
  waiting for transfers between devices: 26 us -> 14.5 us
  local copies, waits for them, and re-layouts: 5.81 us -> 0.05 us
  Pallas kernels: 10.5 us -> 14.3 us
  starting transfers between devices: 22.9 us -> 24.5 us
  other arithmetic: 0.08 us -> 1.25 us
    all_to_all x1, waiting for transfers between devices: 24.9 us -> 13.5 us  [per_device(): lax.all_to_all(pairs, PANEL, 0, 0, axis_index_groups=same_core, tiled=True)]
    ppermute x0 -> x1, starting transfers between devices: none -> 8.79 us  [per_device(): got = lax.ppermute(given, PANEL, [(p, p ^ 1) for p in range(panels)])]
    all_to_all x1, starting transfers between devices: 10.5 us -> 3.7 us  [per_device(): lax.all_to_all(pairs, PANEL, 0, 0, axis_index_groups=same_core, tiled=True)]
    unnamed x26 -> x18, local copies, waits for them, and re-layouts: 5.81 us -> 0.05 us
    pallas_call x1 -> x2, Pallas kernels: 2.72 us -> 6.58 us  [the longest x1 3.43 us: beam_partials(): pl.pallas_call(given_kernel, in_specs=[hbm] * 3, out_specs=[vmem] * 2, ou...]
    convert_element_type x0 -> x1, other arithmetic: none -> 1.17 us  [per_device(): (kept.astype(jnp.float32) + got.astype(jnp.float32)).astype(jnp.bfloat16)]
  transfers between devices with their start and end apart: 3 -> 4, of which waited for: 2 -> 2; matrix products, arithmetic and copies ran while one was open for 0% -> 0% of each run, Pallas kernels for 0% -> 6%
where the time goes in v2:
time: 55 us; the launch traced here: 54.7 us
  starting transfers between devices  24.5 us (45%)
  waiting for transfers between devices  14.5 us (26%)
  Pallas kernels  14.3 us (26%)
  other arithmetic  1.25 us (2%)
    all_to_all x1, waiting for transfers between devices, per_device(): lax.all_to_all(pairs, PANEL, 0, 0, axis_index_groups=same_core, tiled=True)  13.5 us
    ppermute x1, starting transfers between devices, per_device(): right = lax.ppermute(head, both, [(i + 1, i) for i in range(count - 1)])  10.2 us
    ppermute x1, starting transfers between devices, per_device(): got = lax.ppermute(given, PANEL, [(p, p ^ 1) for p in range(panels)])  8.79 us
    pallas_call x1, Pallas kernels, receive(): pl.pallas_call(receiver_kernel, in_specs=[smem] * 3 + [vmem] * 9, out_spe...  6.89 us
    all_to_all x1, starting transfers between devices, per_device(): lax.all_to_all(pairs, PANEL, 0, 0, axis_index_groups=same_core, tiled=True)  3.7 us
    pallas_call x1, Pallas kernels, beam_partials(): pl.pallas_call(given_kernel, in_specs=[hbm] * 3, out_specs=[vmem] * 2, ou...  3.43 us
    pallas_call x1, Pallas kernels, beam_partials(): pl.pallas_call(kept_kernel, in_specs=[vmem, hbm], out_specs=vmem, out_sha...  3.15 us
    ppermute x1, starting transfers between devices, per_device(): left = lax.ppermute(tail, both, [(i, i + 1) for i in range(count - 1)])  1.91 us
  transfers between devices with their start and end apart: 4, of which 2 were waited for; matrix products, arithmetic and copies ran while one was open for 0% of the time, Pallas kernels for 6%

profile of v2, /device:TPU:1, one launch (start us, length us, event | category | flops | bytes accessed | tf_op | source)
XLA Modules:
  0.0 54.7 jit_solution(8377220657318979670)
XLA Ops:
  0.0 3.4 %given.1 = (bf16[8,14,32,128]{3,2,1,0:T(8,128)(2,1)S(1)}, bf16[256,128]{1,0:T(8,128)(2,1)S(1)}) custom-call(s32[1,128]{1,0:T(1,128)} %bitcast.9, bf16[128,128]{1,0:T(8,128)(2,1)} %rows_ref.1, bf16[16,14,32,256]{3,2,1,0:T(8,128)(2,1)} %wave_ref.3), custom_call_target="tpu_custom_call" | custom-call | tf_op jit(solution)/shard_map/given/pallas_call | solution.py:87
  3.4 8.8 %collective-permute-start = (bf16[8,14,32,128]{3,2,1,0:T(8,128)(2,1)S(1)}, bf16[8,14,32,128]{3,2,1,0:T(8,128)(2,1)S(1)}, u32[]{:S(2)}, u32[]{:S(2)}) collective-permute-start(bf16[8,14,32,128]{3,2,1,0:T(8,128)(2,1)S(1)} %get-tuple-element.11), channel_id=1, source_target_pairs={{0,32},{32,0},{64,96},{96,64},{128,160},{160,128},{192,224},{224,1... | collective-permute-start | bytes 2752520 | tf_op jit(solution)/shard_map/ppermute | solution.py:284
  12.2 3.2 %kept.1 = bf16[8,14,32,128]{3,2,1,0:T(8,128)(2,1)S(1)} custom-call(bf16[256,128]{1,0:T(8,128)(2,1)S(1)} %get-tuple-element.10.matrix_ref, bf16[16,14,32,256]{3,2,1,0:T(8,128)(2,1)} %wave_ref.3), custom_call_target="tpu_custom_call" | custom-call | flops 234881024 | bytes 1835008 | tf_op jit(solution)/shard_map/kept/pallas_call | solution.py:101
  15.4 0.0 copy-start.5
  15.4 0.0 copy-start.7
  15.4 0.0 collective-permute-done
  15.4 1.2 %add_convert_fusion = bf16[8,14,32,128]{3,2,1,0:T(8,128)(2,1)} fusion(bf16[8,14,32,128]{3,2,1,0:T(8,128)(2,1)S(1)} %collective-permute-done, bf16[8,14,32,128]{3,2,1,0:T(8,128)(2,1)S(1)} %kept.1), kind=kLoop, calls=%fused_computation | loop fusion | flops 1835008 | bytes 2752512 | tf_op jit(solution)/shard_map/convert_element_type | solution.py:285
  16.6 0.0 copy-start
  16.6 0.0 copy-start.1
  16.6 0.0 copy-start.2
  16.6 0.0 copy-start.3
  16.6 0.0 copy-start.4
  16.6 0.0 copy-start.6
  16.6 0.0 copy-start.8
  16.7 3.7 %all-to-all-start = ((bf16[8,14,32,128]{3,2,1,0:T(8,128)(2,1)}), bf16[8,14,32,128]{3,2,1,0:T(8,128)(2,1)S(1)}, u32[]{:S(2)}, u32[]{:S(2)}) async-start(bf16[8,14,32,128]{3,2,1,0:T(8,128)(2,1)} %add_convert_fusion), calls=%async_computation | async-start | bytes 1835008 | tf_op jit(solution)/shard_map/all_to_all | solution.py:287
  20.4 13.5 %all-to-all-done.parts_ref = bf16[8,14,32,128]{3,2,1,0:T(8,128)(2,1)S(1)} async-done(((bf16[8,14,32,128]{3,2,1,0:T(8,128)(2,1)}), bf16[8,14,32,128]{3,2,1,0:T(8,128)(2,1)S(1)}, u32[]{:S(2)}, u32[]{:S(2)}) %all-to-all-start) | async-done | bytes 917536 | tf_op jit(solution)/shard_map/all_to_all | solution.py:287
  33.9 0.0 copy-done.5
  33.9 0.0 copy-done.7
  33.9 0.8 %sum_beams.1 = (bf16[16,32,128]{2,1,0:T(8,128)(2,1)S(1)}, bf16[16,8,128]{2,1,0:T(8,128)(2,1)S(1)}, bf16[16,8,128]{2,1,0:T(8,128)(2,1)S(1)}) custom-call(s32[2]{0:T(128)S(1)} %copy-done.5, f32[2,32]{1,0:T(2,128)S(1)} %copy-done.7, bf16[8,14,32,128]{3,2,1,0:T(8,128)(2,1)S(1)} %all-to-all-done.parts_ref), custom_call_target="tpu_custom_call" | custom-call | tf_op jit(solution)/shard_map/sum_beams/pallas_call | solution.py:158
  34.7 1.9 %collective-permute-start.1 = (bf16[16,8,128]{2,1,0:T(8,128)(2,1)S(1)}, bf16[16,8,128]{2,1,0:T(8,128)(2,1)S(1)}, u32[]{:S(2)}, u32[]{:S(2)}) collective-permute-start(bf16[16,8,128]{2,1,0:T(8,128)(2,1)S(1)} %get-tuple-element.13), channel_id=1, source_target_pairs={{0,1},{1,2},{2,3},{3,4},{4,5},{5,6},{6,7},{7,8},{8,9},{9,10},{10,1... | collective-permute-start | bytes 98312 | tf_op jit(solution)/shard_map/ppermute | solution.py:291
  36.6 10.2 %collective-permute-start.2 = (bf16[16,8,128]{2,1,0:T(8,128)(2,1)S(1)}, bf16[16,8,128]{2,1,0:T(8,128)(2,1)S(1)}, u32[]{:S(2)}, u32[]{:S(2)}) collective-permute-start(bf16[16,8,128]{2,1,0:T(8,128)(2,1)S(1)} %get-tuple-element.14), channel_id=1, source_target_pairs={{1,0},{2,1},{3,2},{4,3},{5,4},{6,5},{7,6},{8,7},{9,8},{10,9},{11,1... | collective-permute-start | bytes 98312 | tf_op jit(solution)/shard_map/ppermute | solution.py:292
  46.8 0.1 add_convert_fusion.1.ends_ref
  46.9 0.0 collective-permute-done.1.left_ref
  46.9 0.9 %collective-permute-done.2.right_ref = bf16[16,8,128]{2,1,0:T(8,128)(2,1)S(1)} collective-permute-done((bf16[16,8,128]{2,1,0:T(8,128)(2,1)S(1)}, bf16[16,8,128]{2,1,0:T(8,128)(2,1)S(1)}, u32[]{:S(2)}, u32[]{:S(2)}) %collective-permute-start.2) | collective-permute-done | bytes 32800 | tf_op jit(solution)/shard_map/ppermute | solution.py:292
  47.8 0.0 copy-done
  47.8 0.0 copy-done.1
  47.8 0.0 copy-done.2
  47.8 0.0 copy-done.3
  47.8 0.0 copy-done.4
  47.8 0.0 copy-done.6
  47.8 0.0 copy-done.8
  47.9 6.9 %receiver.1 = f32[14,32,128]{2,1,0:T(8,128)} custom-call(s32[2]{0:T(128)S(1)} %add_convert_fusion.1.ends_ref, s32[2]{0:T(128)S(1)} %copy-done.5, s32[8]{0:T(128)S(1)} %copy-done.8, bf16[16,32,128]{2,1,0:T(8,128)(2,1)S(1)} %get-tuple-element.12.own_ref, bf16[16,8,128]{2,1,0:T(8,128)(2,1)S(1)} %collective-permute-done.1.left_ref, ...), custom_call_target="tpu_custom_call" | custom-call | tf_op jit(solution)/shard_map/receiver/pallas_call | solution.py:249
Async XLA Ops:
  3.4 12.0 %collective-permute-start = (bf16[8,14,32,128]{3,2,1,0:T(8,128)(2,1)S(1)}, bf16[8,14,32,128]{3,2,1,0:T(8,128)(2,1)S(1)}, u32[]{:S(2)}, u32[]{:S(2)}) collective-permute-start(bf16[8,14,32,128]{3,2,1,0:T(8,128)(2,1)S(1)} %get-tuple-element.11), channel_id=1, source_target_pairs={{0,32},{32,0},{64,96},{96,64},{128,160},{160,128},{192,224},{224,1... | collective-permute-start | bytes 2752520 | tf_op jit(solution)/shard_map/ppermute | solution.py:284
  15.4 18.5 %copy-start.5 = (s32[2]{0:T(128)S(1)}, s32[2]{0:T(128)}, u32[]{:S(2)}) copy-start(s32[2]{0:T(128)} %syms_ref.3) | copy-start | bytes 28
  15.4 18.5 %copy-start.7 = (f32[2,32]{1,0:T(2,128)S(1)}, f32[2,32]{1,0:T(2,128)}, u32[]{:S(2)}) copy-start(f32[2,32]{1,0:T(2,128)} %pilot_ref.1) | copy-start | bytes 772
  16.6 31.2 %copy-start = (bf16[5,3,3,128,128]{4,3,2,1,0:T(8,128)(2,1)S(1)}, bf16[5,3,3,128,128]{4,3,2,1,0:T(8,128)(2,1)}, u32[]{:S(2)}) copy-start(bf16[5,3,3,128,128]{4,3,2,1,0:T(8,128)(2,1)} %param.19) | copy-start | bytes 4423684
  16.6 31.2 %copy-start.1 = (bf16[3,3,256,128]{3,2,1,0:T(8,128)(2,1)S(1)}, bf16[3,3,256,128]{3,2,1,0:T(8,128)(2,1)}, u32[]{:S(2)}) copy-start(bf16[3,3,256,128]{3,2,1,0:T(8,128)(2,1)} %param.18) | copy-start | bytes 1769476
  16.6 31.2 %copy-start.2 = (bf16[128,256]{1,0:T(8,128)(2,1)S(1)}, bf16[128,256]{1,0:T(8,128)(2,1)}, u32[]{:S(2)}) copy-start(bf16[128,256]{1,0:T(8,128)(2,1)} %in_ref.1) | copy-start | bytes 196612
  16.6 31.2 %copy-start.3 = (bf16[256,128]{1,0:T(8,128)(2,1)S(1)}, bf16[256,128]{1,0:T(8,128)(2,1)}, u32[]{:S(2)}) copy-start(bf16[256,128]{1,0:T(8,128)(2,1)} %out_w_ref.1) | copy-start | bytes 196612
  16.6 31.2 %copy-start.4 = (f32[6,128]{1,0:T(8,128)S(1)}, f32[6,128]{1,0:T(8,128)}, u32[]{:S(2)}) copy-start(f32[6,128]{1,0:T(8,128)} %bias_ref.1) | copy-start | bytes 9220
  16.6 31.2 %copy-start.6 = (f32[256]{0:T(256)S(1)}, f32[256]{0:T(256)}, u32[]{:S(2)}) copy-start(f32[256]{0:T(256)} %param.22) | copy-start | bytes 3076
  16.6 31.2 %copy-start.8 = (s32[8]{0:T(128)S(1)}, s32[8]{0:T(128)}, u32[]{:S(2)}) copy-start(s32[8]{0:T(128)} %order_ref.1) | copy-start | bytes 100
  16.7 17.3 %all-to-all-start = ((bf16[8,14,32,128]{3,2,1,0:T(8,128)(2,1)}), bf16[8,14,32,128]{3,2,1,0:T(8,128)(2,1)S(1)}, u32[]{:S(2)}, u32[]{:S(2)}) async-start(bf16[8,14,32,128]{3,2,1,0:T(8,128)(2,1)} %add_convert_fusion), calls=%async_computation | async-start | bytes 1835008 | tf_op jit(solution)/shard_map/all_to_all | solution.py:287
  34.7 12.2 %collective-permute-start.1 = (bf16[16,8,128]{2,1,0:T(8,128)(2,1)S(1)}, bf16[16,8,128]{2,1,0:T(8,128)(2,1)S(1)}, u32[]{:S(2)}, u32[]{:S(2)}) collective-permute-start(bf16[16,8,128]{2,1,0:T(8,128)(2,1)S(1)} %get-tuple-element.13), channel_id=1, source_target_pairs={{0,1},{1,2},{2,3},{3,4},{4,5},{5,6},{6,7},{7,8},{8,9},{9,10},{10,1... | collective-permute-start | bytes 98312 | tf_op jit(solution)/shard_map/ppermute | solution.py:291
  36.6 11.2 %collective-permute-start.2 = (bf16[16,8,128]{2,1,0:T(8,128)(2,1)S(1)}, bf16[16,8,128]{2,1,0:T(8,128)(2,1)S(1)}, u32[]{:S(2)}, u32[]{:S(2)}) collective-permute-start(bf16[16,8,128]{2,1,0:T(8,128)(2,1)S(1)} %get-tuple-element.14), channel_id=1, source_target_pairs={{1,0},{2,1},{3,2},{4,3},{5,4},{6,5},{7,6},{8,7},{9,8},{10,9},{11,1... | collective-permute-start | bytes 98312 | tf_op jit(solution)/shard_map/ppermute | solution.py:292

commit v3 on v2

v3 whole, which is shorter than its diff:
```python
import jax
import jax.numpy as jnp
from jax import lax
from jax.experimental import pallas as pl
from jax.experimental.pallas import tpu as pltpu
from jax.sharding import PartitionSpec as P

RB_SC = 4
BITS = 8
PILOTS = 2
EDGE = 8
PANEL = "panel"
SUB = "sc"


def lookup_matrix(lookup, rows):
    n, c = rows.shape
    member = lax.broadcasted_iota(jnp.int32, (n, n), 0) == lookup % n
    picked = lax.dot_general(
        member.astype(jnp.bfloat16), rows, (((0,), (0,)), ((), ())), preferred_element_type=jnp.float32
    ).astype(jnp.bfloat16)
    doubled = (
        lax.broadcasted_iota(jnp.int32, (2 * n, n), 0) // 2 == lax.broadcasted_iota(jnp.int32, (2 * n, n), 1)
    )
    w = jnp.dot(doubled.astype(jnp.bfloat16), picked, preferred_element_type=jnp.float32)
    lane = lax.broadcasted_iota(jnp.int32, w.shape, 1)
    turned = pltpu.roll(w, c // 2, 1) * jnp.where(lane < c // 2, -1.0, 1.0)
    odd = lax.broadcasted_iota(jnp.int32, w.shape, 0) % 2 == 1
    return jnp.where(odd, turned, w).astype(jnp.bfloat16)


def matrix_kernel_body(wave_ref, out_ref, blocks_ref, sems, matrix, parity):
    count, syms, subs, c = out_ref.shape
    k = wave_ref.shape[3]

    def fetch(i):
        return pltpu.make_async_copy(wave_ref.at[2 * i + parity], blocks_ref.at[i], sems.at[i])

    for i in range(count):
        fetch(i).start()
    weights = matrix()
    for first, last in ((0, count // 4), (count // 4, count)):
        for i in range(first, last):
            fetch(i).wait()
        lines = blocks_ref[first:last].reshape((last - first) * syms * subs, k)
        out_ref[first:last] = (
            jnp.dot(lines, weights, preferred_element_type=jnp.float32)
            .astype(jnp.bfloat16)
            .reshape(last - first, syms, subs, c)
        )


def given_kernel(lookup_ref, rows_ref, wave_ref, out_ref, matrix_ref, blocks_ref, lookup_buf, rows_buf, sems):
    count = out_ref.shape[0]
    copies = [
        pltpu.make_async_copy(lookup_ref, lookup_buf, sems.at[count]),
        pltpu.make_async_copy(rows_ref, rows_buf, sems.at[count + 1]),
    ]
    for copy in copies:
        copy.start()

    def matrix():
        for copy in copies:
            copy.wait()
        matrix_ref[...] = lookup_matrix(lookup_buf[...], rows_buf[...])
        return matrix_ref[...]

    parity = 1 - lax.axis_index(PANEL) % 2
    matrix_kernel_body(wave_ref, out_ref, blocks_ref, sems, matrix, parity)


def kept_kernel(matrix_ref, wave_ref, out_ref, blocks_ref, sems):
    parity = lax.axis_index(PANEL) % 2
    matrix_kernel_body(wave_ref, out_ref, blocks_ref, sems, lambda: matrix_ref[...], parity)


def beam_partials(wave, lookup, rows):
    groups, syms, subs, k = wave.shape
    n, c = rows.shape
    half = groups // 2
    lookup, rows, wave = (
        pltpu.with_memory_space_constraint(array, pltpu.HBM) for array in (lookup.reshape(1, -1), rows, wave)
    )
    hbm = pl.BlockSpec(memory_space=pltpu.HBM)
    vmem = pl.BlockSpec(memory_space=pltpu.VMEM)
    params = pltpu.CompilerParams(vmem_limit_bytes=8 * 2**20)
    out = jax.ShapeDtypeStruct((half, syms, subs, c), jnp.bfloat16)
    blocks = pltpu.VMEM((half, syms, subs, k), jnp.bfloat16)
    given, matrix = pl.pallas_call(
        given_kernel,
        in_specs=[hbm] * 3,
        out_specs=[vmem] * 2,
        out_shape=[out, jax.ShapeDtypeStruct((k, c), jnp.bfloat16)],
        scratch_shapes=[
            blocks,
            pltpu.VMEM((1, n), jnp.int32),
            pltpu.VMEM((n, c), jnp.bfloat16),
            pltpu.SemaphoreType.DMA((half + 2,)),
        ],
        compiler_params=params,
        name="given",
    )(lookup, rows, wave)
    kept = pl.pallas_call(
        kept_kernel,
        in_specs=[vmem, hbm],
        out_specs=vmem,
        out_shape=out,
        scratch_shapes=[blocks, pltpu.SemaphoreType.DMA((half,))],
        compiler_params=params,
        cost_estimate=pl.CostEstimate(
            flops=2 * half * syms * subs * k * c, bytes_accessed=2 * half * syms * subs * k, transcendentals=0
        ),
        name="kept",
    )(matrix, wave)
    return given, kept


def as_column(row, count):
    diagonal = lax.broadcasted_iota(jnp.int32, (count, count), 0) == lax.broadcasted_iota(
        jnp.int32, (count, count), 1
    )
    return jnp.sum(jnp.where(diagonal, jnp.broadcast_to(row, (count, count)), 0.0), axis=1, keepdims=True)


def estimate_of(beams, pilot_re, pilot_im):
    c = beams.shape[-1]
    return beams * pilot_re + pltpu.roll(beams, c // 2, beams.ndim - 1) * pilot_im


def signed_pilots(pilot_ref, c):
    s = pilot_ref.shape[1]
    re = jnp.broadcast_to(as_column(pilot_ref[0:1, :], s), (s, c))
    im = jnp.broadcast_to(as_column(pilot_ref[1:2, :], s), (s, c))
    lane = lax.broadcasted_iota(jnp.int32, (s, c), 1)
    return re, jnp.where(lane < c // 2, im, -im)


def position():
    blocks = lax.axis_size(SUB)
    return lax.axis_index(PANEL) * blocks + lax.axis_index(SUB), lax.axis_size(PANEL) * blocks


def first_half(rows, low, high):
    return jnp.where(lax.broadcasted_iota(jnp.int32, rows, len(rows) - 2) < EDGE // 2, low, high)


def sum_kernel(syms_ref, pilot_ref, parts_ref, own_ref, first_ref, second_ref, beams_ref):
    panels, syms, subs, c = parts_ref.shape
    for t in range(syms):
        total = parts_ref[0, t].astype(jnp.float32)
        for p in range(1, panels):
            total = total + parts_ref[p, t].astype(jnp.float32)
        beams_ref[t] = total.astype(jnp.bfloat16).astype(jnp.float32)
    re, im = signed_pilots(pilot_ref, c)
    for i in range(PILOTS):
        beams_ref[syms + i] = estimate_of(beams_ref[syms_ref[i]], re, im)
    half = EDGE // 2
    even = beams_ref[:, pl.ds(0, subs // 2, 2), :]
    odd = beams_ref[:, pl.ds(1, subs // 2, 2), :]
    own_ref[:, :, :c] = even.astype(jnp.bfloat16)
    own_ref[:, :, c:] = odd.astype(jnp.bfloat16)
    rows = (syms + PILOTS, EDGE, c)
    head = first_half(rows, even[:, :EDGE], pltpu.roll(odd[:, :EDGE], half, 1))
    tail = first_half(rows, pltpu.roll(even[:, subs // 2 - EDGE :], half, 1), odd[:, subs // 2 - EDGE :])
    to_right = position()[0] % 2 == 0
    first_ref[...] = jnp.where(to_right, tail, head).astype(jnp.bfloat16)
    second_ref[...] = jnp.where(to_right, head, tail).astype(jnp.bfloat16)


def sum_beams(parts, pilot_syms, pilot_values):
    _, syms, subs, c = parts.shape
    vmem = pl.BlockSpec(memory_space=pltpu.VMEM)
    edge = jax.ShapeDtypeStruct((syms + PILOTS, EDGE, c), jnp.bfloat16)
    return pl.pallas_call(
        sum_kernel,
        in_specs=[pl.BlockSpec(memory_space=pltpu.SMEM), vmem, vmem],
        out_specs=[vmem] * 3,
        out_shape=[jax.ShapeDtypeStruct((syms + PILOTS, subs // 2, 2 * c), jnp.bfloat16), edge, edge],
        scratch_shapes=[pltpu.VMEM((syms + PILOTS, subs, c), jnp.float32)],
        compiler_params=pltpu.CompilerParams(vmem_limit_bytes=8 * 2**20),
        name="sum_beams",
    )(pilot_syms, pilot_values, parts)


def pilot_rows(syms_ref, rows, syms):
    spread = []
    for t in range(syms):
        row = jnp.zeros(rows.shape[1:], rows.dtype)
        for i in range(PILOTS):
            row = jnp.where(syms_ref[i] == t, rows[i], row)
        spread.append(row)
    return jnp.stack(spread, 0)


def with_estimates(syms_ref, pairs, syms):
    c = pairs.shape[2] // 2
    beams, estimates = pairs[:syms], pilot_rows(syms_ref, pairs[syms:], syms)
    return jnp.concatenate([beams[..., :c], estimates[..., :c], beams[..., c:], estimates[..., c:]], axis=2)


def layer_sums(taps, kernel, bias):
    depth = kernel.shape[0] // 3
    zeros = jnp.zeros((depth // 3, kernel.shape[1]), kernel.dtype)
    total = jnp.concatenate([bias, bias], axis=1)
    for dt in range(3):
        part = kernel[dt * depth : (dt + 1) * depth]
        wide = jnp.concatenate(
            [jnp.concatenate([part, zeros], axis=0), jnp.concatenate([zeros, part], axis=0)], axis=1
        )
        total = total + jnp.dot(taps(dt), wide, preferred_element_type=jnp.float32)
    return jnp.maximum(total, 0.0)


def demapped(pairs, in_ref, in_bias_ref, out_w_ref):
    rows, c = pairs.shape[0], pairs.shape[1] // 2
    field = jnp.concatenate([pairs[:, :c], pairs[:, c:]], axis=0)
    hidden = jnp.dot(field, in_ref[...], preferred_element_type=jnp.float32)
    hidden = jnp.maximum(hidden + in_bias_ref[...], 0.0).astype(jnp.bfloat16)
    llr = jnp.dot(hidden, out_w_ref[...], preferred_element_type=jnp.float32)
    return llr[:rows], llr[rows:]


def bit_limits(order_ref, pairs, bits):
    row = lax.broadcasted_iota(jnp.int32, (len(pairs), bits), 0)
    limit = jnp.zeros((len(pairs), bits), jnp.int32)
    for block in sorted({2 * pair // RB_SC for pair in pairs}):
        at = [r for r, pair in enumerate(pairs) if 2 * pair // RB_SC == block]
        limit = jnp.where((row >= at[0]) & (row <= at[-1]), 2 * order_ref[block], limit)
    return limit


def store_llr(ref, llrs, limit, syms_ref):
    rows = limit.shape[0]
    bit = lax.broadcasted_iota(jnp.int32, limit.shape, 1) % BITS
    for t in range(ref.shape[0]):
        data = jnp.where((syms_ref[0] == t) | (syms_ref[1] == t), 0, 1)
        keep = bit < limit * data
        for side, llr in enumerate(llrs):
            ref[t, pl.ds(side, rows, 2), :] = jnp.where(keep, llr[t * rows : (t + 1) * rows], 0.0)


def interior_kernel(
    syms_ref, order_ref, own_ref, first_ref, rest_ref, bias_ref, in_ref, in_bias_ref, out_w_ref,
    llr_ref, patch_ref, wide_ref, even_ref, odd_ref,
):
    syms, pairs, c2 = own_ref.shape
    syms = syms - PILOTS
    layers = rest_ref.shape[0] + 1
    rows = syms * pairs
    for ref in (wide_ref, even_ref, odd_ref):
        ref[0:pairs] = jnp.zeros((pairs, ref.shape[1]), jnp.bfloat16)
        ref[pairs + rows :] = jnp.zeros((pairs, ref.shape[1]), jnp.bfloat16)

    def put(ref, whole):
        lanes = whole.shape[1]
        ref[pairs : pairs + rows, :lanes] = whole.astype(jnp.bfloat16)
        ref[pairs : pairs + rows, lanes:] = pltpu.roll(whole, rows - 1, 0).astype(jnp.bfloat16)

    field = with_estimates(syms_ref, own_ref[...].astype(jnp.float32), syms)
    put(wide_ref, field.reshape(rows, 2 * c2))
    src = wide_ref
    for layer in range(1, layers + 1):
        kernel = first_ref[...] if layer == 1 else rest_ref[layer - 2]
        total = layer_sums(
            lambda dt, src=src: src[dt * pairs : dt * pairs + rows], kernel, bias_ref[layer - 1 : layer, :]
        )
        if layer == layers:
            break
        src = (even_ref, odd_ref)[layer % 2]
        put(src, total)
        spread = total.reshape(syms, pairs, c2)
        last = pairs - 2 - layer
        group = last // 8 * 8
        low = pltpu.roll(spread[:, :8], 2, 1)
        high = spread[:, group : group + 8]
        if last % 8 != 4:
            high = pltpu.roll(high, (4 - last % 8) % 8, 1)
        patch_ref[layer - 1] = first_half((syms, 8, c2), low, high)
    final = pltpu.roll(total, layers // 2, 0).astype(jnp.bfloat16)
    llrs = demapped(final, in_ref, in_bias_ref, out_w_ref)
    store_llr(llr_ref, llrs, bit_limits(order_ref, list(range(pairs)), llr_ref.shape[2]), syms_ref)


def edge_kernel(
    syms_ref, order_ref, got_first_ref, got_second_ref, sent_first_ref, sent_second_ref, patch_ref, inner_ref,
    first_ref, rest_ref, bias_ref, in_ref, in_bias_ref, out_w_ref,
    llr_ref, llr_buf, sems,
):
    syms, half = got_first_ref.shape[0] - PILOTS, EDGE // 2
    layers = rest_ref.shape[0] + 1
    subs = llr_ref.shape[1]
    c2 = 2 * got_first_ref.shape[2]
    rows = syms * EDGE
    middle = pl.ds(EDGE, subs - 2 * EDGE)
    inner_copy = pltpu.make_async_copy(inner_ref.at[:, middle], llr_ref.at[:, middle], sems.at[2])
    inner_copy.start()

    def paired(ref_even, ref_odd):
        columns = jnp.where(to_right, ref_even[...], ref_odd[...]).astype(jnp.float32)
        return jnp.concatenate([columns, pltpu.roll(columns, half, 1)], axis=2)

    def row_of(shape):
        return lax.broadcasted_iota(jnp.int32, shape, len(shape) - 2)

    def convolved(this, after, kernel, bias):
        both = jnp.concatenate([this, after], axis=2)
        lanes = both.shape[2]
        padding = jnp.zeros((1, EDGE, lanes), jnp.float32)
        padded = jnp.concatenate([padding, both, padding], axis=0)
        return layer_sums(
            lambda dt: padded[dt : dt + syms].reshape(rows, lanes).astype(jnp.bfloat16), kernel, bias
        ).reshape(syms, EDGE, c2)

    at, blocks = position()
    to_right = at % 2 == 0
    left, right = paired(got_second_ref, got_first_ref), paired(got_first_ref, got_second_ref)
    tail, head = paired(sent_first_ref, sent_second_ref), paired(sent_second_ref, sent_first_ref)
    low = first_half(left.shape, left, pltpu.roll(head, half, 1))
    high = first_half(left.shape, tail, pltpu.roll(right, half, 1))
    this = first_half(low.shape, pltpu.roll(low, EDGE - 1, 1), pltpu.roll(high, 2, 1))
    after = first_half(low.shape, pltpu.roll(low, EDGE - 2, 1), pltpu.roll(high, 1, 1))
    total = convolved(
        with_estimates(syms_ref, this, syms), with_estimates(syms_ref, after, syms),
        first_ref[...], bias_ref[0:1, :],
    )
    row = row_of((EDGE, c2))
    odd = lax.broadcasted_iota(jnp.int32, (EDGE, c2), 1) // (c2 // 2)
    for layer in range(1, layers):
        below = (row < half) & (2 * row + odd < layers - layer) & (at == 0)
        above = (row >= half) & (2 * (row - half) + odd >= 2 + layer) & (at == blocks - 1)
        total = jnp.where((below | above)[None], 0.0, total)
        patch = patch_ref[layer - 1]
        rows_of = row_of(total.shape)
        this = jnp.where(rows_of < half, total, jnp.where(rows_of == half, patch, pltpu.roll(total, 1, 1)))
        after = jnp.where(
            rows_of < half - 1, pltpu.roll(total, EDGE - 1, 1), jnp.where(rows_of == half - 1, patch, total)
        )
        total = convolved(this, after, rest_ref[layer - 1], bias_ref[layer : layer + 1, :])
    llrs = demapped(total.reshape(rows, c2).astype(jnp.bfloat16), in_ref, in_bias_ref, out_w_ref)
    columns = [*range(half), *range(subs // 2 - half, subs // 2)]
    store_llr(llr_buf, llrs, bit_limits(order_ref, columns, llr_ref.shape[2]), syms_ref)
    copies = [
        pltpu.make_async_copy(
            llr_buf.at[:, pl.ds(side * EDGE, EDGE)], llr_ref.at[:, pl.ds(start, EDGE)], sems.at[side]
        )
        for side, start in enumerate((0, subs - EDGE))
    ]
    for copy in copies:
        copy.start()
    inner_copy.wait()
    for copy in copies:
        copy.wait()


def receive_interior(pilot_syms, mod_order, own, weights):
    syms, pairs, c2 = own.shape
    syms = syms - PILOTS
    bits = weights[-1].shape[1]
    layers = weights[1].shape[0] + 1
    smem = pl.BlockSpec(memory_space=pltpu.SMEM)
    vmem = pl.BlockSpec(memory_space=pltpu.VMEM)
    padded = (syms + 2) * pairs
    return pl.pallas_call(
        interior_kernel,
        in_specs=[smem] * 2 + [vmem] * 7,
        out_specs=[vmem] * 2,
        out_shape=[
            jax.ShapeDtypeStruct((syms, 2 * pairs, bits), jnp.float32),
            jax.ShapeDtypeStruct((layers - 1, syms, EDGE, c2), jnp.float32),
        ],
        scratch_shapes=[
            pltpu.VMEM((padded, 4 * c2), jnp.bfloat16),
            pltpu.VMEM((padded, 2 * c2), jnp.bfloat16),
            pltpu.VMEM((padded, 2 * c2), jnp.bfloat16),
        ],
        compiler_params=pltpu.CompilerParams(vmem_limit_bytes=16 * 2**20),
        cost_estimate=pl.CostEstimate(flops=10**9, bytes_accessed=4 * 10**6, transcendentals=0),
        name="interior",
    )(pilot_syms, mod_order, own, *weights)


def receive_edges(pilot_syms, mod_order, got, sent, patch, weights, inner):
    syms, subs, bits = inner.shape
    smem = pl.BlockSpec(memory_space=pltpu.SMEM)
    vmem = pl.BlockSpec(memory_space=pltpu.VMEM)
    return pl.pallas_call(
        edge_kernel,
        in_specs=[smem] * 2 + [vmem] * 12,
        out_specs=pl.BlockSpec(memory_space=pltpu.HBM),
        out_shape=pltpu.HBM(inner.shape, jnp.float32),
        scratch_shapes=[
            pltpu.VMEM((syms, 2 * EDGE, bits), jnp.float32),
            pltpu.SemaphoreType.DMA((3,)),
        ],
        compiler_params=pltpu.CompilerParams(vmem_limit_bytes=16 * 2**20),
        cost_estimate=pl.CostEstimate(flops=5 * 10**8, bytes_accessed=4 * 10**6, transcendentals=0),
        name="edges",
    )(pilot_syms, mod_order, *got, *sent, patch, inner, *weights)


def per_device(
    captured_waveform,
    element_lookup,
    combiner,
    pilot_syms,
    pilot_values,
    mod_order,
    conv_first,
    conv_rest,
    conv_bias,
    demap_in,
    demap_bias,
    demap_out,
):
    given, kept = beam_partials(captured_waveform, element_lookup, combiner)
    panels = lax.axis_size(PANEL)
    got = lax.ppermute(given, PANEL, [(p, p ^ 1) for p in range(panels)])
    pairs = (kept.astype(jnp.float32) + got.astype(jnp.float32)).astype(jnp.bfloat16)
    same_core = [list(range(core, panels, 2)) for core in range(2)]
    parts = lax.all_to_all(pairs, PANEL, 0, 0, axis_index_groups=same_core, tiled=True)
    own, *sent = sum_beams(parts, pilot_syms, pilot_values)
    both = (PANEL, SUB)
    count = lax.axis_size(both)
    pairs_of = [[(i, i + 1) for i in range(start, count - 1, 2)] for start in (0, 1)]
    got = [
        lax.ppermute(edge, both, pairs + [(j, i) for i, j in pairs]) for edge, pairs in zip(sent, pairs_of)
    ]
    c = combiner.shape[1]
    weights = (
        conv_first.reshape(-1, c),
        conv_rest.reshape(conv_rest.shape[0], -1, c),
        conv_bias,
        demap_in,
        demap_bias.reshape(1, -1),
        demap_out,
    )
    inner, patch = receive_interior(pilot_syms, mod_order, own, weights)
    return receive_edges(pilot_syms, mod_order, got, sent, patch, weights, inner)


def solution(mesh):
    in_specs = (
        P(None, None, SUB, PANEL),
        P(PANEL),
        P(PANEL, None),
        P(),
        P(None, (PANEL, SUB)),
        P((PANEL, SUB)),
        P(),
        P(),
        P(),
        P(),
        P(),
        P(),
    )
    out_specs = P(None, (PANEL, SUB), None)
    return jax.shard_map(
        per_device, mesh=mesh, in_specs=in_specs, out_specs=out_specs, check_vma=False
    )
```

time: 55 us -> 52.9 us (0.962)
  blocking collectives: 0 us -> 16.2 us
  waiting for transfers between devices: 14.5 us -> 0.01 us
  Pallas kernels: 14.3 us -> 12.5 us
  starting transfers between devices: 24.5 us -> 23.4 us
  other arithmetic: 1.25 us -> 0.24 us
    all_to_all x0 -> x1, blocking collectives: none -> 16.2 us  [per_device(): lax.all_to_all(pairs, PANEL, 0, 0, axis_index_groups=same_core, tiled=True)]
    all_to_all x1 -> x0, waiting for transfers between devices: 13.5 us -> none  [per_device(): lax.all_to_all(pairs, PANEL, 0, 0, axis_index_groups=same_core, tiled=True)]
    all_to_all x1 -> x0, starting transfers between devices: 3.7 us -> none  [per_device(): lax.all_to_all(pairs, PANEL, 0, 0, axis_index_groups=same_core, tiled=True)]
    ppermute x2, starting transfers between devices: 12.1 us -> 14.6 us  [per_device(): lax.ppermute(edge, both, pairs + [(j, i) for i, j in pairs])]
    pallas_call x1, Pallas kernels: 3.43 us -> 2.32 us  [beam_partials(): pl.pallas_call(given_kernel, in_specs=[hbm] * 3, out_specs=[vmem] * 2, ou...]
    convert_element_type x1, other arithmetic: 1.17 us -> 0.24 us  [per_device(): (kept.astype(jnp.float32) + got.astype(jnp.float32)).astype(jnp.bfloat16)]
    ppermute x2, waiting for transfers between devices: 0.92 us -> 0.01 us  [per_device(): lax.ppermute(edge, both, pairs + [(j, i) for i, j in pairs])]
    pallas_call x1, Pallas kernels: 3.15 us -> 2.26 us  [beam_partials(): pl.pallas_call(kept_kernel, in_specs=[vmem, hbm], out_specs=vmem, out_sha...]
  transfers between devices with their start and end apart: 4 -> 3, of which waited for: 2 -> 0; matrix products, arithmetic and copies ran while one was open for 0% -> 0% of each run, Pallas kernels for 6% -> 11%
where the time goes in v3:
time: 52.9 us; the launch traced here: 52.6 us
  starting transfers between devices  23.4 us (44%)
  blocking collectives  16.2 us (31%)
  Pallas kernels  12.5 us (24%)
    all_to_all x1, blocking collectives, per_device(): lax.all_to_all(pairs, PANEL, 0, 0, axis_index_groups=same_core, tiled=True)  16.2 us
    ppermute x2, starting transfers between devices, per_device(): lax.ppermute(edge, both, pairs + [(j, i) for i, j in pairs])  14.6 us
    ppermute x1, starting transfers between devices, per_device(): got = lax.ppermute(given, PANEL, [(p, p ^ 1) for p in range(panels)])  8.79 us
    pallas_call x1, Pallas kernels, receive_interior(): pl.pallas_call(interior_kernel, in_specs=[smem] * 2 + [vmem] * 7, out_spe...  3.64 us
    pallas_call x1, Pallas kernels, receive_edges(): pl.pallas_call(edge_kernel, in_specs=[smem] * 2 + [vmem] * 12, out_specs=...  3.46 us
    pallas_call x1, Pallas kernels, beam_partials(): pl.pallas_call(given_kernel, in_specs=[hbm] * 3, out_specs=[vmem] * 2, ou...  2.32 us
    pallas_call x1, Pallas kernels, beam_partials(): pl.pallas_call(kept_kernel, in_specs=[vmem, hbm], out_specs=vmem, out_sha...  2.26 us
  transfers between devices with their start and end apart: 3, of which 0 were waited for; matrix products, arithmetic and copies ran while one was open for 0% of the time, Pallas kernels for 11%

profile of v3, /device:TPU:1, one launch (start us, length us, event | category | flops | bytes accessed | tf_op | source)
XLA Modules:
  0.0 52.6 jit_solution(11001598136705395466)
XLA Ops:
  0.0 2.3 %given.1 = (bf16[8,14,32,128]{3,2,1,0:T(8,128)(2,1)S(1)}, bf16[256,128]{1,0:T(8,128)(2,1)S(1)}) custom-call(s32[1,128]{1,0:T(1,128)} %bitcast.10, bf16[128,128]{1,0:T(8,128)(2,1)} %rows_ref.1, bf16[16,14,32,256]{3,2,1,0:T(8,128)(2,1)} %wave_ref.3), custom_call_target="tpu_custom_call" | custom-call | tf_op jit(solution)/shard_map/given/pallas_call | solution.py:89
  2.3 8.8 %collective-permute-start = (bf16[8,14,32,128]{3,2,1,0:T(8,128)(2,1)S(1)}, bf16[8,14,32,128]{3,2,1,0:T(8,128)(2,1)S(1)}, u32[]{:S(2)}, u32[]{:S(2)}) collective-permute-start(bf16[8,14,32,128]{3,2,1,0:T(8,128)(2,1)S(1)} %get-tuple-element.13), channel_id=1, source_target_pairs={{0,32},{32,0},{64,96},{96,64},{128,160},{160,128},{192,224},{224,1... | collective-permute-start | bytes 2752520 | tf_op jit(solution)/shard_map/ppermute | solution.py:417
  11.1 2.3 %kept.1 = bf16[8,14,32,128]{3,2,1,0:T(8,128)(2,1)S(1)} custom-call(bf16[256,128]{1,0:T(8,128)(2,1)S(1)} %get-tuple-element.12.matrix_ref, bf16[16,14,32,256]{3,2,1,0:T(8,128)(2,1)} %wave_ref.3), custom_call_target="tpu_custom_call" | custom-call | flops 234881024 | bytes 1835008 | tf_op jit(solution)/shard_map/kept/pallas_call | solution.py:103
  13.4 0.0 copy-start.5
  13.4 0.0 copy-start.7
  13.4 0.0 collective-permute-done
  13.4 0.2 add_convert_fusion
  13.7 0.0 copy-start
  13.7 0.0 copy-start.1
  13.7 0.0 copy-start.2
  13.7 0.0 copy-start.3
  13.7 0.0 copy-start.4
  13.7 0.0 copy-start.6
  13.8 0.0 copy-start.8
  13.8 16.2 %all_to_all.5.parts_ref = bf16[8,14,32,128]{3,2,1,0:T(8,128)(2,1)S(1)} all-to-all(bf16[8,14,32,128]{3,2,1,0:T(8,128)(2,1)S(1)} %add_convert_fusion), channel_id=1, replica_groups={{0,64,128,192,256,320,384,448},{32,96,160,224,288,352,416,480},{1,65,12..., dimensions={0} | all-to-all | bytes 1835008 | tf_op jit(solution)/shard_map/all_to_all | solution.py:420
  29.9 0.0 copy-done.5
  30.0 0.0 copy-done.7
  30.0 0.8 %sum_beams.1 = (bf16[16,16,256]{2,1,0:T(8,128)(2,1)S(1)}, bf16[16,8,128]{2,1,0:T(8,128)(2,1)S(1)}, bf16[16,8,128]{2,1,0:T(8,128)(2,1)S(1)}) custom-call(s32[2]{0:T(128)S(1)} %copy-done.5, f32[2,32]{1,0:T(2,128)S(1)} %copy-done.7, bf16[8,14,32,128]{3,2,1,0:T(8,128)(2,1)S(1)} %all_to_all.5.parts_ref), custom_call_target="tpu_custom_call" | custom-call | tf_op jit(solution)/shard_map/sum_beams/pallas_call | solution.py:174
  30.8 1.9 %collective-permute-start.1 = (bf16[16,8,128]{2,1,0:T(8,128)(2,1)S(1)}, bf16[16,8,128]{2,1,0:T(8,128)(2,1)S(1)}, u32[]{:S(2)}, u32[]{:S(2)}) collective-permute-start(bf16[16,8,128]{2,1,0:T(8,128)(2,1)S(1)} %get-tuple-element.14.sent_first_ref), channel_id=1, source_target_pairs={{0,1},{2,3},{4,5},{6,7},{8,9},{10,11},{12,13},{14,15},{16,17},{18,... | collective-permute-start | bytes 98312 | tf_op jit(solution)/shard_map/ppermute | solution.py:426
  32.7 12.7 %collective-permute-start.2 = (bf16[16,8,128]{2,1,0:T(8,128)(2,1)S(1)}, bf16[16,8,128]{2,1,0:T(8,128)(2,1)S(1)}, u32[]{:S(2)}, u32[]{:S(2)}) collective-permute-start(bf16[16,8,128]{2,1,0:T(8,128)(2,1)S(1)} %get-tuple-element.15.sent_second_ref), channel_id=1, source_target_pairs={{1,2},{3,4},{5,6},{7,8},{9,10},{11,12},{13,14},{15,16},{17,18},{19... | collective-permute-start | bytes 98312 | tf_op jit(solution)/shard_map/ppermute | solution.py:426
  45.4 0.0 copy-done
  45.4 0.0 copy-done.1
  45.5 0.0 copy-done.2
  45.5 0.0 copy-done.3
  45.5 0.0 copy-done.4
  45.5 0.0 copy-done.6
  45.5 0.0 copy-done.8
  45.5 3.6 %interior.1 = (f32[14,32,128]{2,1,0:T(8,128)S(1)}, f32[5,14,8,256]{3,2,1,0:T(8,128)S(1)}) custom-call(s32[2]{0:T(128)S(1)} %copy-done.5, s32[8]{0:T(128)S(1)} %copy-done.8, bf16[16,16,256]{2,1,0:T(8,128)(2,1)S(1)} %get-tuple-element.16.own_ref, bf16[2304,128]{1,0:T(8,128)(2,1)S(1)} %bitcast.6, bf16[5,1152,128]{2,1,0:T(8,128)(2,1)S(1)} %bitcast.4, ...), custom_call_target="tpu_custom_call" | custom-call | flops 1000000000 | bytes 4000000 | tf_op jit(solution)/shard_map/interior/pallas_call | solution.py:363
  49.2 0.0 collective-permute-done.1.got_first_ref
  49.2 0.0 collective-permute-done.2.got_second_ref
  49.2 3.5 %edges.1 = f32[14,32,128]{2,1,0:T(8,128)} custom-call(s32[2]{0:T(128)S(1)} %copy-done.5, s32[8]{0:T(128)S(1)} %copy-done.8, bf16[16,8,128]{2,1,0:T(8,128)(2,1)S(1)} %collective-permute-done.1.got_first_ref, bf16[16,8,128]{2,1,0:T(8,128)(2,1)S(1)} %collective-permute-done.2.got_second_ref, bf16[16,8,128]{2,1,0:T(8,128)(2,1)S(1)} %get-tuple-element.14.sent_first_ref, ...), custom_call_target="tpu_custom_call" | custom-call | flops 500000000 | bytes 4000000 | tf_op jit(solution)/shard_map/edges/pallas_call | solution.py:386
Async XLA Ops:
  2.3 11.1 %collective-permute-start = (bf16[8,14,32,128]{3,2,1,0:T(8,128)(2,1)S(1)}, bf16[8,14,32,128]{3,2,1,0:T(8,128)(2,1)S(1)}, u32[]{:S(2)}, u32[]{:S(2)}) collective-permute-start(bf16[8,14,32,128]{3,2,1,0:T(8,128)(2,1)S(1)} %get-tuple-element.13), channel_id=1, source_target_pairs={{0,32},{32,0},{64,96},{96,64},{128,160},{160,128},{192,224},{224,1... | collective-permute-start | bytes 2752520 | tf_op jit(solution)/shard_map/ppermute | solution.py:417
  13.4 16.6 %copy-start.5 = (s32[2]{0:T(128)S(1)}, s32[2]{0:T(128)}, u32[]{:S(2)}) copy-start(s32[2]{0:T(128)} %syms_ref.5) | copy-start | bytes 28
  13.4 16.5 %copy-start.7 = (f32[2,32]{1,0:T(2,128)S(1)}, f32[2,32]{1,0:T(2,128)}, u32[]{:S(2)}) copy-start(f32[2,32]{1,0:T(2,128)} %pilot_ref.1) | copy-start | bytes 772
  13.7 31.8 %copy-start = (bf16[5,3,3,128,128]{4,3,2,1,0:T(8,128)(2,1)S(1)}, bf16[5,3,3,128,128]{4,3,2,1,0:T(8,128)(2,1)}, u32[]{:S(2)}) copy-start(bf16[5,3,3,128,128]{4,3,2,1,0:T(8,128)(2,1)} %param.19) | copy-start | bytes 4423684
  13.7 31.8 %copy-start.1 = (bf16[3,3,256,128]{3,2,1,0:T(8,128)(2,1)S(1)}, bf16[3,3,256,128]{3,2,1,0:T(8,128)(2,1)}, u32[]{:S(2)}) copy-start(bf16[3,3,256,128]{3,2,1,0:T(8,128)(2,1)} %param.18) | copy-start | bytes 1769476
  13.7 31.8 %copy-start.2 = (bf16[128,256]{1,0:T(8,128)(2,1)S(1)}, bf16[128,256]{1,0:T(8,128)(2,1)}, u32[]{:S(2)}) copy-start(bf16[128,256]{1,0:T(8,128)(2,1)} %in_ref.3) | copy-start | bytes 196612
  13.7 31.8 %copy-start.3 = (bf16[256,128]{1,0:T(8,128)(2,1)S(1)}, bf16[256,128]{1,0:T(8,128)(2,1)}, u32[]{:S(2)}) copy-start(bf16[256,128]{1,0:T(8,128)(2,1)} %out_w_ref.3) | copy-start | bytes 196612
  13.7 31.7 %copy-start.4 = (f32[6,128]{1,0:T(8,128)S(1)}, f32[6,128]{1,0:T(8,128)}, u32[]{:S(2)}) copy-start(f32[6,128]{1,0:T(8,128)} %bias_ref.3) | copy-start | bytes 9220
  13.7 31.7 %copy-start.6 = (f32[256]{0:T(256)S(1)}, f32[256]{0:T(256)}, u32[]{:S(2)}) copy-start(f32[256]{0:T(256)} %param.22) | copy-start | bytes 3076
  13.8 31.7 %copy-start.8 = (s32[8]{0:T(128)S(1)}, s32[8]{0:T(128)}, u32[]{:S(2)}) copy-start(s32[8]{0:T(128)} %order_ref.3) | copy-start | bytes 100
  30.8 18.4 %collective-permute-start.1 = (bf16[16,8,128]{2,1,0:T(8,128)(2,1)S(1)}, bf16[16,8,128]{2,1,0:T(8,128)(2,1)S(1)}, u32[]{:S(2)}, u32[]{:S(2)}) collective-permute-start(bf16[16,8,128]{2,1,0:T(8,128)(2,1)S(1)} %get-tuple-element.14.sent_first_ref), channel_id=1, source_target_pairs={{0,1},{2,3},{4,5},{6,7},{8,9},{10,11},{12,13},{14,15},{16,17},{18,... | collective-permute-start | bytes 98312 | tf_op jit(solution)/shard_map/ppermute | solution.py:426
  32.7 16.4 %collective-permute-start.2 = (bf16[16,8,128]{2,1,0:T(8,128)(2,1)S(1)}, bf16[16,8,128]{2,1,0:T(8,128)(2,1)S(1)}, u32[]{:S(2)}, u32[]{:S(2)}) collective-permute-start(bf16[16,8,128]{2,1,0:T(8,128)(2,1)S(1)} %get-tuple-element.15.sent_second_ref), channel_id=1, source_target_pairs={{1,2},{3,4},{5,6},{7,8},{9,10},{11,12},{13,14},{15,16},{17,18},{19... | collective-permute-start | bytes 98312 | tf_op jit(solution)/shard_map/ppermute | solution.py:426

commit v4 on v3

--- a/solution.py
+++ b/solution.py
@@ -8,6 +8,7 @@
 RB_SC = 4
 BITS = 8
 PILOTS = 2
+FIRST = 1
 EDGE = 8
 PANEL = "panel"
 SUB = "sc"
@@ -144,7 +145,8 @@
     return jnp.where(lax.broadcasted_iota(jnp.int32, rows, len(rows) - 2) < EDGE // 2, low, high)
 
 
-def sum_kernel(syms_ref, pilot_ref, parts_ref, own_ref, first_ref, second_ref, beams_ref):
+def sum_kernel(syms_ref, order_ref, pilot_ref, parts_ref, *refs):
+    *weights, own_ref, tail_ref, head_ref, llr_ref, patch_ref, wide_ref, even_ref, odd_ref, beams_ref = refs
     panels, syms, subs, c = parts_ref.shape
     for t in range(syms):
         total = parts_ref[0, t].astype(jnp.float32)
@@ -162,24 +164,62 @@
     rows = (syms + PILOTS, EDGE, c)
     head = first_half(rows, even[:, :EDGE], pltpu.roll(odd[:, :EDGE], half, 1))
     tail = first_half(rows, pltpu.roll(even[:, subs // 2 - EDGE :], half, 1), odd[:, subs // 2 - EDGE :])
-    to_right = position()[0] % 2 == 0
-    first_ref[...] = jnp.where(to_right, tail, head).astype(jnp.bfloat16)
-    second_ref[...] = jnp.where(to_right, head, tail).astype(jnp.bfloat16)
-
-
-def sum_beams(parts, pilot_syms, pilot_values):
+    tail_ref[...] = tail.astype(jnp.bfloat16)
+    head_ref[...] = head.astype(jnp.bfloat16)
+
+    @pl.when(waits_long())
+    def _():
+        interior(syms_ref, order_ref, own_ref, *weights, llr_ref, patch_ref, wide_ref, even_ref, odd_ref)
+
+
+def late_kernel(syms_ref, order_ref, own_ref, *refs):
+    *weights, early_llr_ref, early_patch_ref, llr_ref, patch_ref, wide_ref, even_ref, odd_ref = refs
+    del early_llr_ref, early_patch_ref
+
+    @pl.when(jnp.logical_not(waits_long()))
+    def _():
+        interior(syms_ref, order_ref, own_ref, *weights, llr_ref, patch_ref, wide_ref, even_ref, odd_ref)
+
+
+def waits_long():
+    return lax.axis_index(SUB) < FIRST
+
+
+def interior_shapes(syms, subs, c, layers, bits):
+    return [
+        jax.ShapeDtypeStruct((syms, subs, bits), jnp.float32),
+        jax.ShapeDtypeStruct((layers - 1, syms, EDGE, 2 * c), jnp.float32),
+    ]
+
+
+def interior_scratch(syms, subs, c):
+    padded = (syms + 2) * (subs // 2)
+    return [pltpu.VMEM((padded, lanes * c), jnp.bfloat16) for lanes in (8, 4, 4)]
+
+
+def sum_beams(parts, pilot_syms, mod_order, pilot_values, weights):
     _, syms, subs, c = parts.shape
+    smem = pl.BlockSpec(memory_space=pltpu.SMEM)
     vmem = pl.BlockSpec(memory_space=pltpu.VMEM)
     edge = jax.ShapeDtypeStruct((syms + PILOTS, EDGE, c), jnp.bfloat16)
+    layers, bits = weights[1].shape[0] + 1, weights[-1].shape[1]
     return pl.pallas_call(
         sum_kernel,
-        in_specs=[pl.BlockSpec(memory_space=pltpu.SMEM), vmem, vmem],
-        out_specs=[vmem] * 3,
-        out_shape=[jax.ShapeDtypeStruct((syms + PILOTS, subs // 2, 2 * c), jnp.bfloat16), edge, edge],
-        scratch_shapes=[pltpu.VMEM((syms + PILOTS, subs, c), jnp.float32)],
-        compiler_params=pltpu.CompilerParams(vmem_limit_bytes=8 * 2**20),
+        in_specs=[smem] * 2 + [vmem] * 8,
+        out_specs=[vmem] * 5,
+        out_shape=[
+            jax.ShapeDtypeStruct((syms + PILOTS, subs // 2, 2 * c), jnp.bfloat16),
+            edge,
+            edge,
+            *interior_shapes(syms, subs, c, layers, bits),
+        ],
+        scratch_shapes=[
+            *interior_scratch(syms, subs, c),
+            pltpu.VMEM((syms + PILOTS, subs, c), jnp.float32),
+        ],
+        compiler_params=pltpu.CompilerParams(vmem_limit_bytes=16 * 2**20),
         name="sum_beams",
-    )(pilot_syms, pilot_values, parts)
+    )(pilot_syms, mod_order, pilot_values, parts, *weights)
 
 
 def pilot_rows(syms_ref, rows, syms):
@@ -239,7 +279,7 @@
             ref[t, pl.ds(side, rows, 2), :] = jnp.where(keep, llr[t * rows : (t + 1) * rows], 0.0)
 
 
-def interior_kernel(
+def interior(
     syms_ref, order_ref, own_ref, first_ref, rest_ref, bias_ref, in_ref, in_bias_ref, out_w_ref,
     llr_ref, patch_ref, wide_ref, even_ref, odd_ref,
 ):
@@ -282,21 +322,21 @@
 
 
 def edge_kernel(
-    syms_ref, order_ref, got_first_ref, got_second_ref, sent_first_ref, sent_second_ref, patch_ref, inner_ref,
+    syms_ref, order_ref, left_ref, right_ref, tail_ref, head_ref, patch_ref, inner_ref,
     first_ref, rest_ref, bias_ref, in_ref, in_bias_ref, out_w_ref,
     llr_ref, llr_buf, sems,
 ):
-    syms, half = got_first_ref.shape[0] - PILOTS, EDGE // 2
+    syms, half = left_ref.shape[0] - PILOTS, EDGE // 2
     layers = rest_ref.shape[0] + 1
     subs = llr_ref.shape[1]
-    c2 = 2 * got_first_ref.shape[2]
+    c2 = 2 * left_ref.shape[2]
     rows = syms * EDGE
     middle = pl.ds(EDGE, subs - 2 * EDGE)
     inner_copy = pltpu.make_async_copy(inner_ref.at[:, middle], llr_ref.at[:, middle], sems.at[2])
     inner_copy.start()
 
-    def paired(ref_even, ref_odd):
-        columns = jnp.where(to_right, ref_even[...], ref_odd[...]).astype(jnp.float32)
+    def paired(ref):
+        columns = ref[...].astype(jnp.float32)
         return jnp.concatenate([columns, pltpu.roll(columns, half, 1)], axis=2)
 
     def row_of(shape):
@@ -312,9 +352,7 @@
         ).reshape(syms, EDGE, c2)
 
     at, blocks = position()
-    to_right = at % 2 == 0
-    left, right = paired(got_second_ref, got_first_ref), paired(got_first_ref, got_second_ref)
-    tail, head = paired(sent_first_ref, sent_second_ref), paired(sent_second_ref, sent_first_ref)
+    left, right, tail, head = (paired(ref) for ref in (left_ref, right_ref, tail_ref, head_ref))
     low = first_half(left.shape, left, pltpu.roll(head, half, 1))
     high = first_half(left.shape, tail, pltpu.roll(right, half, 1))
     this = first_half(low.shape, pltpu.roll(low, EDGE - 1, 1), pltpu.roll(high, 2, 1))
@@ -352,31 +390,23 @@
         copy.wait()
 
 
-def receive_interior(pilot_syms, mod_order, own, weights):
+def receive_interior(pilot_syms, mod_order, own, weights, early):
     syms, pairs, c2 = own.shape
     syms = syms - PILOTS
-    bits = weights[-1].shape[1]
-    layers = weights[1].shape[0] + 1
+    layers, bits = weights[1].shape[0] + 1, weights[-1].shape[1]
     smem = pl.BlockSpec(memory_space=pltpu.SMEM)
     vmem = pl.BlockSpec(memory_space=pltpu.VMEM)
-    padded = (syms + 2) * pairs
     return pl.pallas_call(
-        interior_kernel,
-        in_specs=[smem] * 2 + [vmem] * 7,
+        late_kernel,
+        in_specs=[smem] * 2 + [vmem] * 9,
         out_specs=[vmem] * 2,
-        out_shape=[
-            jax.ShapeDtypeStruct((syms, 2 * pairs, bits), jnp.float32),
-            jax.ShapeDtypeStruct((layers - 1, syms, EDGE, c2), jnp.float32),
-        ],
-        scratch_shapes=[
-            pltpu.VMEM((padded, 4 * c2), jnp.bfloat16),
-            pltpu.VMEM((padded, 2 * c2), jnp.bfloat16),
-            pltpu.VMEM((padded, 2 * c2), jnp.bfloat16),
-        ],
+        out_shape=interior_shapes(syms, 2 * pairs, c2 // 2, layers, bits),
+        input_output_aliases={9: 0, 10: 1},
+        scratch_shapes=interior_scratch(syms, 2 * pairs, c2 // 2),
         compiler_params=pltpu.CompilerParams(vmem_limit_bytes=16 * 2**20),
         cost_estimate=pl.CostEstimate(flops=10**9, bytes_accessed=4 * 10**6, transcendentals=0),
         name="interior",
-    )(pilot_syms, mod_order, own, *weights)
+    )(pilot_syms, mod_order, own, *weights, *early)
 
 
 def receive_edges(pilot_syms, mod_order, got, sent, patch, weights, inner):
@@ -418,13 +448,6 @@
     pairs = (kept.astype(jnp.float32) + got.astype(jnp.float32)).astype(jnp.bfloat16)
     same_core = [list(range(core, panels, 2)) for core in range(2)]
     parts = lax.all_to_all(pairs, PANEL, 0, 0, axis_index_groups=same_core, tiled=True)
-    own, *sent = sum_beams(parts, pilot_syms, pilot_values)
-    both = (PANEL, SUB)
-    count = lax.axis_size(both)
-    pairs_of = [[(i, i + 1) for i in range(start, count - 1, 2)] for start in (0, 1)]
-    got = [
-        lax.ppermute(edge, both, pairs + [(j, i) for i, j in pairs]) for edge, pairs in zip(sent, pairs_of)
-    ]
     c = combiner.shape[1]
     weights = (
         conv_first.reshape(-1, c),
@@ -434,8 +457,13 @@
         demap_bias.reshape(1, -1),
         demap_out,
     )
-    inner, patch = receive_interior(pilot_syms, mod_order, own, weights)
-    return receive_edges(pilot_syms, mod_order, got, sent, patch, weights, inner)
+    own, tail, head, *early = sum_beams(parts, pilot_syms, mod_order, pilot_values, weights)
+    both = (PANEL, SUB)
+    count = lax.axis_size(both)
+    left = lax.ppermute(tail, both, [(i, i + 1) for i in range(count - 1)])
+    right = lax.ppermute(head, both, [(i + 1, i) for i in range(count - 1)])
+    inner, patch = receive_interior(pilot_syms, mod_order, own, weights, early)
+    return receive_edges(pilot_syms, mod_order, (left, right), (tail, head), patch, weights, inner)
 
 
 def solution(mesh):

time: 52.9 us -> 49.4 us (0.934)
  starting transfers between devices: 23.4 us -> 19.4 us
    ppermute x2, starting transfers between devices: 14.6 us -> 10.6 us  [the longest x1 8.67 us: per_device(): right = lax.ppermute(head, both, [(i + 1, i) for i in range(count - 1)])]
  transfers between devices with their start and end apart: 3 -> 3, of which waited for: 0 -> 1; matrix products, arithmetic and copies ran while one was open for 0% -> 0% of each run, Pallas kernels for 11% -> 6%
where the time goes in v4:
time: 49.4 us; the launch traced here: 49.2 us
  starting transfers between devices  19.4 us (39%)
  blocking collectives  16.3 us (33%)
  Pallas kernels  12.5 us (25%)
    all_to_all x1, blocking collectives, per_device(): lax.all_to_all(pairs, PANEL, 0, 0, axis_index_groups=same_core, tiled=True)  16.3 us
    ppermute x1, starting transfers between devices, per_device(): got = lax.ppermute(given, PANEL, [(p, p ^ 1) for p in range(panels)])  8.79 us
    ppermute x1, starting transfers between devices, per_device(): right = lax.ppermute(head, both, [(i + 1, i) for i in range(count - 1)])  8.67 us
    pallas_call x1, Pallas kernels, sum_beams(): pl.pallas_call(sum_kernel, in_specs=[smem] * 2 + [vmem] * 8, out_specs=[v...  3.95 us
    pallas_call x1, Pallas kernels, receive_edges(): pl.pallas_call(edge_kernel, in_specs=[smem] * 2 + [vmem] * 12, out_specs=...  3.45 us
    pallas_call x1, Pallas kernels, beam_partials(): pl.pallas_call(given_kernel, in_specs=[hbm] * 3, out_specs=[vmem] * 2, ou...  2.32 us
    pallas_call x1, Pallas kernels, beam_partials(): pl.pallas_call(kept_kernel, in_specs=[vmem, hbm], out_specs=vmem, out_sha...  2.26 us
    ppermute x1, starting transfers between devices, per_device(): left = lax.ppermute(tail, both, [(i, i + 1) for i in range(count - 1)])  1.92 us
  transfers between devices with their start and end apart: 3, of which 1 were waited for; matrix products, arithmetic and copies ran while one was open for 0% of the time, Pallas kernels for 6%

profile of v4, /device:TPU:1, one launch (start us, length us, event | category | flops | bytes accessed | tf_op | source)
XLA Modules:
  0.0 49.2 jit_solution(15416374224403845733)
XLA Ops:
  0.0 2.3 %given.1 = (bf16[8,14,32,128]{3,2,1,0:T(8,128)(2,1)S(1)}, bf16[256,128]{1,0:T(8,128)(2,1)S(1)}) custom-call(s32[1,128]{1,0:T(1,128)} %bitcast.13, bf16[128,128]{1,0:T(8,128)(2,1)} %rows_ref.1, bf16[16,14,32,256]{3,2,1,0:T(8,128)(2,1)} %wave_ref.3), custom_call_target="tpu_custom_call" | custom-call | tf_op jit(solution)/shard_map/given/pallas_call | solution.py:90
  2.3 8.8 %collective-permute-start = (bf16[8,14,32,128]{3,2,1,0:T(8,128)(2,1)S(1)}, bf16[8,14,32,128]{3,2,1,0:T(8,128)(2,1)S(1)}, u32[]{:S(2)}, u32[]{:S(2)}) collective-permute-start(bf16[8,14,32,128]{3,2,1,0:T(8,128)(2,1)S(1)} %get-tuple-element.15), channel_id=1, source_target_pairs={{0,32},{32,0},{64,96},{96,64},{128,160},{160,128},{192,224},{224,1... | collective-permute-start | bytes 2752520 | tf_op jit(solution)/shard_map/ppermute | solution.py:447
  11.1 2.3 %kept.1 = bf16[8,14,32,128]{3,2,1,0:T(8,128)(2,1)S(1)} custom-call(bf16[256,128]{1,0:T(8,128)(2,1)S(1)} %get-tuple-element.14.matrix_ref, bf16[16,14,32,256]{3,2,1,0:T(8,128)(2,1)} %wave_ref.3), custom_call_target="tpu_custom_call" | custom-call | flops 234881024 | bytes 1835008 | tf_op jit(solution)/shard_map/kept/pallas_call | solution.py:104
  13.4 0.0 copy-start
  13.4 0.0 copy-start.1
  13.4 0.0 copy-start.2
  13.4 0.0 copy-start.3
  13.4 0.0 copy-start.4
  13.5 0.0 copy-start.5
  13.5 0.0 copy-start.6
  13.5 0.0 copy-start.7
  13.5 0.0 copy-start.8
  13.5 0.0 collective-permute-done
  13.5 0.2 add_convert_fusion
  13.8 16.3 %all_to_all.5.parts_ref = bf16[8,14,32,128]{3,2,1,0:T(8,128)(2,1)S(1)} all-to-all(bf16[8,14,32,128]{3,2,1,0:T(8,128)(2,1)S(1)} %add_convert_fusion), channel_id=1, replica_groups={{0,64,128,192,256,320,384,448},{32,96,160,224,288,352,416,480},{1,65,12..., dimensions={0} | all-to-all | bytes 1835008 | tf_op jit(solution)/shard_map/all_to_all | solution.py:450
  30.1 0.0 copy-done
  30.1 0.0 copy-done.1
  30.1 0.0 copy-done.2
  30.1 0.0 copy-done.3
  30.1 0.0 copy-done.4
  30.1 0.0 copy-done.5
  30.1 0.0 copy-done.6
  30.1 0.0 copy-done.7
  30.2 0.0 copy-done.8
  30.2 3.9 %sum_beams.1 = (bf16[16,16,256]{2,1,0:T(8,128)(2,1)S(1)}, bf16[16,8,128]{2,1,0:T(8,128)(2,1)S(1)}, bf16[16,8,128]{2,1,0:T(8,128)(2,1)S(1)}, f32[14,32,128]{2,1,0:T(8,128)S(1)}, f32[5,14,8,256]{3,2,1,0:T(8,128)S(1)}) custom-call(s32[2]{0:T(128)S(1)} %copy-done.6, s32[8]{0:T(128)S(1)} %copy-done.7, f32[2,32]{1,0:T(2,128)S(1)} %copy-done.8, ...), custom_call_target="tpu_custom_call" | custom-call | tf_op jit(solution)/shard_map/sum_beams/pallas_call | solution.py:206
  34.1 1.9 %collective-permute-start.1 = (bf16[16,8,128]{2,1,0:T(8,128)(2,1)S(1)}, bf16[16,8,128]{2,1,0:T(8,128)(2,1)S(1)}, u32[]{:S(2)}, u32[]{:S(2)}) collective-permute-start(bf16[16,8,128]{2,1,0:T(8,128)(2,1)S(1)} %get-tuple-element.16.tail_ref), channel_id=1, source_target_pairs={{0,1},{1,2},{2,3},{3,4},{4,5},{5,6},{6,7},{7,8},{8,9},{9,10},{10,1... | collective-permute-start | bytes 98312 | tf_op jit(solution)/shard_map/ppermute | solution.py:463
  36.0 8.7 %collective-permute-start.2 = (bf16[16,8,128]{2,1,0:T(8,128)(2,1)S(1)}, bf16[16,8,128]{2,1,0:T(8,128)(2,1)S(1)}, u32[]{:S(2)}, u32[]{:S(2)}) collective-permute-start(bf16[16,8,128]{2,1,0:T(8,128)(2,1)S(1)} %get-tuple-element.17.head_ref), channel_id=1, source_target_pairs={{1,0},{2,1},{3,2},{4,3},{5,4},{6,5},{7,6},{8,7},{9,8},{10,9},{11,1... | collective-permute-start | bytes 98312 | tf_op jit(solution)/shard_map/ppermute | solution.py:464
  44.7 0.6 %interior.1 = (f32[14,32,128]{2,1,0:T(8,128)S(1)}, f32[5,14,8,256]{3,2,1,0:T(8,128)S(1)}) custom-call(s32[2]{0:T(128)S(1)} %copy-done.6, s32[8]{0:T(128)S(1)} %copy-done.7, bf16[16,16,256]{2,1,0:T(8,128)(2,1)S(1)} %get-tuple-element.18.own_ref, bf16[2304,128]{1,0:T(8,128)(2,1)S(1)} %bitcast.8, ...), custom_call_target="tpu_custom_call", output_to_operand_aliasing={{0}: (9, {}), {1}: (10, {})} | custom-call | flops 1000000000 | bytes 4000000 | tf_op jit(solution)/shard_map/interior/pallas_call | solution.py:399
  45.3 0.0 collective-permute-done.1.left_ref
  45.3 0.4 collective-permute-done.2.right_ref
  45.7 3.5 %edges.1 = f32[14,32,128]{2,1,0:T(8,128)} custom-call(s32[2]{0:T(128)S(1)} %copy-done.6, s32[8]{0:T(128)S(1)} %copy-done.7, bf16[16,8,128]{2,1,0:T(8,128)(2,1)S(1)} %collective-permute-done.1.left_ref, bf16[16,8,128]{2,1,0:T(8,128)(2,1)S(1)} %collective-permute-done.2.right_ref, bf16[16,8,128]{2,1,0:T(8,128)(2,1)S(1)} %get-tuple-element.16.tail_ref, ...), custom_call_target="tpu_custom_call" | custom-call | flops 500000000 | bytes 4000000 | tf_op jit(solution)/shard_map/edges/pallas_call | solution.py:416
Async XLA Ops:
  2.3 11.2 %collective-permute-start = (bf16[8,14,32,128]{3,2,1,0:T(8,128)(2,1)S(1)}, bf16[8,14,32,128]{3,2,1,0:T(8,128)(2,1)S(1)}, u32[]{:S(2)}, u32[]{:S(2)}) collective-permute-start(bf16[8,14,32,128]{3,2,1,0:T(8,128)(2,1)S(1)} %get-tuple-element.15), channel_id=1, source_target_pairs={{0,32},{32,0},{64,96},{96,64},{128,160},{160,128},{192,224},{224,1... | collective-permute-start | bytes 2752520 | tf_op jit(solution)/shard_map/ppermute | solution.py:447
  13.4 16.7 %copy-start = (bf16[5,3,3,128,128]{4,3,2,1,0:T(8,128)(2,1)S(1)}, bf16[5,3,3,128,128]{4,3,2,1,0:T(8,128)(2,1)}, u32[]{:S(2)}) copy-start(bf16[5,3,3,128,128]{4,3,2,1,0:T(8,128)(2,1)} %param.19) | copy-start | bytes 4423684
  13.4 16.7 %copy-start.1 = (bf16[3,3,256,128]{3,2,1,0:T(8,128)(2,1)S(1)}, bf16[3,3,256,128]{3,2,1,0:T(8,128)(2,1)}, u32[]{:S(2)}) copy-start(bf16[3,3,256,128]{3,2,1,0:T(8,128)(2,1)} %param.18) | copy-start | bytes 1769476
  13.4 16.7 %copy-start.2 = (bf16[128,256]{1,0:T(8,128)(2,1)S(1)}, bf16[128,256]{1,0:T(8,128)(2,1)}, u32[]{:S(2)}) copy-start(bf16[128,256]{1,0:T(8,128)(2,1)} %in_ref.1) | copy-start | bytes 196612
  13.4 16.7 %copy-start.3 = (bf16[256,128]{1,0:T(8,128)(2,1)S(1)}, bf16[256,128]{1,0:T(8,128)(2,1)}, u32[]{:S(2)}) copy-start(bf16[256,128]{1,0:T(8,128)(2,1)} %out_w_ref.1) | copy-start | bytes 196612
  13.4 16.7 %copy-start.4 = (f32[6,128]{1,0:T(8,128)S(1)}, f32[6,128]{1,0:T(8,128)}, u32[]{:S(2)}) copy-start(f32[6,128]{1,0:T(8,128)} %bias_ref.1) | copy-start | bytes 9220
  13.5 16.7 %copy-start.5 = (f32[256]{0:T(256)S(1)}, f32[256]{0:T(256)}, u32[]{:S(2)}) copy-start(f32[256]{0:T(256)} %param.22) | copy-start | bytes 3076
  13.5 16.7 %copy-start.6 = (s32[2]{0:T(128)S(1)}, s32[2]{0:T(128)}, u32[]{:S(2)}) copy-start(s32[2]{0:T(128)} %syms_ref.5) | copy-start | bytes 28
  13.5 16.7 %copy-start.7 = (s32[8]{0:T(128)S(1)}, s32[8]{0:T(128)}, u32[]{:S(2)}) copy-start(s32[8]{0:T(128)} %order_ref.5) | copy-start | bytes 100
  13.5 16.7 %copy-start.8 = (f32[2,32]{1,0:T(2,128)S(1)}, f32[2,32]{1,0:T(2,128)}, u32[]{:S(2)}) copy-start(f32[2,32]{1,0:T(2,128)} %pilot_ref.1) | copy-start | bytes 772
  34.1 11.2 %collective-permute-start.1 = (bf16[16,8,128]{2,1,0:T(8,128)(2,1)S(1)}, bf16[16,8,128]{2,1,0:T(8,128)(2,1)S(1)}, u32[]{:S(2)}, u32[]{:S(2)}) collective-permute-start(bf16[16,8,128]{2,1,0:T(8,128)(2,1)S(1)} %get-tuple-element.16.tail_ref), channel_id=1, source_target_pairs={{0,1},{1,2},{2,3},{3,4},{4,5},{5,6},{6,7},{7,8},{8,9},{9,10},{10,1... | collective-permute-start | bytes 98312 | tf_op jit(solution)/shard_map/ppermute | solution.py:463
  36.0 9.7 %collective-permute-start.2 = (bf16[16,8,128]{2,1,0:T(8,128)(2,1)S(1)}, bf16[16,8,128]{2,1,0:T(8,128)(2,1)S(1)}, u32[]{:S(2)}, u32[]{:S(2)}) collective-permute-start(bf16[16,8,128]{2,1,0:T(8,128)(2,1)S(1)} %get-tuple-element.17.head_ref), channel_id=1, source_target_pairs={{1,0},{2,1},{3,2},{4,3},{5,4},{6,5},{7,6},{8,7},{9,8},{10,9},{11,1... | collective-permute-start | bytes 98312 | tf_op jit(solution)/shard_map/ppermute | solution.py:464

commit v5 on v4

v5 whole, which is shorter than its diff:
```python
import jax
import jax.numpy as jnp
from jax import lax
from jax.experimental import pallas as pl
from jax.experimental.pallas import tpu as pltpu
from jax.sharding import PartitionSpec as P

RB_SC = 4
BITS = 8
PILOTS = 2
FIRST = 1
EDGE = 8
PANEL = "panel"
SUB = "sc"


def lookup_matrix(lookup, rows):
    n, c = rows.shape
    member = lax.broadcasted_iota(jnp.int32, (n, n), 0) == lookup % n
    picked = lax.dot_general(
        member.astype(jnp.bfloat16), rows, (((0,), (0,)), ((), ())), preferred_element_type=jnp.float32
    ).astype(jnp.bfloat16)
    doubled = (
        lax.broadcasted_iota(jnp.int32, (2 * n, n), 0) // 2 == lax.broadcasted_iota(jnp.int32, (2 * n, n), 1)
    )
    w = jnp.dot(doubled.astype(jnp.bfloat16), picked, preferred_element_type=jnp.float32)
    lane = lax.broadcasted_iota(jnp.int32, w.shape, 1)
    turned = pltpu.roll(w, c // 2, 1) * jnp.where(lane < c // 2, -1.0, 1.0)
    odd = lax.broadcasted_iota(jnp.int32, w.shape, 0) % 2 == 1
    return jnp.where(odd, turned, w).astype(jnp.bfloat16)


def matrix_kernel_body(wave_ref, out_ref, blocks_ref, sems, matrix, parity):
    count, syms, subs, c = out_ref.shape
    k = wave_ref.shape[3]

    def fetch(i):
        return pltpu.make_async_copy(wave_ref.at[2 * i + parity], blocks_ref.at[i], sems.at[i])

    for i in range(count):
        fetch(i).start()
    weights = matrix()
    for first, last in ((0, count // 4), (count // 4, count)):
        for i in range(first, last):
            fetch(i).wait()
        lines = blocks_ref[first:last].reshape((last - first) * syms * subs, k)
        out_ref[first:last] = (
            jnp.dot(lines, weights, preferred_element_type=jnp.float32)
            .astype(jnp.bfloat16)
            .reshape(last - first, syms, subs, c)
        )


def given_kernel(lookup_ref, rows_ref, wave_ref, out_ref, matrix_ref, blocks_ref, lookup_buf, rows_buf, sems):
    count = out_ref.shape[0]
    copies = [
        pltpu.make_async_copy(lookup_ref, lookup_buf, sems.at[count]),
        pltpu.make_async_copy(rows_ref, rows_buf, sems.at[count + 1]),
    ]
    for copy in copies:
        copy.start()

    def matrix():
        for copy in copies:
            copy.wait()
        matrix_ref[...] = lookup_matrix(lookup_buf[...], rows_buf[...])
        return matrix_ref[...]

    parity = 1 - lax.axis_index(PANEL) % 2
    matrix_kernel_body(wave_ref, out_ref, blocks_ref, sems, matrix, parity)


def kept_kernel(
    matrix_ref, syms_ref, order_ref, pilot_ref, wave_ref, out_ref, chosen_ref, keep_ref, pilots_ref, blocks_ref, sems
):
    parity = lax.axis_index(PANEL) % 2
    matrix_kernel_body(wave_ref, out_ref, blocks_ref, sems, lambda: matrix_ref[...], parity)
    for i in range(PILOTS):
        at = jnp.broadcast_to(entry(syms_ref[...].astype(jnp.float32), i), chosen_ref.shape[1:])
        row = lax.broadcasted_iota(jnp.int32, chosen_ref.shape[1:], 0)
        chosen_ref[i] = jnp.where(row.astype(jnp.float32) == at, 1.0, 0.0)
    subs, bits = keep_ref.shape
    blocks = order_ref.shape[1]
    mine = lax.broadcasted_iota(jnp.int32, (subs, blocks), 0) // RB_SC == lax.broadcasted_iota(
        jnp.int32, (subs, blocks), 1
    )
    orders = jnp.broadcast_to(order_ref[...].astype(jnp.float32), (subs, blocks))
    limit = 2.0 * jnp.sum(jnp.where(mine, orders, 0.0), axis=1, keepdims=True)
    bit = lax.broadcasted_iota(jnp.int32, (subs, bits), 1) % BITS
    keep_ref[...] = jnp.where(bit.astype(jnp.float32) < limit, 1.0, 0.0)
    pilots_ref[0], pilots_ref[1] = signed_pilots(pilot_ref, pilots_ref.shape[2])


def beam_partials(wave, lookup, rows, pilot_syms, mod_order, pilot_values, bits):
    groups, syms, subs, k = wave.shape
    n, c = rows.shape
    half = groups // 2
    lookup, rows, wave = (
        pltpu.with_memory_space_constraint(array, pltpu.HBM) for array in (lookup.reshape(1, -1), rows, wave)
    )
    hbm = pl.BlockSpec(memory_space=pltpu.HBM)
    vmem = pl.BlockSpec(memory_space=pltpu.VMEM)
    params = pltpu.CompilerParams(vmem_limit_bytes=8 * 2**20)
    out = jax.ShapeDtypeStruct((half, syms, subs, c), jnp.bfloat16)
    blocks = pltpu.VMEM((half, syms, subs, k), jnp.bfloat16)
    given, matrix = pl.pallas_call(
        given_kernel,
        in_specs=[hbm] * 3,
        out_specs=[vmem] * 2,
        out_shape=[out, jax.ShapeDtypeStruct((k, c), jnp.bfloat16)],
        scratch_shapes=[
            blocks,
            pltpu.VMEM((1, n), jnp.int32),
            pltpu.VMEM((n, c), jnp.bfloat16),
            pltpu.SemaphoreType.DMA((half + 2,)),
        ],
        compiler_params=params,
        name="given",
    )(lookup, rows, wave)
    kept, *facts = pl.pallas_call(
        kept_kernel,
        in_specs=[vmem] * 4 + [hbm],
        out_specs=[vmem] * 4,
        out_shape=[
            out,
            jax.ShapeDtypeStruct((PILOTS, pl.cdiv(syms, 8) * 8, c), jnp.float32),
            jax.ShapeDtypeStruct((subs, bits), jnp.float32),
            jax.ShapeDtypeStruct((2, subs, c), jnp.float32),
        ],
        scratch_shapes=[blocks, pltpu.SemaphoreType.DMA((half,))],
        compiler_params=params,
        cost_estimate=pl.CostEstimate(
            flops=2 * half * syms * subs * k * c, bytes_accessed=2 * half * syms * subs * k, transcendentals=0
        ),
        name="kept",
    )(matrix, pilot_syms.reshape(1, -1), mod_order.reshape(1, -1), pilot_values, wave)
    return given, kept, facts


def entry(row, i):
    lane = lax.broadcasted_iota(jnp.int32, row.shape, 1)
    return jnp.sum(jnp.where(lane == i, row, 0.0), axis=1, keepdims=True)


def chosen_rows(chosen_ref, i, t, like):
    return jnp.broadcast_to(chosen_ref[i, t : t + 1, :], like.shape[-2:]) > 0.0


def as_column(row, count):
    diagonal = lax.broadcasted_iota(jnp.int32, (count, count), 0) == lax.broadcasted_iota(
        jnp.int32, (count, count), 1
    )
    return jnp.sum(jnp.where(diagonal, jnp.broadcast_to(row, (count, count)), 0.0), axis=1, keepdims=True)


def estimate_of(beams, pilot_re, pilot_im):
    c = beams.shape[-1]
    return beams * pilot_re + pltpu.roll(beams, c // 2, beams.ndim - 1) * pilot_im


def signed_pilots(pilot_ref, c):
    s = pilot_ref.shape[1]
    re = jnp.broadcast_to(as_column(pilot_ref[0:1, :], s), (s, c))
    im = jnp.broadcast_to(as_column(pilot_ref[1:2, :], s), (s, c))
    lane = lax.broadcasted_iota(jnp.int32, (s, c), 1)
    return re, jnp.where(lane < c // 2, im, -im)


def position():
    blocks = lax.axis_size(SUB)
    return lax.axis_index(PANEL) * blocks + lax.axis_index(SUB), lax.axis_size(PANEL) * blocks


def sum_kernel(chosen_ref, keep_ref, pilots_ref, parts_ref, *refs):
    *weights, own_ref, tail_ref, head_ref, llr_ref, patch_ref, wide_ref, even_ref, odd_ref = refs
    panels, syms, subs, c = parts_ref.shape

    def put(t, values):
        own_ref[t] = values
        head_ref[t] = values[:EDGE]
        tail_ref[t] = values[subs - EDGE :]

    at_pilots = [jnp.zeros((subs, c), jnp.float32) for _ in range(PILOTS)]
    for t in range(syms):
        total = parts_ref[0, t].astype(jnp.float32)
        for p in range(1, panels):
            total = total + parts_ref[p, t].astype(jnp.float32)
        beams = total.astype(jnp.bfloat16)
        put(t, beams)
        for i in range(PILOTS):
            at_pilots[i] = jnp.where(chosen_rows(chosen_ref, i, t, beams), beams.astype(jnp.float32), at_pilots[i])
    for i in range(PILOTS):
        put(syms + i, estimate_of(at_pilots[i], pilots_ref[0], pilots_ref[1]).astype(jnp.bfloat16))

    @pl.when(waits_long())
    def _():
        interior(chosen_ref, keep_ref, own_ref, *weights, llr_ref, patch_ref, wide_ref, even_ref, odd_ref)


def late_kernel(chosen_ref, keep_ref, own_ref, *refs):
    *weights, early_llr_ref, early_patch_ref, llr_ref, patch_ref, wide_ref, even_ref, odd_ref = refs
    del early_llr_ref, early_patch_ref

    @pl.when(jnp.logical_not(waits_long()))
    def _():
        interior(chosen_ref, keep_ref, own_ref, *weights, llr_ref, patch_ref, wide_ref, even_ref, odd_ref)


def waits_long():
    return lax.axis_index(SUB) < FIRST


def interior_shapes(syms, subs, c, layers, bits):
    return [
        jax.ShapeDtypeStruct((syms, subs, bits), jnp.float32),
        jax.ShapeDtypeStruct((layers - 1, syms, 2 * EDGE, c), jnp.float32),
    ]


def interior_scratch(syms, subs, c):
    padded = (syms + 2) * subs
    return [pltpu.VMEM((padded, lanes * c), jnp.bfloat16) for lanes in (2, 1, 1)]


def sum_beams(parts, facts, weights):
    _, syms, subs, c = parts.shape
    vmem = pl.BlockSpec(memory_space=pltpu.VMEM)
    edge = jax.ShapeDtypeStruct((syms + PILOTS, EDGE, c), jnp.bfloat16)
    layers, bits = weights[1].shape[0] + 1, weights[-1].shape[1]
    return pl.pallas_call(
        sum_kernel,
        in_specs=[vmem] * 10,
        out_specs=[vmem] * 5,
        out_shape=[
            jax.ShapeDtypeStruct((syms + PILOTS, subs, c), jnp.bfloat16),
            edge,
            edge,
            *interior_shapes(syms, subs, c, layers, bits),
        ],
        scratch_shapes=interior_scratch(syms, subs, c),
        compiler_params=pltpu.CompilerParams(vmem_limit_bytes=16 * 2**20),
        name="sum_beams",
    )(*facts, parts, *weights)


def pilot_rows(chosen_ref, rows, syms):
    spread = []
    for t in range(syms):
        row = jnp.zeros(rows.shape[1:], rows.dtype)
        for i in range(PILOTS):
            row = jnp.where(chosen_rows(chosen_ref, i, t, row), rows[i], row)
        spread.append(row)
    return jnp.stack(spread, 0)


def with_estimates(chosen_ref, pieces, syms):
    return jnp.concatenate([pieces[:syms], pilot_rows(chosen_ref, pieces[syms:], syms)], axis=2)


def taps_of(kernel, dt, dc):
    depth = kernel.shape[0] // 9
    return kernel[(3 * dt + dc) * depth : (3 * dt + dc + 1) * depth]


def demapped(field, in_ref, in_bias_ref, out_w_ref):
    hidden = jnp.dot(field, in_ref[...], preferred_element_type=jnp.float32)
    hidden = jnp.maximum(hidden + in_bias_ref[...], 0.0).astype(jnp.bfloat16)
    return jnp.dot(hidden, out_w_ref[...], preferred_element_type=jnp.float32)


def store_llr(ref, llr, keep, chosen_ref):
    rows = keep.shape[0]
    for t in range(ref.shape[0]):
        kept = keep > 0.0
        for i in range(PILOTS):
            kept = kept & jnp.logical_not(chosen_rows(chosen_ref, i, t, keep))
        ref[t] = jnp.where(kept, llr[t * rows : (t + 1) * rows], 0.0)


def interior(
    chosen_ref, keep_ref, own_ref, first_ref, rest_ref, bias_ref, in_ref, in_bias_ref, out_w_ref,
    llr_ref, patch_ref, wide_ref, even_ref, odd_ref,
):
    syms, subs, c = own_ref.shape
    syms = syms - PILOTS
    layers = rest_ref.shape[0] + 1
    rows = syms * subs
    for ref in (wide_ref, even_ref, odd_ref):
        ref[0:subs] = jnp.zeros((subs, ref.shape[1]), jnp.bfloat16)
        ref[subs + rows :] = jnp.zeros((subs, ref.shape[1]), jnp.bfloat16)
    wide_ref[subs : subs + rows, :c] = own_ref[:syms].reshape(rows, c)
    estimates = pilot_rows(chosen_ref, own_ref[syms:].astype(jnp.float32), syms)
    for t in range(syms):
        wide_ref[subs * (t + 1) : subs * (t + 2), c:] = estimates[t].astype(jnp.bfloat16)
    src = wide_ref
    for layer in range(1, layers + 1):
        kernel = first_ref[...] if layer == 1 else rest_ref[layer - 2]
        taps = jnp.concatenate([src[dt * subs : dt * subs + rows] for dt in range(3)], axis=1)
        wide = jnp.concatenate(
            [jnp.concatenate([taps_of(kernel, dt, dc) for dc in range(3)], axis=1) for dt in range(3)], axis=0
        )
        sums = jnp.dot(taps, wide, preferred_element_type=jnp.float32)
        total = sums[:, :c] + bias_ref[layer - 1 : layer, :]
        for dc in range(1, 3):
            total = total + pltpu.roll(sums[:, dc * c : (dc + 1) * c], rows - dc, 0)
        total = jnp.maximum(total, 0.0)
        if layer == layers:
            break
        src = (even_ref, odd_ref)[layer % 2]
        src[subs : subs + rows] = total.astype(jnp.bfloat16)
        spread = total.reshape(syms, subs, c)
        last = subs - 4 - 2 * layer
        group, place = last // EDGE * EDGE, last % EDGE
        high = spread[:, group : group + EDGE]
        if place != EDGE - 2:
            high = pltpu.roll(high, EDGE - 2 - place, 1)
        patch_ref[layer - 1] = jnp.concatenate([pltpu.roll(spread[:, :EDGE], EDGE - 2, 1), high], axis=1)
    final = pltpu.roll(total, layers, 0).astype(jnp.bfloat16)
    llr = demapped(final, in_ref, in_bias_ref, out_w_ref)
    store_llr(llr_ref, llr, keep_ref[...], chosen_ref)


def edge_kernel(
    chosen_ref, keep_ref, left_ref, right_ref, tail_ref, head_ref, patch_ref, inner_ref,
    first_ref, rest_ref, bias_ref, in_ref, in_bias_ref, out_w_ref,
    llr_ref, llr_buf, sems,
):
    syms, c = left_ref.shape[0] - PILOTS, left_ref.shape[2]
    layers = rest_ref.shape[0] + 1
    subs = llr_ref.shape[1]
    width = 2 * EDGE
    rows = syms * width
    middle = pl.ds(EDGE, subs - 2 * EDGE)
    inner_copy = pltpu.make_async_copy(inner_ref.at[:, middle], llr_ref.at[:, middle], sems.at[2])
    inner_copy.start()

    def joined(before, after, start):
        if start == 0:
            return before
        if start == EDGE:
            return after
        row = lax.broadcasted_iota(jnp.int32, before.shape, 1)
        turn = EDGE - start
        return jnp.where(row < turn, pltpu.roll(before, turn, 1), pltpu.roll(after, turn, 1))

    def convolved(shifted, kernel, bias):
        field = jnp.concatenate(shifted, axis=2)
        wide = jnp.concatenate(
            [jnp.concatenate([taps_of(kernel, dt, dc) for dt in range(3)], axis=1) for dc in range(3)], axis=0
        )
        sums = jnp.dot(
            field.reshape(rows, field.shape[2]).astype(jnp.bfloat16), wide, preferred_element_type=jnp.float32
        ).reshape(syms, width, 3 * c)
        nothing = jnp.zeros((1, width, c), jnp.float32)
        total = sums[:, :, c : 2 * c] + bias[None]
        total = total + jnp.concatenate([nothing, sums[:-1, :, :c]], axis=0)
        total = total + jnp.concatenate([sums[1:, :, 2 * c :], nothing], axis=0)
        return jnp.maximum(total, 0.0)

    at, blocks = position()
    left, right, tail, head = (ref[...].astype(jnp.float32) for ref in (left_ref, right_ref, tail_ref, head_ref))
    shifted = []
    for dc in range(3):
        low = joined(left, head, EDGE - layers + dc)
        high = joined(tail, right, EDGE - 4 + dc)
        shifted.append(with_estimates(chosen_ref, jnp.concatenate([low, high], axis=1), syms))
    total = convolved(shifted, first_ref[...], bias_ref[0:1, :])
    row = lax.broadcasted_iota(jnp.int32, (width, c), 0)
    for layer in range(1, layers):
        below = (row < layers - layer) & (at == 0)
        above = (row >= EDGE + 2 + layer) & (at == blocks - 1)
        total = jnp.where((below | above)[None], 0.0, total)
        patch = patch_ref[layer - 1]
        inner_low, inner_high = patch[:, :EDGE], patch[:, EDGE:]
        low, high = total[:, :EDGE], total[:, EDGE:]
        shifted = [
            jnp.concatenate([joined(low, inner_low, dc), joined(inner_high, high, EDGE - 2 + dc)], axis=1)
            for dc in range(3)
        ]
        total = convolved(shifted, rest_ref[layer - 1], bias_ref[layer : layer + 1, :])
    llr = demapped(total.reshape(rows, c).astype(jnp.bfloat16), in_ref, in_bias_ref, out_w_ref)
    keep = jnp.concatenate([keep_ref[:EDGE], keep_ref[subs - EDGE :]], axis=0)
    store_llr(llr_buf, llr, keep, chosen_ref)
    copies = [
        pltpu.make_async_copy(
            llr_buf.at[:, pl.ds(side * EDGE, EDGE)], llr_ref.at[:, pl.ds(start, EDGE)], sems.at[side]
        )
        for side, start in enumerate((0, subs - EDGE))
    ]
    for copy in copies:
        copy.start()
    inner_copy.wait()
    for copy in copies:
        copy.wait()


def receive_interior(facts, own, weights, early):
    syms, subs, c = own.shape
    syms = syms - PILOTS
    layers, bits = weights[1].shape[0] + 1, weights[-1].shape[1]
    vmem = pl.BlockSpec(memory_space=pltpu.VMEM)
    return pl.pallas_call(
        late_kernel,
        in_specs=[vmem] * 11,
        out_specs=[vmem] * 2,
        out_shape=interior_shapes(syms, subs, c, layers, bits),
        input_output_aliases={9: 0, 10: 1},
        scratch_shapes=interior_scratch(syms, subs, c),
        compiler_params=pltpu.CompilerParams(vmem_limit_bytes=16 * 2**20),
        cost_estimate=pl.CostEstimate(flops=10**9, bytes_accessed=4 * 10**6, transcendentals=0),
        name="interior",
    )(*facts[:2], own, *weights, *early)


def receive_edges(facts, got, sent, patch, weights, inner):
    syms, subs, bits = inner.shape
    vmem = pl.BlockSpec(memory_space=pltpu.VMEM)
    return pl.pallas_call(
        edge_kernel,
        in_specs=[vmem] * 14,
        out_specs=pl.BlockSpec(memory_space=pltpu.HBM),
        out_shape=pltpu.HBM(inner.shape, jnp.float32),
        scratch_shapes=[
            pltpu.VMEM((syms, 2 * EDGE, bits), jnp.float32),
            pltpu.SemaphoreType.DMA((3,)),
        ],
        compiler_params=pltpu.CompilerParams(vmem_limit_bytes=16 * 2**20),
        cost_estimate=pl.CostEstimate(flops=5 * 10**8, bytes_accessed=4 * 10**6, transcendentals=0),
        name="edges",
    )(*facts[:2], *got, *sent, patch, inner, *weights)


def per_device(
    captured_waveform,
    element_lookup,
    combiner,
    pilot_syms,
    pilot_values,
    mod_order,
    conv_first,
    conv_rest,
    conv_bias,
    demap_in,
    demap_bias,
    demap_out,
):
    given, kept, facts = beam_partials(
        captured_waveform, element_lookup, combiner, pilot_syms, mod_order, pilot_values, demap_out.shape[1]
    )
    panels = lax.axis_size(PANEL)
    got = lax.ppermute(given, PANEL, [(p, p ^ 1) for p in range(panels)])
    pairs = (kept.astype(jnp.float32) + got.astype(jnp.float32)).astype(jnp.bfloat16)
    same_core = [list(range(core, panels, 2)) for core in range(2)]
    parts = lax.all_to_all(pairs, PANEL, 0, 0, axis_index_groups=same_core, tiled=True)
    c = combiner.shape[1]
    weights = (
        conv_first.reshape(-1, c),
        conv_rest.reshape(conv_rest.shape[0], -1, c),
        conv_bias,
        demap_in,
        demap_bias.reshape(1, -1),
        demap_out,
    )
    own, tail, head, *early = sum_beams(parts, facts, weights)
    both = (PANEL, SUB)
    count = lax.axis_size(both)
    left = lax.ppermute(tail, both, [(i, i + 1) for i in range(count - 1)])
    right = lax.ppermute(head, both, [(i + 1, i) for i in range(count - 1)])
    inner, patch = receive_interior(facts, own, weights, early)
    return receive_edges(facts, (left, right), (tail, head), patch, weights, inner)


def solution(mesh):
    in_specs = (
        P(None, None, SUB, PANEL),
        P(PANEL),
        P(PANEL, None),
        P(),
        P(None, (PANEL, SUB)),
        P((PANEL, SUB)),
        P(),
        P(),
        P(),
        P(),
        P(),
        P(),
    )
    out_specs = P(None, (PANEL, SUB), None)
    return jax.shard_map(
        per_device, mesh=mesh, in_specs=in_specs, out_specs=out_specs, check_vma=False
    )
```

time: 49.4 us -> 47.7 us (0.966)
  Pallas kernels: 12.5 us -> 9.56 us
  starting transfers between devices: 19.4 us -> 20.1 us
  waiting for transfers between devices: 0.43 us -> 0.97 us
    pallas_call x4, Pallas kernels: 10.2 us -> 7.19 us  [the longest x1 2.62 us: sum_beams(): pl.pallas_call(sum_kernel, in_specs=[vmem] * 10, out_specs=[vmem] * 5, ou...]
    ppermute x1, starting transfers between devices: 8.67 us -> 9.41 us  [per_device(): right = lax.ppermute(head, both, [(i + 1, i) for i in range(count - 1)])]
    ppermute x1, waiting for transfers between devices: 0.43 us -> 0.97 us  [per_device(): right = lax.ppermute(head, both, [(i + 1, i) for i in range(count - 1)])]
  transfers between devices with their start and end apart: 3 -> 3, of which waited for: 1 -> 1; matrix products, arithmetic and copies ran while one was open for 0% -> 0% of each run, Pallas kernels for 6% -> 5%
where the time goes in v5:
time: 47.7 us; the launch traced here: 47.4 us
  starting transfers between devices  20.1 us (42%)
  blocking collectives  16.3 us (34%)
  Pallas kernels  9.56 us (20%)
  waiting for transfers between devices  0.97 us (2%)
    all_to_all x1, blocking collectives, per_device(): lax.all_to_all(pairs, PANEL, 0, 0, axis_index_groups=same_core, tiled=True)  16.3 us
    ppermute x1, starting transfers between devices, per_device(): right = lax.ppermute(head, both, [(i + 1, i) for i in range(count - 1)])  9.41 us
    ppermute x1, starting transfers between devices, per_device(): got = lax.ppermute(given, PANEL, [(p, p ^ 1) for p in range(panels)])  8.79 us
    pallas_call x1, Pallas kernels, sum_beams(): pl.pallas_call(sum_kernel, in_specs=[vmem] * 10, out_specs=[vmem] * 5, ou...  2.62 us
    pallas_call x1, Pallas kernels, beam_partials(): pl.pallas_call(given_kernel, in_specs=[hbm] * 3, out_specs=[vmem] * 2, ou...  2.36 us
    pallas_call x1, Pallas kernels, receive_edges(): pl.pallas_call(edge_kernel, in_specs=[vmem] * 14, out_specs=pl.BlockSpec(...  2.29 us
    pallas_call x1, Pallas kernels, beam_partials(): pl.pallas_call(kept_kernel, in_specs=[vmem] * 4 + [hbm], out_specs=[vmem]...  2.27 us
    ppermute x1, starting transfers between devices, per_device(): left = lax.ppermute(tail, both, [(i, i + 1) for i in range(count - 1)])  1.92 us
  transfers between devices with their start and end apart: 3, of which 1 were waited for; matrix products, arithmetic and copies ran while one was open for 0% of the time, Pallas kernels for 5%

profile of v5, /device:TPU:1, one launch (start us, length us, event | category | flops | bytes accessed | tf_op | source)
XLA Modules:
  0.0 47.4 jit_solution(15373153929809863303)
XLA Ops:
  0.0 0.0 copy-start.6
  0.0 0.0 copy-start.7
  0.0 0.0 copy-start.8
  0.0 2.4 %given.1 = (bf16[8,14,32,128]{3,2,1,0:T(8,128)(2,1)S(1)}, bf16[256,128]{1,0:T(8,128)(2,1)S(1)}) custom-call(s32[1,128]{1,0:T(1,128)} %bitcast.17, bf16[128,128]{1,0:T(8,128)(2,1)} %rows_ref.1, bf16[16,14,32,256]{3,2,1,0:T(8,128)(2,1)} %wave_ref.3), custom_call_target="tpu_custom_call" | custom-call | tf_op jit(solution)/shard_map/given/pallas_call | solution.py:106
  2.4 8.8 %collective-permute-start = (bf16[8,14,32,128]{3,2,1,0:T(8,128)(2,1)S(1)}, bf16[8,14,32,128]{3,2,1,0:T(8,128)(2,1)S(1)}, u32[]{:S(2)}, u32[]{:S(2)}) collective-permute-start(bf16[8,14,32,128]{3,2,1,0:T(8,128)(2,1)S(1)} %get-tuple-element.23), channel_id=1, source_target_pairs={{0,32},{32,0},{64,96},{96,64},{128,160},{160,128},{192,224},{224,1... | collective-permute-start | bytes 2752520 | tf_op jit(solution)/shard_map/ppermute | solution.py:451
  11.2 0.0 copy-done.6
  11.2 0.0 copy-done.7
  11.2 0.0 copy-done.8
  11.2 2.3 %kept.1 = (bf16[8,14,32,128]{3,2,1,0:T(8,128)(2,1)S(1)}, f32[2,16,128]{2,1,0:T(8,128)S(1)}, f32[32,128]{1,0:T(8,128)S(1)}, f32[2,32,128]{2,1,0:T(8,128)S(1)}) custom-call(bf16[256,128]{1,0:T(8,128)(2,1)S(1)} %get-tuple-element.18.matrix_ref, s32[1,2]{1,0:T(1,128)S(1)} %bitcast.15, s32[1,8]{1,0:T(1,128)S(1)} %bitcast.16, f32[2,32]{1,0:T(2,128)S(1)} %copy-done.6, ...), custom_call_target="tpu_custom_call" | custom-call | flops 234881024 | bytes 1835008 | tf_op jit(solution)/shard_map/kept/pallas_call | solution.py:120
  13.5 0.0 collective-permute-done
  13.5 0.0 copy-start
  13.5 0.0 copy-start.1
  13.5 0.0 copy-start.2
  13.5 0.0 copy-start.3
  13.5 0.0 copy-start.4
  13.5 0.0 copy-start.5
  13.6 0.2 add_convert_fusion
  13.8 16.3 %all_to_all.5.parts_ref = bf16[8,14,32,128]{3,2,1,0:T(8,128)(2,1)S(1)} all-to-all(bf16[8,14,32,128]{3,2,1,0:T(8,128)(2,1)S(1)} %add_convert_fusion), channel_id=1, replica_groups={{0,64,128,192,256,320,384,448},{32,96,160,224,288,352,416,480},{1,65,12..., dimensions={0} | all-to-all | bytes 1835008 | tf_op jit(solution)/shard_map/all_to_all | solution.py:454
  30.1 0.0 copy-done
  30.1 0.0 copy-done.1
  30.1 0.0 copy-done.2
  30.1 0.0 copy-done.3
  30.1 0.0 copy-done.4
  30.1 0.0 copy-done.5
  30.1 2.6 %sum_beams.1 = (bf16[16,32,128]{2,1,0:T(8,128)(2,1)S(1)}, bf16[16,8,128]{2,1,0:T(8,128)(2,1)S(1)}, bf16[16,8,128]{2,1,0:T(8,128)(2,1)S(1)}, f32[14,32,128]{2,1,0:T(8,128)S(1)}, f32[5,14,16,128]{3,2,1,0:T(8,128)S(1)}) custom-call(f32[2,16,128]{2,1,0:T(8,128)S(1)} %get-tuple-element.19.chosen_ref, f32[32,128]{1,0:T(8,128)S(1)} %get-tuple-element.20.keep_ref, ...), custom_call_target="tpu_custom_call" | custom-call | tf_op jit(solution)/shard_map/sum_beams/pallas_call | solution.py:230
  32.8 1.9 %collective-permute-start.1 = (bf16[16,8,128]{2,1,0:T(8,128)(2,1)S(1)}, bf16[16,8,128]{2,1,0:T(8,128)(2,1)S(1)}, u32[]{:S(2)}, u32[]{:S(2)}) collective-permute-start(bf16[16,8,128]{2,1,0:T(8,128)(2,1)S(1)} %get-tuple-element.24.tail_ref), channel_id=1, source_target_pairs={{0,1},{1,2},{2,3},{3,4},{4,5},{5,6},{6,7},{7,8},{8,9},{9,10},{10,1... | collective-permute-start | bytes 98312 | tf_op jit(solution)/shard_map/ppermute | solution.py:467
  34.7 9.4 %collective-permute-start.2 = (bf16[16,8,128]{2,1,0:T(8,128)(2,1)S(1)}, bf16[16,8,128]{2,1,0:T(8,128)(2,1)S(1)}, u32[]{:S(2)}, u32[]{:S(2)}) collective-permute-start(bf16[16,8,128]{2,1,0:T(8,128)(2,1)S(1)} %get-tuple-element.25.head_ref), channel_id=1, source_target_pairs={{1,0},{2,1},{3,2},{4,3},{5,4},{6,5},{7,6},{8,7},{9,8},{10,9},{11,1... | collective-permute-start | bytes 98312 | tf_op jit(solution)/shard_map/ppermute | solution.py:468
  44.1 0.0 collective-permute-done.1.left_ref
  44.2 1.0 %collective-permute-done.2.right_ref = bf16[16,8,128]{2,1,0:T(8,128)(2,1)S(1)} collective-permute-done((bf16[16,8,128]{2,1,0:T(8,128)(2,1)S(1)}, bf16[16,8,128]{2,1,0:T(8,128)(2,1)S(1)}, u32[]{:S(2)}, u32[]{:S(2)}) %collective-permute-start.2) | collective-permute-done | bytes 32800 | tf_op jit(solution)/shard_map/ppermute | solution.py:468
  45.1 2.3 %edges.1 = f32[14,32,128]{2,1,0:T(8,128)} custom-call(f32[2,16,128]{2,1,0:T(8,128)S(1)} %get-tuple-element.19.chosen_ref, f32[32,128]{1,0:T(8,128)S(1)} %get-tuple-element.20.keep_ref, bf16[16,8,128]{2,1,0:T(8,128)(2,1)S(1)} %collective-permute-done.1.left_ref, bf16[16,8,128]{2,1,0:T(8,128)(2,1)S(1)} %collective-permute-done.2.right_ref, ...), custom_call_target="tpu_custom_call" | custom-call | flops 500000000 | bytes 4000000 | tf_op jit(solution)/shard_map/edges/pallas_call | solution.py:418
  (1 shorter events, 0.0 us)
Async XLA Ops:
  0.0 11.2 %copy-start.6 = (f32[2,32]{1,0:T(2,128)S(1)}, f32[2,32]{1,0:T(2,128)}, u32[]{:S(2)}) copy-start(f32[2,32]{1,0:T(2,128)} %pilot_ref.1) | copy-start | bytes 772
  0.0 11.2 %copy-start.7 = (s32[2]{0:T(128)S(1)}, s32[2]{0:T(128)}, u32[]{:S(2)}) copy-start(s32[2]{0:T(128)} %param.15) | copy-start | bytes 28
  0.0 11.2 %copy-start.8 = (s32[8]{0:T(128)S(1)}, s32[8]{0:T(128)}, u32[]{:S(2)}) copy-start(s32[8]{0:T(128)} %param.17) | copy-start | bytes 100
  2.4 11.1 %collective-permute-start = (bf16[8,14,32,128]{3,2,1,0:T(8,128)(2,1)S(1)}, bf16[8,14,32,128]{3,2,1,0:T(8,128)(2,1)S(1)}, u32[]{:S(2)}, u32[]{:S(2)}) collective-permute-start(bf16[8,14,32,128]{3,2,1,0:T(8,128)(2,1)S(1)} %get-tuple-element.23), channel_id=1, source_target_pairs={{0,32},{32,0},{64,96},{96,64},{128,160},{160,128},{192,224},{224,1... | collective-permute-start | bytes 2752520 | tf_op jit(solution)/shard_map/ppermute | solution.py:451
  13.5 16.6 %copy-start = (bf16[5,3,3,128,128]{4,3,2,1,0:T(8,128)(2,1)S(1)}, bf16[5,3,3,128,128]{4,3,2,1,0:T(8,128)(2,1)}, u32[]{:S(2)}) copy-start(bf16[5,3,3,128,128]{4,3,2,1,0:T(8,128)(2,1)} %param.19) | copy-start | bytes 4423684
  13.5 16.6 %copy-start.1 = (bf16[3,3,256,128]{3,2,1,0:T(8,128)(2,1)S(1)}, bf16[3,3,256,128]{3,2,1,0:T(8,128)(2,1)}, u32[]{:S(2)}) copy-start(bf16[3,3,256,128]{3,2,1,0:T(8,128)(2,1)} %param.18) | copy-start | bytes 1769476
  13.5 16.6 %copy-start.2 = (bf16[128,256]{1,0:T(8,128)(2,1)S(1)}, bf16[128,256]{1,0:T(8,128)(2,1)}, u32[]{:S(2)}) copy-start(bf16[128,256]{1,0:T(8,128)(2,1)} %in_ref.1) | copy-start | bytes 196612
  13.5 16.6 %copy-start.3 = (bf16[256,128]{1,0:T(8,128)(2,1)S(1)}, bf16[256,128]{1,0:T(8,128)(2,1)}, u32[]{:S(2)}) copy-start(bf16[256,128]{1,0:T(8,128)(2,1)} %out_w_ref.1) | copy-start | bytes 196612
  13.5 16.6 %copy-start.4 = (f32[6,128]{1,0:T(8,128)S(1)}, f32[6,128]{1,0:T(8,128)}, u32[]{:S(2)}) copy-start(f32[6,128]{1,0:T(8,128)} %bias_ref.1) | copy-start | bytes 9220
  13.5 16.6 %copy-start.5 = (f32[256]{0:T(256)S(1)}, f32[256]{0:T(256)}, u32[]{:S(2)}) copy-start(f32[256]{0:T(256)} %param.22) | copy-start | bytes 3076
  32.8 11.4 %collective-permute-start.1 = (bf16[16,8,128]{2,1,0:T(8,128)(2,1)S(1)}, bf16[16,8,128]{2,1,0:T(8,128)(2,1)S(1)}, u32[]{:S(2)}, u32[]{:S(2)}) collective-permute-start(bf16[16,8,128]{2,1,0:T(8,128)(2,1)S(1)} %get-tuple-element.24.tail_ref), channel_id=1, source_target_pairs={{0,1},{1,2},{2,3},{3,4},{4,5},{5,6},{6,7},{7,8},{8,9},{9,10},{10,1... | collective-permute-start | bytes 98312 | tf_op jit(solution)/shard_map/ppermute | solution.py:467
  34.7 10.4 %collective-permute-start.2 = (bf16[16,8,128]{2,1,0:T(8,128)(2,1)S(1)}, bf16[16,8,128]{2,1,0:T(8,128)(2,1)S(1)}, u32[]{:S(2)}, u32[]{:S(2)}) collective-permute-start(bf16[16,8,128]{2,1,0:T(8,128)(2,1)S(1)} %get-tuple-element.25.head_ref), channel_id=1, source_target_pairs={{1,0},{2,1},{3,2},{4,3},{5,4},{6,5},{7,6},{8,7},{9,8},{10,9},{11,1... | collective-permute-start | bytes 98312 | tf_op jit(solution)/shard_map/ppermute | solution.py:468

commit v6 on v5

--- a/solution.py
+++ b/solution.py
@@ -8,6 +8,7 @@
 RB_SC = 4
 BITS = 8
 PILOTS = 2
+COPIES = 4
 FIRST = 1
 EDGE = 8
 PANEL = "panel"
@@ -32,16 +33,18 @@
 
 def matrix_kernel_body(wave_ref, out_ref, blocks_ref, sems, matrix, parity):
     count, syms, subs, c = out_ref.shape
-    k = wave_ref.shape[3]
+    k = wave_ref.shape[4]
+    step = count // COPIES
 
     def fetch(i):
-        return pltpu.make_async_copy(wave_ref.at[2 * i + parity], blocks_ref.at[i], sems.at[i])
-
-    for i in range(count):
+        some = pl.ds(i * step, step)
+        return pltpu.make_async_copy(wave_ref.at[some, parity], blocks_ref.at[some], sems.at[i])
+
+    for i in range(COPIES):
         fetch(i).start()
     weights = matrix()
-    for first, last in ((0, count // 4), (count // 4, count)):
-        for i in range(first, last):
+    for first, last in ((0, step), (step, count)):
+        for i in range(first // step, last // step):
             fetch(i).wait()
         lines = blocks_ref[first:last].reshape((last - first) * syms * subs, k)
         out_ref[first:last] = (
@@ -52,10 +55,9 @@
 
 
 def given_kernel(lookup_ref, rows_ref, wave_ref, out_ref, matrix_ref, blocks_ref, lookup_buf, rows_buf, sems):
-    count = out_ref.shape[0]
     copies = [
-        pltpu.make_async_copy(lookup_ref, lookup_buf, sems.at[count]),
-        pltpu.make_async_copy(rows_ref, rows_buf, sems.at[count + 1]),
+        pltpu.make_async_copy(lookup_ref, lookup_buf, sems.at[COPIES]),
+        pltpu.make_async_copy(rows_ref, rows_buf, sems.at[COPIES + 1]),
     ]
     for copy in copies:
         copy.start()
@@ -73,22 +75,25 @@
 def kept_kernel(
     matrix_ref, syms_ref, order_ref, pilot_ref, wave_ref, out_ref, chosen_ref, keep_ref, pilots_ref, blocks_ref, sems
 ):
+    def matrix():
+        for i in range(PILOTS):
+            at = jnp.broadcast_to(entry(syms_ref[...].astype(jnp.float32), i), chosen_ref.shape[1:])
+            row = lax.broadcasted_iota(jnp.int32, chosen_ref.shape[1:], 0)
+            chosen_ref[i] = jnp.where(row.astype(jnp.float32) == at, 1.0, 0.0)
+        subs, bits = keep_ref.shape
+        blocks = order_ref.shape[1]
+        mine = lax.broadcasted_iota(jnp.int32, (subs, blocks), 0) // RB_SC == lax.broadcasted_iota(
+            jnp.int32, (subs, blocks), 1
+        )
+        orders = jnp.broadcast_to(order_ref[...].astype(jnp.float32), (subs, blocks))
+        limit = 2.0 * jnp.sum(jnp.where(mine, orders, 0.0), axis=1, keepdims=True)
+        bit = lax.broadcasted_iota(jnp.int32, (subs, bits), 1) % BITS
+        keep_ref[...] = jnp.where(bit.astype(jnp.float32) < limit, 1.0, 0.0)
+        pilots_ref[0], pilots_ref[1] = signed_pilots(pilot_ref, pilots_ref.shape[2])
+        return matrix_ref[...]
+
     parity = lax.axis_index(PANEL) % 2
-    matrix_kernel_body(wave_ref, out_ref, blocks_ref, sems, lambda: matrix_ref[...], parity)
-    for i in range(PILOTS):
-        at = jnp.broadcast_to(entry(syms_ref[...].astype(jnp.float32), i), chosen_ref.shape[1:])
-        row = lax.broadcasted_iota(jnp.int32, chosen_ref.shape[1:], 0)
-        chosen_ref[i] = jnp.where(row.astype(jnp.float32) == at, 1.0, 0.0)
-    subs, bits = keep_ref.shape
-    blocks = order_ref.shape[1]
-    mine = lax.broadcasted_iota(jnp.int32, (subs, blocks), 0) // RB_SC == lax.broadcasted_iota(
-        jnp.int32, (subs, blocks), 1
-    )
-    orders = jnp.broadcast_to(order_ref[...].astype(jnp.float32), (subs, blocks))
-    limit = 2.0 * jnp.sum(jnp.where(mine, orders, 0.0), axis=1, keepdims=True)
-    bit = lax.broadcasted_iota(jnp.int32, (subs, bits), 1) % BITS
-    keep_ref[...] = jnp.where(bit.astype(jnp.float32) < limit, 1.0, 0.0)
-    pilots_ref[0], pilots_ref[1] = signed_pilots(pilot_ref, pilots_ref.shape[2])
+    matrix_kernel_body(wave_ref, out_ref, blocks_ref, sems, matrix, parity)
 
 
 def beam_partials(wave, lookup, rows, pilot_syms, mod_order, pilot_values, bits):
@@ -96,7 +101,8 @@
     n, c = rows.shape
     half = groups // 2
     lookup, rows, wave = (
-        pltpu.with_memory_space_constraint(array, pltpu.HBM) for array in (lookup.reshape(1, -1), rows, wave)
+        pltpu.with_memory_space_constraint(array, pltpu.HBM)
+        for array in (lookup.reshape(1, -1), rows, wave.reshape(half, 2, syms, subs, k))
     )
     hbm = pl.BlockSpec(memory_space=pltpu.HBM)
     vmem = pl.BlockSpec(memory_space=pltpu.VMEM)
@@ -112,7 +118,7 @@
             blocks,
             pltpu.VMEM((1, n), jnp.int32),
             pltpu.VMEM((n, c), jnp.bfloat16),
-            pltpu.SemaphoreType.DMA((half + 2,)),
+            pltpu.SemaphoreType.DMA((COPIES + 2,)),
         ],
         compiler_params=params,
         name="given",
@@ -127,7 +133,7 @@
             jax.ShapeDtypeStruct((subs, bits), jnp.float32),
             jax.ShapeDtypeStruct((2, subs, c), jnp.float32),
         ],
-        scratch_shapes=[blocks, pltpu.SemaphoreType.DMA((half,))],
+        scratch_shapes=[blocks, pltpu.SemaphoreType.DMA((COPIES,))],
         compiler_params=params,
         cost_estimate=pl.CostEstimate(
             flops=2 * half * syms * subs * k * c, bytes_accessed=2 * half * syms * subs * k, transcendentals=0
@@ -349,9 +355,9 @@
             [jnp.concatenate([taps_of(kernel, dt, dc) for dt in range(3)], axis=1) for dc in range(3)], axis=0
         )
         sums = jnp.dot(
-            field.reshape(rows, field.shape[2]).astype(jnp.bfloat16), wide, preferred_element_type=jnp.float32
-        ).reshape(syms, width, 3 * c)
-        nothing = jnp.zeros((1, width, c), jnp.float32)
+            field.reshape(syms * EDGE, field.shape[2]).astype(jnp.bfloat16), wide, preferred_element_type=jnp.float32
+        ).reshape(syms, EDGE, 3 * c)
+        nothing = jnp.zeros((1, EDGE, c), jnp.float32)
         total = sums[:, :, c : 2 * c] + bias[None]
         total = total + jnp.concatenate([nothing, sums[:-1, :, :c]], axis=0)
         total = total + jnp.concatenate([sums[1:, :, 2 * c :], nothing], axis=0)
@@ -359,25 +365,22 @@
 
     at, blocks = position()
     left, right, tail, head = (ref[...].astype(jnp.float32) for ref in (left_ref, right_ref, tail_ref, head_ref))
-    shifted = []
-    for dc in range(3):
-        low = joined(left, head, EDGE - layers + dc)
-        high = joined(tail, right, EDGE - 4 + dc)
-        shifted.append(with_estimates(chosen_ref, jnp.concatenate([low, high], axis=1), syms))
-    total = convolved(shifted, first_ref[...], bias_ref[0:1, :])
-    row = lax.broadcasted_iota(jnp.int32, (width, c), 0)
+    fields = [
+        [with_estimates(chosen_ref, joined(*ends, start + dc), syms) for dc in range(3)]
+        for ends, start in (((left, head), EDGE - layers), ((tail, right), EDGE - 4))
+    ]
+    low, high = (convolved(field, first_ref[...], bias_ref[0:1, :]) for field in fields)
+    row = lax.broadcasted_iota(jnp.int32, (EDGE, c), 0)
     for layer in range(1, layers):
-        below = (row < layers - layer) & (at == 0)
-        above = (row >= EDGE + 2 + layer) & (at == blocks - 1)
-        total = jnp.where((below | above)[None], 0.0, total)
+        low = jnp.where(((row < layers - layer) & (at == 0))[None], 0.0, low)
+        high = jnp.where(((row >= 2 + layer) & (at == blocks - 1))[None], 0.0, high)
         patch = patch_ref[layer - 1]
-        inner_low, inner_high = patch[:, :EDGE], patch[:, EDGE:]
-        low, high = total[:, :EDGE], total[:, EDGE:]
-        shifted = [
-            jnp.concatenate([joined(low, inner_low, dc), joined(inner_high, high, EDGE - 2 + dc)], axis=1)
-            for dc in range(3)
+        fields = [
+            [joined(low, patch[:, :EDGE], dc) for dc in range(3)],
+            [joined(patch[:, EDGE:], high, EDGE - 2 + dc) for dc in range(3)],
         ]
-        total = convolved(shifted, rest_ref[layer - 1], bias_ref[layer : layer + 1, :])
+        low, high = (convolved(field, rest_ref[layer - 1], bias_ref[layer : layer + 1, :]) for field in fields)
+    total = jnp.concatenate([low, high], axis=1)
     llr = demapped(total.reshape(rows, c).astype(jnp.bfloat16), in_ref, in_bias_ref, out_w_ref)
     keep = jnp.concatenate([keep_ref[:EDGE], keep_ref[subs - EDGE :]], axis=0)
     store_llr(llr_buf, llr, keep, chosen_ref)

time: 47.7 us -> 47.3 us (level)
  no operation moved by 1% of the time
where the time goes in v6:
time: 47.3 us; the launch traced here: 47.1 us
  starting transfers between devices  20.3 us (43%)
  blocking collectives  16.1 us (34%)
  Pallas kernels  9.26 us (20%)
  waiting for transfers between devices  0.97 us (2%)
    all_to_all x1, blocking collectives, per_device(): lax.all_to_all(pairs, PANEL, 0, 0, axis_index_groups=same_core, tiled=True)  16.1 us
    ppermute x1, starting transfers between devices, per_device(): right = lax.ppermute(head, both, [(i + 1, i) for i in range(count - 1)])  9.62 us
    ppermute x1, starting transfers between devices, per_device(): got = lax.ppermute(given, PANEL, [(p, p ^ 1) for p in range(panels)])  8.79 us
    pallas_call x1, Pallas kernels, sum_beams(): pl.pallas_call(sum_kernel, in_specs=[vmem] * 10, out_specs=[vmem] * 5, ou...  2.62 us
    pallas_call x1, Pallas kernels, beam_partials(): pl.pallas_call(given_kernel, in_specs=[hbm] * 3, out_specs=[vmem] * 2, ou...  2.32 us
    pallas_call x1, Pallas kernels, receive_edges(): pl.pallas_call(edge_kernel, in_specs=[vmem] * 14, out_specs=pl.BlockSpec(...  2.2 us
    pallas_call x1, Pallas kernels, beam_partials(): pl.pallas_call(kept_kernel, in_specs=[vmem] * 4 + [hbm], out_specs=[vmem]...  2.11 us
    ppermute x1, starting transfers between devices, per_device(): left = lax.ppermute(tail, both, [(i, i + 1) for i in range(count - 1)])  1.92 us
  transfers between devices with their start and end apart: 3, of which 1 were waited for; matrix products, arithmetic and copies ran while one was open for 0% of the time, Pallas kernels for 5%

profile of v6, /device:TPU:1, one launch (start us, length us, event | category | flops | bytes accessed | tf_op | source)
XLA Modules:
  0.0 47.1 jit_solution(191159602957667278)
XLA Ops:
  0.0 0.0 copy-start.6
  0.0 0.0 copy-start.7
  0.0 0.0 copy-start.8
  0.0 2.3 %given.1 = (bf16[8,14,32,128]{3,2,1,0:T(8,128)(2,1)S(1)}, bf16[256,128]{1,0:T(8,128)(2,1)S(1)}) custom-call(s32[1,128]{1,0:T(1,128)} %bitcast.20, bf16[128,128]{1,0:T(8,128)(2,1)} %rows_ref.1, bf16[8,2,14,32,256]{4,3,2,1,0:T(8,128)(2,1)} %bitcast.18), custom_call_target="tpu_custom_call" | custom-call | tf_op jit(solution)/shard_map/given/pallas_call | solution.py:112
  2.3 8.8 %collective-permute-start = (bf16[8,14,32,128]{3,2,1,0:T(8,128)(2,1)S(1)}, bf16[8,14,32,128]{3,2,1,0:T(8,128)(2,1)S(1)}, u32[]{:S(2)}, u32[]{:S(2)}) collective-permute-start(bf16[8,14,32,128]{3,2,1,0:T(8,128)(2,1)S(1)} %get-tuple-element.23), channel_id=1, source_target_pairs={{0,32},{32,0},{64,96},{96,64},{128,160},{160,128},{192,224},{224,1... | collective-permute-start | bytes 2752520 | tf_op jit(solution)/shard_map/ppermute | solution.py:454
  11.1 0.0 copy-done.6
  11.1 0.0 copy-done.7
  11.2 0.0 copy-done.8
  11.2 2.1 %kept.1 = (bf16[8,14,32,128]{3,2,1,0:T(8,128)(2,1)S(1)}, f32[2,16,128]{2,1,0:T(8,128)S(1)}, f32[32,128]{1,0:T(8,128)S(1)}, f32[2,32,128]{2,1,0:T(8,128)S(1)}) custom-call(bf16[256,128]{1,0:T(8,128)(2,1)S(1)} %get-tuple-element.18.matrix_ref, s32[1,2]{1,0:T(1,128)S(1)} %bitcast.16, s32[1,8]{1,0:T(1,128)S(1)} %bitcast.17, f32[2,32]{1,0:T(2,128)S(1)} %copy-done.6, ...), custom_call_target="tpu_custom_call" | custom-call | flops 234881024 | bytes 1835008 | tf_op jit(solution)/shard_map/kept/pallas_call | solution.py:126
  13.3 0.0 collective-permute-done
  13.3 0.0 copy-start
  13.3 0.0 copy-start.1
  13.3 0.0 copy-start.2
  13.3 0.0 copy-start.3
  13.3 0.0 copy-start.4
  13.3 0.0 copy-start.5
  13.4 0.2 add_convert_fusion
  13.6 16.1 %all_to_all.5.parts_ref = bf16[8,14,32,128]{3,2,1,0:T(8,128)(2,1)S(1)} all-to-all(bf16[8,14,32,128]{3,2,1,0:T(8,128)(2,1)S(1)} %add_convert_fusion), channel_id=1, replica_groups={{0,64,128,192,256,320,384,448},{32,96,160,224,288,352,416,480},{1,65,12..., dimensions={0} | all-to-all | bytes 1835008 | tf_op jit(solution)/shard_map/all_to_all | solution.py:457
  29.7 0.0 copy-done
  29.7 0.0 copy-done.1
  29.7 0.0 copy-done.2
  29.7 0.0 copy-done.3
  29.7 0.0 copy-done.4
  29.7 0.0 copy-done.5
  29.7 2.6 %sum_beams.1 = (bf16[16,32,128]{2,1,0:T(8,128)(2,1)S(1)}, bf16[16,8,128]{2,1,0:T(8,128)(2,1)S(1)}, bf16[16,8,128]{2,1,0:T(8,128)(2,1)S(1)}, f32[14,32,128]{2,1,0:T(8,128)S(1)}, f32[5,14,16,128]{3,2,1,0:T(8,128)S(1)}) custom-call(f32[2,16,128]{2,1,0:T(8,128)S(1)} %get-tuple-element.19.chosen_ref, f32[32,128]{1,0:T(8,128)S(1)} %get-tuple-element.20.keep_ref, ...), custom_call_target="tpu_custom_call" | custom-call | tf_op jit(solution)/shard_map/sum_beams/pallas_call | solution.py:236
  32.3 1.9 %collective-permute-start.1 = (bf16[16,8,128]{2,1,0:T(8,128)(2,1)S(1)}, bf16[16,8,128]{2,1,0:T(8,128)(2,1)S(1)}, u32[]{:S(2)}, u32[]{:S(2)}) collective-permute-start(bf16[16,8,128]{2,1,0:T(8,128)(2,1)S(1)} %get-tuple-element.24.tail_ref), channel_id=1, source_target_pairs={{0,1},{1,2},{2,3},{3,4},{4,5},{5,6},{6,7},{7,8},{8,9},{9,10},{10,1... | collective-permute-start | bytes 98312 | tf_op jit(solution)/shard_map/ppermute | solution.py:470
  34.3 9.6 %collective-permute-start.2 = (bf16[16,8,128]{2,1,0:T(8,128)(2,1)S(1)}, bf16[16,8,128]{2,1,0:T(8,128)(2,1)S(1)}, u32[]{:S(2)}, u32[]{:S(2)}) collective-permute-start(bf16[16,8,128]{2,1,0:T(8,128)(2,1)S(1)} %get-tuple-element.25.head_ref), channel_id=1, source_target_pairs={{1,0},{2,1},{3,2},{4,3},{5,4},{6,5},{7,6},{8,7},{9,8},{10,9},{11,1... | collective-permute-start | bytes 98312 | tf_op jit(solution)/shard_map/ppermute | solution.py:471
  43.9 0.0 collective-permute-done.1.left_ref
  43.9 1.0 %collective-permute-done.2.right_ref = bf16[16,8,128]{2,1,0:T(8,128)(2,1)S(1)} collective-permute-done((bf16[16,8,128]{2,1,0:T(8,128)(2,1)S(1)}, bf16[16,8,128]{2,1,0:T(8,128)(2,1)S(1)}, u32[]{:S(2)}, u32[]{:S(2)}) %collective-permute-start.2) | collective-permute-done | bytes 32800 | tf_op jit(solution)/shard_map/ppermute | solution.py:471
  44.9 2.2 %edges.1 = f32[14,32,128]{2,1,0:T(8,128)} custom-call(f32[2,16,128]{2,1,0:T(8,128)S(1)} %get-tuple-element.19.chosen_ref, f32[32,128]{1,0:T(8,128)S(1)} %get-tuple-element.20.keep_ref, bf16[16,8,128]{2,1,0:T(8,128)(2,1)S(1)} %collective-permute-done.1.left_ref, bf16[16,8,128]{2,1,0:T(8,128)(2,1)S(1)} %collective-permute-done.2.right_ref, ...), custom_call_target="tpu_custom_call" | custom-call | flops 500000000 | bytes 4000000 | tf_op jit(solution)/shard_map/edges/pallas_call | solution.py:421
  (1 shorter events, 0.0 us)
Async XLA Ops:
  0.0 11.1 %copy-start.6 = (f32[2,32]{1,0:T(2,128)S(1)}, f32[2,32]{1,0:T(2,128)}, u32[]{:S(2)}) copy-start(f32[2,32]{1,0:T(2,128)} %pilot_ref.1) | copy-start | bytes 772
  0.0 11.1 %copy-start.7 = (s32[2]{0:T(128)S(1)}, s32[2]{0:T(128)}, u32[]{:S(2)}) copy-start(s32[2]{0:T(128)} %param.15) | copy-start | bytes 28
  0.0 11.1 %copy-start.8 = (s32[8]{0:T(128)S(1)}, s32[8]{0:T(128)}, u32[]{:S(2)}) copy-start(s32[8]{0:T(128)} %param.17) | copy-start | bytes 100
  2.3 10.9 %collective-permute-start = (bf16[8,14,32,128]{3,2,1,0:T(8,128)(2,1)S(1)}, bf16[8,14,32,128]{3,2,1,0:T(8,128)(2,1)S(1)}, u32[]{:S(2)}, u32[]{:S(2)}) collective-permute-start(bf16[8,14,32,128]{3,2,1,0:T(8,128)(2,1)S(1)} %get-tuple-element.23), channel_id=1, source_target_pairs={{0,32},{32,0},{64,96},{96,64},{128,160},{160,128},{192,224},{224,1... | collective-permute-start | bytes 2752520 | tf_op jit(solution)/shard_map/ppermute | solution.py:454
  13.3 16.4 %copy-start = (bf16[5,3,3,128,128]{4,3,2,1,0:T(8,128)(2,1)S(1)}, bf16[5,3,3,128,128]{4,3,2,1,0:T(8,128)(2,1)}, u32[]{:S(2)}) copy-start(bf16[5,3,3,128,128]{4,3,2,1,0:T(8,128)(2,1)} %param.19) | copy-start | bytes 4423684
  13.3 16.4 %copy-start.1 = (bf16[3,3,256,128]{3,2,1,0:T(8,128)(2,1)S(1)}, bf16[3,3,256,128]{3,2,1,0:T(8,128)(2,1)}, u32[]{:S(2)}) copy-start(bf16[3,3,256,128]{3,2,1,0:T(8,128)(2,1)} %param.18) | copy-start | bytes 1769476
  13.3 16.4 %copy-start.2 = (bf16[128,256]{1,0:T(8,128)(2,1)S(1)}, bf16[128,256]{1,0:T(8,128)(2,1)}, u32[]{:S(2)}) copy-start(bf16[128,256]{1,0:T(8,128)(2,1)} %in_ref.1) | copy-start | bytes 196612
  13.3 16.4 %copy-start.3 = (bf16[256,128]{1,0:T(8,128)(2,1)S(1)}, bf16[256,128]{1,0:T(8,128)(2,1)}, u32[]{:S(2)}) copy-start(bf16[256,128]{1,0:T(8,128)(2,1)} %out_w_ref.1) | copy-start | bytes 196612
  13.3 16.4 %copy-start.4 = (f32[6,128]{1,0:T(8,128)S(1)}, f32[6,128]{1,0:T(8,128)}, u32[]{:S(2)}) copy-start(f32[6,128]{1,0:T(8,128)} %bias_ref.1) | copy-start | bytes 9220
  13.3 16.4 %copy-start.5 = (f32[256]{0:T(256)S(1)}, f32[256]{0:T(256)}, u32[]{:S(2)}) copy-start(f32[256]{0:T(256)} %param.22) | copy-start | bytes 3076
  32.3 11.6 %collective-permute-start.1 = (bf16[16,8,128]{2,1,0:T(8,128)(2,1)S(1)}, bf16[16,8,128]{2,1,0:T(8,128)(2,1)S(1)}, u32[]{:S(2)}, u32[]{:S(2)}) collective-permute-start(bf16[16,8,128]{2,1,0:T(8,128)(2,1)S(1)} %get-tuple-element.24.tail_ref), channel_id=1, source_target_pairs={{0,1},{1,2},{2,3},{3,4},{4,5},{5,6},{6,7},{7,8},{8,9},{9,10},{10,1... | collective-permute-start | bytes 98312 | tf_op jit(solution)/shard_map/ppermute | solution.py:470
  34.3 10.6 %collective-permute-start.2 = (bf16[16,8,128]{2,1,0:T(8,128)(2,1)S(1)}, bf16[16,8,128]{2,1,0:T(8,128)(2,1)S(1)}, u32[]{:S(2)}, u32[]{:S(2)}) collective-permute-start(bf16[16,8,128]{2,1,0:T(8,128)(2,1)S(1)} %get-tuple-element.25.head_ref), channel_id=1, source_target_pairs={{1,0},{2,1},{3,2},{4,3},{5,4},{6,5},{7,6},{8,7},{9,8},{10,9},{11,1... | collective-permute-start | bytes 98312 | tf_op jit(solution)/shard_map/ppermute | solution.py:471

commit v7 on v6

--- a/solution.py
+++ b/solution.py
@@ -380,18 +380,13 @@
             [joined(patch[:, EDGE:], high, EDGE - 2 + dc) for dc in range(3)],
         ]
         low, high = (convolved(field, rest_ref[layer - 1], bias_ref[layer : layer + 1, :]) for field in fields)
-    total = jnp.concatenate([low, high], axis=1)
-    llr = demapped(total.reshape(rows, c).astype(jnp.bfloat16), in_ref, in_bias_ref, out_w_ref)
-    keep = jnp.concatenate([keep_ref[:EDGE], keep_ref[subs - EDGE :]], axis=0)
-    store_llr(llr_buf, llr, keep, chosen_ref)
-    copies = [
-        pltpu.make_async_copy(
-            llr_buf.at[:, pl.ds(side * EDGE, EDGE)], llr_ref.at[:, pl.ds(start, EDGE)], sems.at[side]
-        )
-        for side, start in enumerate((0, subs - EDGE))
-    ]
-    for copy in copies:
+    copies = []
+    for side, (field, start) in enumerate(((low, 0), (high, subs - EDGE))):
+        llr = demapped(field.reshape(syms * EDGE, c).astype(jnp.bfloat16), in_ref, in_bias_ref, out_w_ref)
+        store_llr(llr_buf.at[side], llr, keep_ref[start : start + EDGE], chosen_ref)
+        copy = pltpu.make_async_copy(llr_buf.at[side], llr_ref.at[:, pl.ds(start, EDGE)], sems.at[side])
         copy.start()
+        copies.append(copy)
     inner_copy.wait()
     for copy in copies:
         copy.wait()
@@ -424,7 +419,7 @@
         out_specs=pl.BlockSpec(memory_space=pltpu.HBM),
         out_shape=pltpu.HBM(inner.shape, jnp.float32),
         scratch_shapes=[
-            pltpu.VMEM((syms, 2 * EDGE, bits), jnp.float32),
+            pltpu.VMEM((2, syms, EDGE, bits), jnp.float32),
             pltpu.SemaphoreType.DMA((3,)),
         ],
         compiler_params=pltpu.CompilerParams(vmem_limit_bytes=16 * 2**20),

time: 47.3 us -> 47.3 us (level)
  no operation moved by 1% of the time
where the time goes in v7:
time: 47.3 us; the launch traced here: 47.1 us
  starting transfers between devices  20.3 us (43%)
  blocking collectives  16.1 us (34%)
  Pallas kernels  9.23 us (20%)
  waiting for transfers between devices  0.97 us (2%)
    all_to_all x1, blocking collectives, per_device(): lax.all_to_all(pairs, PANEL, 0, 0, axis_index_groups=same_core, tiled=True)  16.1 us
    ppermute x1, starting transfers between devices, per_device(): right = lax.ppermute(head, both, [(i + 1, i) for i in range(count - 1)])  9.62 us
    ppermute x1, starting transfers between devices, per_device(): got = lax.ppermute(given, PANEL, [(p, p ^ 1) for p in range(panels)])  8.79 us
    pallas_call x1, Pallas kernels, sum_beams(): pl.pallas_call(sum_kernel, in_specs=[vmem] * 10, out_specs=[vmem] * 5, ou...  2.62 us
    pallas_call x1, Pallas kernels, beam_partials(): pl.pallas_call(given_kernel, in_specs=[hbm] * 3, out_specs=[vmem] * 2, ou...  2.32 us
    pallas_call x1, Pallas kernels, receive_edges(): pl.pallas_call(edge_kernel, in_specs=[vmem] * 14, out_specs=pl.BlockSpec(...  2.17 us
    pallas_call x1, Pallas kernels, beam_partials(): pl.pallas_call(kept_kernel, in_specs=[vmem] * 4 + [hbm], out_specs=[vmem]...  2.11 us
    ppermute x1, starting transfers between devices, per_device(): left = lax.ppermute(tail, both, [(i, i + 1) for i in range(count - 1)])  1.92 us
  transfers between devices with their start and end apart: 3, of which 1 were waited for; matrix products, arithmetic and copies ran while one was open for 0% of the time, Pallas kernels for 5%

profile of v7, /device:TPU:1, one launch (start us, length us, event | category | flops | bytes accessed | tf_op | source)
XLA Modules:
  0.0 47.1 jit_solution(3329532069039688932)
XLA Ops:
  0.0 0.0 copy-start.6
  0.0 0.0 copy-start.7
  0.0 0.0 copy-start.8
  0.0 2.3 %given.1 = (bf16[8,14,32,128]{3,2,1,0:T(8,128)(2,1)S(1)}, bf16[256,128]{1,0:T(8,128)(2,1)S(1)}) custom-call(s32[1,128]{1,0:T(1,128)} %bitcast.20, bf16[128,128]{1,0:T(8,128)(2,1)} %rows_ref.1, bf16[8,2,14,32,256]{4,3,2,1,0:T(8,128)(2,1)} %bitcast.18), custom_call_target="tpu_custom_call" | custom-call | tf_op jit(solution)/shard_map/given/pallas_call | solution.py:112
  2.3 8.8 %collective-permute-start = (bf16[8,14,32,128]{3,2,1,0:T(8,128)(2,1)S(1)}, bf16[8,14,32,128]{3,2,1,0:T(8,128)(2,1)S(1)}, u32[]{:S(2)}, u32[]{:S(2)}) collective-permute-start(bf16[8,14,32,128]{3,2,1,0:T(8,128)(2,1)S(1)} %get-tuple-element.23), channel_id=1, source_target_pairs={{0,32},{32,0},{64,96},{96,64},{128,160},{160,128},{192,224},{224,1... | collective-permute-start | bytes 2752520 | tf_op jit(solution)/shard_map/ppermute | solution.py:449
  11.1 0.0 copy-done.6
  11.1 0.0 copy-done.7
  11.2 0.0 copy-done.8
  11.2 2.1 %kept.1 = (bf16[8,14,32,128]{3,2,1,0:T(8,128)(2,1)S(1)}, f32[2,16,128]{2,1,0:T(8,128)S(1)}, f32[32,128]{1,0:T(8,128)S(1)}, f32[2,32,128]{2,1,0:T(8,128)S(1)}) custom-call(bf16[256,128]{1,0:T(8,128)(2,1)S(1)} %get-tuple-element.18.matrix_ref, s32[1,2]{1,0:T(1,128)S(1)} %bitcast.16, s32[1,8]{1,0:T(1,128)S(1)} %bitcast.17, f32[2,32]{1,0:T(2,128)S(1)} %copy-done.6, ...), custom_call_target="tpu_custom_call" | custom-call | flops 234881024 | bytes 1835008 | tf_op jit(solution)/shard_map/kept/pallas_call | solution.py:126
  13.3 0.0 collective-permute-done
  13.3 0.0 copy-start
  13.3 0.0 copy-start.1
  13.3 0.0 copy-start.2
  13.3 0.0 copy-start.3
  13.3 0.0 copy-start.4
  13.3 0.0 copy-start.5
  13.4 0.2 add_convert_fusion
  13.6 16.1 %all_to_all.5.parts_ref = bf16[8,14,32,128]{3,2,1,0:T(8,128)(2,1)S(1)} all-to-all(bf16[8,14,32,128]{3,2,1,0:T(8,128)(2,1)S(1)} %add_convert_fusion), channel_id=1, replica_groups={{0,64,128,192,256,320,384,448},{32,96,160,224,288,352,416,480},{1,65,12..., dimensions={0} | all-to-all | bytes 1835008 | tf_op jit(solution)/shard_map/all_to_all | solution.py:452
  29.7 0.0 copy-done
  29.7 0.0 copy-done.1
  29.7 0.0 copy-done.2
  29.7 0.0 copy-done.3
  29.7 0.0 copy-done.4
  29.7 0.0 copy-done.5
  29.7 2.6 %sum_beams.1 = (bf16[16,32,128]{2,1,0:T(8,128)(2,1)S(1)}, bf16[16,8,128]{2,1,0:T(8,128)(2,1)S(1)}, bf16[16,8,128]{2,1,0:T(8,128)(2,1)S(1)}, f32[14,32,128]{2,1,0:T(8,128)S(1)}, f32[5,14,16,128]{3,2,1,0:T(8,128)S(1)}) custom-call(f32[2,16,128]{2,1,0:T(8,128)S(1)} %get-tuple-element.19.chosen_ref, f32[32,128]{1,0:T(8,128)S(1)} %get-tuple-element.20.keep_ref, ...), custom_call_target="tpu_custom_call" | custom-call | tf_op jit(solution)/shard_map/sum_beams/pallas_call | solution.py:236
  32.3 1.9 %collective-permute-start.1 = (bf16[16,8,128]{2,1,0:T(8,128)(2,1)S(1)}, bf16[16,8,128]{2,1,0:T(8,128)(2,1)S(1)}, u32[]{:S(2)}, u32[]{:S(2)}) collective-permute-start(bf16[16,8,128]{2,1,0:T(8,128)(2,1)S(1)} %get-tuple-element.24.tail_ref), channel_id=1, source_target_pairs={{0,1},{1,2},{2,3},{3,4},{4,5},{5,6},{6,7},{7,8},{8,9},{9,10},{10,1... | collective-permute-start | bytes 98312 | tf_op jit(solution)/shard_map/ppermute | solution.py:465
  34.3 9.6 %collective-permute-start.2 = (bf16[16,8,128]{2,1,0:T(8,128)(2,1)S(1)}, bf16[16,8,128]{2,1,0:T(8,128)(2,1)S(1)}, u32[]{:S(2)}, u32[]{:S(2)}) collective-permute-start(bf16[16,8,128]{2,1,0:T(8,128)(2,1)S(1)} %get-tuple-element.25.head_ref), channel_id=1, source_target_pairs={{1,0},{2,1},{3,2},{4,3},{5,4},{6,5},{7,6},{8,7},{9,8},{10,9},{11,1... | collective-permute-start | bytes 98312 | tf_op jit(solution)/shard_map/ppermute | solution.py:466
  43.9 0.0 collective-permute-done.1.left_ref
  43.9 1.0 %collective-permute-done.2.right_ref = bf16[16,8,128]{2,1,0:T(8,128)(2,1)S(1)} collective-permute-done((bf16[16,8,128]{2,1,0:T(8,128)(2,1)S(1)}, bf16[16,8,128]{2,1,0:T(8,128)(2,1)S(1)}, u32[]{:S(2)}, u32[]{:S(2)}) %collective-permute-start.2) | collective-permute-done | bytes 32800 | tf_op jit(solution)/shard_map/ppermute | solution.py:466
  44.9 2.2 %edges.1 = f32[14,32,128]{2,1,0:T(8,128)} custom-call(f32[2,16,128]{2,1,0:T(8,128)S(1)} %get-tuple-element.19.chosen_ref, f32[32,128]{1,0:T(8,128)S(1)} %get-tuple-element.20.keep_ref, bf16[16,8,128]{2,1,0:T(8,128)(2,1)S(1)} %collective-permute-done.1.left_ref, bf16[16,8,128]{2,1,0:T(8,128)(2,1)S(1)} %collective-permute-done.2.right_ref, ...), custom_call_target="tpu_custom_call" | custom-call | flops 500000000 | bytes 4000000 | tf_op jit(solution)/shard_map/edges/pallas_call | solution.py:416
  (1 shorter events, 0.0 us)
Async XLA Ops:
  0.0 11.1 %copy-start.6 = (f32[2,32]{1,0:T(2,128)S(1)}, f32[2,32]{1,0:T(2,128)}, u32[]{:S(2)}) copy-start(f32[2,32]{1,0:T(2,128)} %pilot_ref.1) | copy-start | bytes 772
  0.0 11.1 %copy-start.7 = (s32[2]{0:T(128)S(1)}, s32[2]{0:T(128)}, u32[]{:S(2)}) copy-start(s32[2]{0:T(128)} %param.15) | copy-start | bytes 28
  0.0 11.1 %copy-start.8 = (s32[8]{0:T(128)S(1)}, s32[8]{0:T(128)}, u32[]{:S(2)}) copy-start(s32[8]{0:T(128)} %param.17) | copy-start | bytes 100
  2.3 10.9 %collective-permute-start = (bf16[8,14,32,128]{3,2,1,0:T(8,128)(2,1)S(1)}, bf16[8,14,32,128]{3,2,1,0:T(8,128)(2,1)S(1)}, u32[]{:S(2)}, u32[]{:S(2)}) collective-permute-start(bf16[8,14,32,128]{3,2,1,0:T(8,128)(2,1)S(1)} %get-tuple-element.23), channel_id=1, source_target_pairs={{0,32},{32,0},{64,96},{96,64},{128,160},{160,128},{192,224},{224,1... | collective-permute-start | bytes 2752520 | tf_op jit(solution)/shard_map/ppermute | solution.py:449
  13.3 16.4 %copy-start = (bf16[5,3,3,128,128]{4,3,2,1,0:T(8,128)(2,1)S(1)}, bf16[5,3,3,128,128]{4,3,2,1,0:T(8,128)(2,1)}, u32[]{:S(2)}) copy-start(bf16[5,3,3,128,128]{4,3,2,1,0:T(8,128)(2,1)} %param.19) | copy-start | bytes 4423684
  13.3 16.4 %copy-start.1 = (bf16[3,3,256,128]{3,2,1,0:T(8,128)(2,1)S(1)}, bf16[3,3,256,128]{3,2,1,0:T(8,128)(2,1)}, u32[]{:S(2)}) copy-start(bf16[3,3,256,128]{3,2,1,0:T(8,128)(2,1)} %param.18) | copy-start | bytes 1769476
  13.3 16.4 %copy-start.2 = (bf16[128,256]{1,0:T(8,128)(2,1)S(1)}, bf16[128,256]{1,0:T(8,128)(2,1)}, u32[]{:S(2)}) copy-start(bf16[128,256]{1,0:T(8,128)(2,1)} %in_ref.1) | copy-start | bytes 196612
  13.3 16.4 %copy-start.3 = (bf16[256,128]{1,0:T(8,128)(2,1)S(1)}, bf16[256,128]{1,0:T(8,128)(2,1)}, u32[]{:S(2)}) copy-start(bf16[256,128]{1,0:T(8,128)(2,1)} %out_w_ref.1) | copy-start | bytes 196612
  13.3 16.4 %copy-start.4 = (f32[6,128]{1,0:T(8,128)S(1)}, f32[6,128]{1,0:T(8,128)}, u32[]{:S(2)}) copy-start(f32[6,128]{1,0:T(8,128)} %bias_ref.1) | copy-start | bytes 9220
  13.3 16.4 %copy-start.5 = (f32[256]{0:T(256)S(1)}, f32[256]{0:T(256)}, u32[]{:S(2)}) copy-start(f32[256]{0:T(256)} %param.22) | copy-start | bytes 3076
  32.3 11.6 %collective-permute-start.1 = (bf16[16,8,128]{2,1,0:T(8,128)(2,1)S(1)}, bf16[16,8,128]{2,1,0:T(8,128)(2,1)S(1)}, u32[]{:S(2)}, u32[]{:S(2)}) collective-permute-start(bf16[16,8,128]{2,1,0:T(8,128)(2,1)S(1)} %get-tuple-element.24.tail_ref), channel_id=1, source_target_pairs={{0,1},{1,2},{2,3},{3,4},{4,5},{5,6},{6,7},{7,8},{8,9},{9,10},{10,1... | collective-permute-start | bytes 98312 | tf_op jit(solution)/shard_map/ppermute | solution.py:465
  34.3 10.6 %collective-permute-start.2 = (bf16[16,8,128]{2,1,0:T(8,128)(2,1)S(1)}, bf16[16,8,128]{2,1,0:T(8,128)(2,1)S(1)}, u32[]{:S(2)}, u32[]{:S(2)}) collective-permute-start(bf16[16,8,128]{2,1,0:T(8,128)(2,1)S(1)} %get-tuple-element.25.head_ref), channel_id=1, source_target_pairs={{1,0},{2,1},{3,2},{4,3},{5,4},{6,5},{7,6},{8,7},{9,8},{10,9},{11,1... | collective-permute-start | bytes 98312 | tf_op jit(solution)/shard_map/ppermute | solution.py:466

commit v8 on v6

--- a/solution.py
+++ b/solution.py
@@ -92,8 +92,44 @@
         pilots_ref[0], pilots_ref[1] = signed_pilots(pilot_ref, pilots_ref.shape[2])
         return matrix_ref[...]
 
-    parity = lax.axis_index(PANEL) % 2
-    matrix_kernel_body(wave_ref, out_ref, blocks_ref, sems, matrix, parity)
+    weights = matrix()
+
+    @pl.when(first_to_exchange())
+    def _():
+        matrix_kernel_body(wave_ref, out_ref, blocks_ref, sems, lambda: weights, lax.axis_index(PANEL) % 2)
+
+
+def first_to_exchange():
+    return lax.axis_index(PANEL) % 2 == 0
+
+
+def pair_kernel(matrix_ref, kept_ref, got_ref, wave_ref, out_ref, blocks_ref, sems):
+    @pl.when(first_to_exchange())
+    def _():
+        out_ref[...] = (kept_ref[...].astype(jnp.float32) + got_ref[...].astype(jnp.float32)).astype(jnp.bfloat16)
+
+    @pl.when(jnp.logical_not(first_to_exchange()))
+    def _():
+        matrix_kernel_body(
+            wave_ref, out_ref, blocks_ref, sems, lambda: matrix_ref[...], lax.axis_index(PANEL) % 2
+        )
+        out_ref[...] = (out_ref[...].astype(jnp.float32) + got_ref[...].astype(jnp.float32)).astype(jnp.bfloat16)
+
+
+def pair_sums(matrix, kept, got, wave):
+    half, syms, subs, _ = kept.shape
+    k = wave.shape[3]
+    vmem = pl.BlockSpec(memory_space=pltpu.VMEM)
+    wave = pltpu.with_memory_space_constraint(wave.reshape(half, 2, syms, subs, k), pltpu.HBM)
+    return pl.pallas_call(
+        pair_kernel,
+        in_specs=[vmem] * 3 + [pl.BlockSpec(memory_space=pltpu.HBM)],
+        out_specs=vmem,
+        out_shape=jax.ShapeDtypeStruct(kept.shape, kept.dtype),
+        scratch_shapes=[pltpu.VMEM((half, syms, subs, k), jnp.bfloat16), pltpu.SemaphoreType.DMA((COPIES,))],
+        compiler_params=pltpu.CompilerParams(vmem_limit_bytes=8 * 2**20),
+        name="pair_sums",
+    )(matrix, kept, got, wave)
 
 
 def beam_partials(wave, lookup, rows, pilot_syms, mod_order, pilot_values, bits):
@@ -140,7 +176,7 @@
         ),
         name="kept",
     )(matrix, pilot_syms.reshape(1, -1), mod_order.reshape(1, -1), pilot_values, wave)
-    return given, kept, facts
+    return given, kept, facts, matrix
 
 
 def entry(row, i):
@@ -447,12 +483,12 @@
     demap_bias,
     demap_out,
 ):
-    given, kept, facts = beam_partials(
+    given, kept, facts, matrix = beam_partials(
         captured_waveform, element_lookup, combiner, pilot_syms, mod_order, pilot_values, demap_out.shape[1]
     )
     panels = lax.axis_size(PANEL)
     got = lax.ppermute(given, PANEL, [(p, p ^ 1) for p in range(panels)])
-    pairs = (kept.astype(jnp.float32) + got.astype(jnp.float32)).astype(jnp.bfloat16)
+    pairs = pair_sums(matrix, kept, got, captured_waveform)
     same_core = [list(range(core, panels, 2)) for core in range(2)]
     parts = lax.all_to_all(pairs, PANEL, 0, 0, axis_index_groups=same_core, tiled=True)
     c = combiner.shape[1]

time: 47.3 us -> 47.3 us (level)
  waiting for transfers between devices: 0.97 us -> 2.88 us
  starting transfers between devices: 20.3 us -> 18.5 us
    pallas_call x0 -> x1, Pallas kernels: none -> 2.3 us  [pair_sums(): pl.pallas_call(pair_kernel, in_specs=[vmem] * 3 + [pl.BlockSpec(memory_sp...]
    pallas_call x1, Pallas kernels: 2.11 us -> 0.13 us  [beam_partials(): pl.pallas_call(kept_kernel, in_specs=[vmem] * 4 + [hbm], out_specs=[vmem]...]
    ppermute x1, waiting for transfers between devices: 0.01 us -> 1.91 us  [per_device(): got = lax.ppermute(given, PANEL, [(p, p ^ 1) for p in range(panels)])]
    ppermute x1, starting transfers between devices: 9.62 us -> 7.8 us  [per_device(): right = lax.ppermute(head, both, [(i + 1, i) for i in range(count - 1)])]
  transfers between devices with their start and end apart: 3 -> 3, of which waited for: 1 -> 2; matrix products, arithmetic and copies ran while one was open for 0% -> 0% of each run, Pallas kernels for 5% -> 0%
where the time goes in v8:
time: 47.3 us; the launch traced here: 47.1 us
  starting transfers between devices  18.5 us (39%)
  blocking collectives  15.9 us (34%)
  Pallas kernels  9.6 us (20%)
  waiting for transfers between devices  2.88 us (6%)
    all_to_all x1, blocking collectives, per_device(): lax.all_to_all(pairs, PANEL, 0, 0, axis_index_groups=same_core, tiled=True)  15.9 us
    ppermute x1, starting transfers between devices, per_device(): got = lax.ppermute(given, PANEL, [(p, p ^ 1) for p in range(panels)])  8.79 us
    ppermute x1, starting transfers between devices, per_device(): right = lax.ppermute(head, both, [(i + 1, i) for i in range(count - 1)])  7.8 us
    pallas_call x1, Pallas kernels, sum_beams(): pl.pallas_call(sum_kernel, in_specs=[vmem] * 10, out_specs=[vmem] * 5, ou...  2.62 us
    pallas_call x1, Pallas kernels, beam_partials(): pl.pallas_call(given_kernel, in_specs=[hbm] * 3, out_specs=[vmem] * 2, ou...  2.32 us
    pallas_call x1, Pallas kernels, pair_sums(): pl.pallas_call(pair_kernel, in_specs=[vmem] * 3 + [pl.BlockSpec(memory_sp...  2.3 us
    pallas_call x1, Pallas kernels, receive_edges(): pl.pallas_call(edge_kernel, in_specs=[vmem] * 14, out_specs=pl.BlockSpec(...  2.21 us
    ppermute x1, starting transfers between devices, per_device(): left = lax.ppermute(tail, both, [(i, i + 1) for i in range(count - 1)])  1.92 us
  transfers between devices with their start and end apart: 3, of which 2 were waited for; matrix products, arithmetic and copies ran while one was open for 0% of the time, Pallas kernels for 0%

profile of v8, /device:TPU:1, one launch (start us, length us, event | category | flops | bytes accessed | tf_op | source)
XLA Modules:
  0.0 47.1 jit_solution(14836056634220832357)
XLA Ops:
  0.0 0.0 copy-start.8
  0.0 0.0 copy-start.6
  0.0 0.0 copy-start.7
  0.0 2.3 %given.1 = (bf16[8,14,32,128]{3,2,1,0:T(8,128)(2,1)S(1)}, bf16[256,128]{1,0:T(8,128)(2,1)S(1)}) custom-call(s32[1,128]{1,0:T(1,128)} %bitcast.21, bf16[128,128]{1,0:T(8,128)(2,1)} %rows_ref.1, bf16[8,2,14,32,256]{4,3,2,1,0:T(8,128)(2,1)} %bitcast.18), custom_call_target="tpu_custom_call" | custom-call | tf_op jit(solution)/shard_map/given/pallas_call | solution.py:148
  2.3 8.8 %collective-permute-start = (bf16[8,14,32,128]{3,2,1,0:T(8,128)(2,1)S(1)}, bf16[8,14,32,128]{3,2,1,0:T(8,128)(2,1)S(1)}, u32[]{:S(2)}, u32[]{:S(2)}) collective-permute-start(bf16[8,14,32,128]{3,2,1,0:T(8,128)(2,1)S(1)} %get-tuple-element.23), channel_id=1, source_target_pairs={{0,32},{32,0},{64,96},{96,64},{128,160},{160,128},{192,224},{224,1... | collective-permute-start | bytes 2752520 | tf_op jit(solution)/shard_map/ppermute | solution.py:490
  11.1 0.0 copy-done.8
  11.1 0.0 copy-done.6
  11.2 0.0 copy-done.7
  11.2 0.1 kept.1
  11.3 1.9 %collective-permute-done.got_ref = bf16[8,14,32,128]{3,2,1,0:T(8,128)(2,1)S(1)} collective-permute-done((bf16[8,14,32,128]{3,2,1,0:T(8,128)(2,1)S(1)}, bf16[8,14,32,128]{3,2,1,0:T(8,128)(2,1)S(1)}, u32[]{:S(2)}, u32[]{:S(2)}) %collective-permute-start) | collective-permute-done | bytes 917536 | tf_op jit(solution)/shard_map/ppermute | solution.py:490
  13.2 0.0 copy-start
  13.2 0.0 copy-start.1
  13.2 0.0 copy-start.2
  13.2 0.0 copy-start.3
  13.2 0.0 copy-start.4
  13.2 0.0 copy-start.5
  13.2 2.3 %pair_sums.1 = bf16[8,14,32,128]{3,2,1,0:T(8,128)(2,1)S(1)} custom-call(bf16[256,128]{1,0:T(8,128)(2,1)S(1)} %get-tuple-element.18.matrix_ref, bf16[8,14,32,128]{3,2,1,0:T(8,128)(2,1)S(1)} %get-tuple-element.22.kept_ref, bf16[8,14,32,128]{3,2,1,0:T(8,128)(2,1)S(1)} %collective-permute-done.got_ref, bf16[8,2,14,32,256]{4,3,2,1,0:T(8,128)(2,1)} %bitcast.20), custom_call_target="tpu_custom_call" | custom-call | tf_op jit(solution)/shard_map/pair_sums/pallas_call | solution.py:124
  15.5 15.9 %all_to_all.5.parts_ref = bf16[8,14,32,128]{3,2,1,0:T(8,128)(2,1)S(1)} all-to-all(bf16[8,14,32,128]{3,2,1,0:T(8,128)(2,1)S(1)} %pair_sums.1), channel_id=1, replica_groups={{0,64,128,192,256,320,384,448},{32,96,160,224,288,352,416,480},{1,65,12..., dimensions={0} | all-to-all | bytes 1835008 | tf_op jit(solution)/shard_map/all_to_all | solution.py:493
  31.5 0.0 copy-done
  31.5 0.0 copy-done.1
  31.5 0.0 copy-done.2
  31.5 0.0 copy-done.3
  31.5 0.0 copy-done.4
  31.5 0.0 copy-done.5
  31.5 2.6 %sum_beams.1 = (bf16[16,32,128]{2,1,0:T(8,128)(2,1)S(1)}, bf16[16,8,128]{2,1,0:T(8,128)(2,1)S(1)}, bf16[16,8,128]{2,1,0:T(8,128)(2,1)S(1)}, f32[14,32,128]{2,1,0:T(8,128)S(1)}, f32[5,14,16,128]{3,2,1,0:T(8,128)S(1)}) custom-call(f32[2,16,128]{2,1,0:T(8,128)S(1)} %get-tuple-element.19.chosen_ref, f32[32,128]{1,0:T(8,128)S(1)} %get-tuple-element.20.keep_ref, ...), custom_call_target="tpu_custom_call" | custom-call | tf_op jit(solution)/shard_map/sum_beams/pallas_call | solution.py:272
  34.1 1.9 %collective-permute-start.1 = (bf16[16,8,128]{2,1,0:T(8,128)(2,1)S(1)}, bf16[16,8,128]{2,1,0:T(8,128)(2,1)S(1)}, u32[]{:S(2)}, u32[]{:S(2)}) collective-permute-start(bf16[16,8,128]{2,1,0:T(8,128)(2,1)S(1)} %get-tuple-element.24.tail_ref), channel_id=1, source_target_pairs={{0,1},{1,2},{2,3},{3,4},{4,5},{5,6},{6,7},{7,8},{8,9},{9,10},{10,1... | collective-permute-start | bytes 98312 | tf_op jit(solution)/shard_map/ppermute | solution.py:506
  36.1 7.8 %collective-permute-start.2 = (bf16[16,8,128]{2,1,0:T(8,128)(2,1)S(1)}, bf16[16,8,128]{2,1,0:T(8,128)(2,1)S(1)}, u32[]{:S(2)}, u32[]{:S(2)}) collective-permute-start(bf16[16,8,128]{2,1,0:T(8,128)(2,1)S(1)} %get-tuple-element.25.head_ref), channel_id=1, source_target_pairs={{1,0},{2,1},{3,2},{4,3},{5,4},{6,5},{7,6},{8,7},{9,8},{10,9},{11,1... | collective-permute-start | bytes 98312 | tf_op jit(solution)/shard_map/ppermute | solution.py:507
  43.9 0.0 collective-permute-done.1.left_ref
  43.9 1.0 %collective-permute-done.2.right_ref = bf16[16,8,128]{2,1,0:T(8,128)(2,1)S(1)} collective-permute-done((bf16[16,8,128]{2,1,0:T(8,128)(2,1)S(1)}, bf16[16,8,128]{2,1,0:T(8,128)(2,1)S(1)}, u32[]{:S(2)}, u32[]{:S(2)}) %collective-permute-start.2) | collective-permute-done | bytes 32800 | tf_op jit(solution)/shard_map/ppermute | solution.py:507
  44.9 2.2 %edges.1 = f32[14,32,128]{2,1,0:T(8,128)} custom-call(f32[2,16,128]{2,1,0:T(8,128)S(1)} %get-tuple-element.19.chosen_ref, f32[32,128]{1,0:T(8,128)S(1)} %get-tuple-element.20.keep_ref, bf16[16,8,128]{2,1,0:T(8,128)(2,1)S(1)} %collective-permute-done.1.left_ref, bf16[16,8,128]{2,1,0:T(8,128)(2,1)S(1)} %collective-permute-done.2.right_ref, ...), custom_call_target="tpu_custom_call" | custom-call | flops 500000000 | bytes 4000000 | tf_op jit(solution)/shard_map/edges/pallas_call | solution.py:457
  (1 shorter events, 0.0 us)
Async XLA Ops:
  0.0 11.1 %copy-start.8 = (s32[8]{0:T(128)S(1)}, s32[8]{0:T(128)}, u32[]{:S(2)}) copy-start(s32[8]{0:T(128)} %param.17) | copy-start | bytes 100
  0.0 11.1 %copy-start.6 = (f32[2,32]{1,0:T(2,128)S(1)}, f32[2,32]{1,0:T(2,128)}, u32[]{:S(2)}) copy-start(f32[2,32]{1,0:T(2,128)} %pilot_ref.1) | copy-start | bytes 772
  0.0 11.1 %copy-start.7 = (s32[2]{0:T(128)S(1)}, s32[2]{0:T(128)}, u32[]{:S(2)}) copy-start(s32[2]{0:T(128)} %param.15) | copy-start | bytes 28
  2.3 10.9 %collective-permute-start = (bf16[8,14,32,128]{3,2,1,0:T(8,128)(2,1)S(1)}, bf16[8,14,32,128]{3,2,1,0:T(8,128)(2,1)S(1)}, u32[]{:S(2)}, u32[]{:S(2)}) collective-permute-start(bf16[8,14,32,128]{3,2,1,0:T(8,128)(2,1)S(1)} %get-tuple-element.23), channel_id=1, source_target_pairs={{0,32},{32,0},{64,96},{96,64},{128,160},{160,128},{192,224},{224,1... | collective-permute-start | bytes 2752520 | tf_op jit(solution)/shard_map/ppermute | solution.py:490
  13.2 18.3 %copy-start = (bf16[5,3,3,128,128]{4,3,2,1,0:T(8,128)(2,1)S(1)}, bf16[5,3,3,128,128]{4,3,2,1,0:T(8,128)(2,1)}, u32[]{:S(2)}) copy-start(bf16[5,3,3,128,128]{4,3,2,1,0:T(8,128)(2,1)} %param.19) | copy-start | bytes 4423684
  13.2 18.3 %copy-start.1 = (bf16[3,3,256,128]{3,2,1,0:T(8,128)(2,1)S(1)}, bf16[3,3,256,128]{3,2,1,0:T(8,128)(2,1)}, u32[]{:S(2)}) copy-start(bf16[3,3,256,128]{3,2,1,0:T(8,128)(2,1)} %param.18) | copy-start | bytes 1769476
  13.2 18.3 %copy-start.2 = (bf16[128,256]{1,0:T(8,128)(2,1)S(1)}, bf16[128,256]{1,0:T(8,128)(2,1)}, u32[]{:S(2)}) copy-start(bf16[128,256]{1,0:T(8,128)(2,1)} %in_ref.1) | copy-start | bytes 196612
  13.2 18.3 %copy-start.3 = (bf16[256,128]{1,0:T(8,128)(2,1)S(1)}, bf16[256,128]{1,0:T(8,128)(2,1)}, u32[]{:S(2)}) copy-start(bf16[256,128]{1,0:T(8,128)(2,1)} %out_w_ref.1) | copy-start | bytes 196612
  13.2 18.3 %copy-start.4 = (f32[6,128]{1,0:T(8,128)S(1)}, f32[6,128]{1,0:T(8,128)}, u32[]{:S(2)}) copy-start(f32[6,128]{1,0:T(8,128)} %bias_ref.1) | copy-start | bytes 9220
  13.2 18.3 %copy-start.5 = (f32[256]{0:T(256)S(1)}, f32[256]{0:T(256)}, u32[]{:S(2)}) copy-start(f32[256]{0:T(256)} %param.22) | copy-start | bytes 3076
  34.1 9.8 %collective-permute-start.1 = (bf16[16,8,128]{2,1,0:T(8,128)(2,1)S(1)}, bf16[16,8,128]{2,1,0:T(8,128)(2,1)S(1)}, u32[]{:S(2)}, u32[]{:S(2)}) collective-permute-start(bf16[16,8,128]{2,1,0:T(8,128)(2,1)S(1)} %get-tuple-element.24.tail_ref), channel_id=1, source_target_pairs={{0,1},{1,2},{2,3},{3,4},{4,5},{5,6},{6,7},{7,8},{8,9},{9,10},{10,1... | collective-permute-start | bytes 98312 | tf_op jit(solution)/shard_map/ppermute | solution.py:506
  36.1 8.8 %collective-permute-start.2 = (bf16[16,8,128]{2,1,0:T(8,128)(2,1)S(1)}, bf16[16,8,128]{2,1,0:T(8,128)(2,1)S(1)}, u32[]{:S(2)}, u32[]{:S(2)}) collective-permute-start(bf16[16,8,128]{2,1,0:T(8,128)(2,1)S(1)} %get-tuple-element.25.head_ref), channel_id=1, source_target_pairs={{1,0},{2,1},{3,2},{4,3},{5,4},{6,5},{7,6},{8,7},{9,8},{10,9},{11,1... | collective-permute-start | bytes 98312 | tf_op jit(solution)/shard_map/ppermute | solution.py:507
